TPU v7x, 32 devices: a whole 2x2x4 slice. The times are simulated.
32 devices in a mesh: lat: 8 (over z, x), lon: 4 (over y, core).
Axes of the slice: x: 2, y: 2, z: 4, core: 2. Of those that a mesh axis runs over, the one named last changes fastest.
Arguments:
- fields: float32 [4, 12, 16, 256, 128], P(None, None, 'lat', 'lon'), may hold values from -36 to 36
- weight_one: float32 [3, 3, 128, 128], replicated, may hold values from -0.1875 to 0.1875
- bias_one: float32 [128], replicated, may hold values from -3 to 3
- gain_one: float32 [128], replicated, may hold values from 0.25 to 1.75
- shift_one: float32 [128], replicated, may hold values from -3 to 3
- weight_two: float32 [3, 3, 128, 128], replicated, may hold values from -0.1875 to 0.1875
- bias_two: float32 [128], replicated, may hold values from -3 to 3
- gain_two: float32 [128], replicated, may hold values from 0.25 to 1.75
- shift_two: float32 [128], replicated, may hold values from -3 to 3
- cotangent: float32 [4, 12, 16, 256, 128], P(None, None, 'lat', 'lon'), may hold values from -6 to 6
Outputs:
- output: float32 [4, 12, 16, 256, 128], P(None, None, 'lat', 'lon')
- grad_fields: float32 [4, 12, 16, 256, 128], P(None, None, 'lat', 'lon')
- grad_weight_one: float32 [3, 3, 128, 128], replicated
- grad_bias_one: float32 [128], replicated
- grad_gain_one: float32 [128], replicated
- grad_shift_one: float32 [128], replicated
- grad_weight_two: float32 [3, 3, 128, 128], replicated
- grad_bias_two: float32 [128], replicated
- grad_gain_two: float32 [128], replicated
- grad_shift_two: float32 [128], replicated
All inputs are finite; a program needn't handle non-finite values.
Results may differ from a plain program's by a relative error of at most 0.0003.
Values sent between devices are 32-bit elements; how exact they have to be, the bound alone decides.
No kernel may reach another device: no remote copies, remote signals or barrier semaphores. Data moves between devices by JAX's collectives and lax.ppermute only.
A program may use at most 192 MiB of HBM per device.

v0:
```python
import jax
import jax.numpy as jnp
from jax import lax
from jax.sharding import PartitionSpec as P

EPSILON = 1e-05


def padded_2(block, sides, width, periodic):
    for axis, dim in sides:
        count = lax.axis_size(axis)
        forward = [(i, i + 1) for i in range(count - 1)]
        if periodic:
            forward.append((count - 1, 0))
        backward = [(target, source) for source, target in forward]
        low = lax.ppermute(
            lax.slice_in_dim(block, block.shape[dim] - width, None, axis=dim), axis, forward
        )
        high = lax.ppermute(lax.slice_in_dim(block, 0, width, axis=dim), axis, backward)
        block = jnp.concatenate([low, block, high], axis=dim)
    return block


def padded(values):
    rowed = padded_2(values, (("lat", 1),), 1, False)
    return padded_2(rowed, (("lon", 2),), 1, True)


def correlate(extended, kernel):
    return lax.conv_general_dilated(
        extended,
        kernel,
        (1, 1),
        "VALID",
        dimension_numbers=("NHWC", "HWIO", "NHWC"),
        precision=lax.Precision.HIGHEST,
    )


def flipped(kernel):
    return jnp.transpose(kernel[::-1, ::-1], (0, 1, 3, 2))


def kernel_grad(extended, slope):
    rows_here = slope.shape[1]
    cols_here = slope.shape[2]
    taps = []
    for row_tap in range(3):
        line = []
        for col_tap in range(3):
            window = extended[:, row_tap : row_tap + rows_here, col_tap : col_tap + cols_here]
            line.append(jnp.einsum("bhwc,bhwd->cd", window, slope, precision=lax.Precision.HIGHEST))
        taps.append(jnp.stack(line))
    return jnp.stack(taps)


def moments(active, count):
    local_total = jnp.sum(active, axis=(0, 1, 2))
    total = lax.psum(local_total, ("lat", "lon"))
    center = total / count
    deviate = active - center
    local_squares = jnp.sum(deviate * deviate, axis=(0, 1, 2))
    squares = lax.psum(local_squares, ("lat", "lon"))
    return (center, squares / count)


def norm_back(incoming, normed, inverse, gain, count):
    local_gain = jnp.sum(incoming * normed, axis=(0, 1, 2))
    local_shift = jnp.sum(incoming, axis=(0, 1, 2))
    dgain, dshift = lax.psum((local_gain, local_shift), ("lat", "lon"))
    dactive = gain * inverse / count * (count * incoming - dshift - normed * dgain)
    return (dactive, local_gain, local_shift)


def silu_slope(preact):
    sigma = jax.nn.sigmoid(preact)
    return sigma * (1.0 + preact * (1.0 - sigma))


def shards(
    fields,
    weight_one,
    bias_one,
    gain_one,
    shift_one,
    weight_two,
    bias_two,
    gain_two,
    shift_two,
    cotangent,
):
    inputs_all, cot_all = (fields, cotangent)
    shape_here = inputs_all.shape
    cycle_factor = lax.axis_size("lon")
    count = float(
        shape_here[1] * shape_here[2] * shape_here[3] * lax.axis_size("lat") * cycle_factor
    )
    flip_one = flipped(weight_one)
    flip_two = flipped(weight_two)
    grad_w1 = jnp.zeros_like(weight_one)
    grad_w2 = jnp.zeros_like(weight_two)
    grad_b1 = jnp.zeros_like(bias_one)
    grad_b2 = jnp.zeros_like(bias_two)
    grad_g1 = jnp.zeros_like(gain_one)
    grad_g2 = jnp.zeros_like(gain_two)
    grad_s1 = jnp.zeros_like(shift_one)
    grad_s2 = jnp.zeros_like(shift_two)
    outputs = []
    input_grads = []
    for batch_index in range(shape_here[0]):
        inputs = inputs_all[batch_index]
        ext_input = padded(inputs)
        pre_one = correlate(ext_input, weight_one) + bias_one
        act_one = jax.nn.silu(pre_one)
        center_one, spread_one = moments(act_one, count)
        inv_one = lax.rsqrt(spread_one + EPSILON)
        normed_one = (act_one - center_one) * inv_one
        hidden = gain_one * normed_one + shift_one
        ext_hidden = padded(hidden)
        pre_two = correlate(ext_hidden, weight_two) + bias_two
        act_two = jax.nn.silu(pre_two)
        center_two, spread_two = moments(act_two, count)
        inv_two = lax.rsqrt(spread_two + EPSILON)
        normed_two = (act_two - center_two) * inv_two
        outputs.append(inputs + gain_two * normed_two + shift_two)
        incoming = cot_all[batch_index]
        dact_two, dgain_two, dshift_two = norm_back(incoming, normed_two, inv_two, gain_two, count)
        grad_g2 = grad_g2 + dgain_two
        grad_s2 = grad_s2 + dshift_two
        dpre_two = dact_two * silu_slope(pre_two)
        grad_w2 = grad_w2 + kernel_grad(ext_hidden, dpre_two)
        grad_b2 = grad_b2 + jnp.sum(dpre_two, axis=(0, 1, 2))
        dhidden = correlate(padded(dpre_two), flip_two)
        dact_one, dgain_one, dshift_one = norm_back(dhidden, normed_one, inv_one, gain_one, count)
        grad_g1 = grad_g1 + dgain_one
        grad_s1 = grad_s1 + dshift_one
        dpre_one = dact_one * silu_slope(pre_one)
        grad_w1 = grad_w1 + kernel_grad(ext_input, dpre_one)
        grad_b1 = grad_b1 + jnp.sum(dpre_one, axis=(0, 1, 2))
        input_grads.append(incoming + correlate(padded(dpre_one), flip_one))
    grad_w1, grad_b1, grad_g1, grad_s1, grad_w2, grad_b2, grad_g2, grad_s2 = lax.psum(
        (grad_w1, grad_b1, grad_g1, grad_s1, grad_w2, grad_b2, grad_g2, grad_s2), ("lat", "lon")
    )
    stacked_out = jnp.stack(outputs)
    stacked_grad = jnp.stack(input_grads)
    final_out, final_grad = (stacked_out, stacked_grad)
    return (
        final_out,
        final_grad,
        grad_w1,
        grad_b1,
        grad_g1,
        grad_s1,
        grad_w2,
        grad_b2,
        grad_g2,
        grad_s2,
    )


def solution(mesh):
    placed = (
        P(None, None, "lat", "lon", None),
        P(),
        P(),
        P(),
        P(),
        P(),
        P(),
        P(),
        P(),
        P(None, None, "lat", "lon", None),
    )
    return jax.shard_map(
        shards,
        mesh=mesh,
        in_specs=placed,
        out_specs=(
            P(None, None, "lat", "lon", None),
            P(None, None, "lat", "lon", None),
            P(),
            P(),
            P(),
            P(),
            P(),
            P(),
            P(),
            P(),
        ),
        check_vma=False,
    )
```

profile of v0, /device:TPU:0, one launch (start us, length us, event | category | flops | bytes accessed | tf_op | source)
XLA Modules:
  0.0 966.2 jit_solution(10397734401332527781)
XLA Ops:
  34.8 25.9 %collective-permute-done.24 = f32[12,1,64,128]{3,0,2,1:T(8,128)S(1)} collective-permute-done((f32[12,1,64,128]{3,0,2,1:T(8,128)S(1)}, f32[12,1,64,128]{3,0,2,1:T(8,128)S(1)}, u32[]{:S(2)}, u32[]{:S(2)}) %collective-permute-start.24) | collective-permute-done | bytes 393248 | tf_op jit(solution)/shard_map/ppermute | solution.py:16
  67.1 16.1 %collective-permute-done.16 = f32[12,1,64,128]{3,0,2,1:T(8,128)S(1)} collective-permute-done((f32[12,1,64,128]{3,0,2,1:T(8,128)S(1)}, f32[12,1,64,128]{3,0,2,1:T(8,128)S(1)}, u32[]{:S(2)}, u32[]{:S(2)}) %collective-permute-start.16) | collective-permute-done | bytes 393248 | tf_op jit(solution)/shard_map/ppermute | solution.py:16
  84.3 10.1 %collective-permute-done.8 = f32[12,1,64,128]{3,0,2,1:T(8,128)S(1)} collective-permute-done((f32[12,1,64,128]{3,0,2,1:T(8,128)S(1)}, f32[12,1,64,128]{3,0,2,1:T(8,128)S(1)}, u32[]{:S(2)}, u32[]{:S(2)}) %collective-permute-start.8) | collective-permute-done | bytes 393248 | tf_op jit(solution)/shard_map/ppermute | solution.py:16
  146.0 40.6 %all-reduce.6 = (f32[128]{0:T(128)}, f32[128]{0:T(128)}, f32[128]{0:T(128)}, f32[128]{0:T(128)}) all-reduce(f32[128]{0:T(128)S(1)} %get-tuple-element.264, f32[128]{0:T(128)S(1)} %get-tuple-element.266, f32[128]{0:T(128)S(1)} %get-tuple-element.268, f32[128]{0:T(128)S(1)} %get-tuple-element.270), channel_id=1, replica_groups=mesh['lat'=8,'lon'=4] {'lat','lon'}, use_global_device_ids=true, to_apply=%region_25.26 | all-reduce | flops 512 | bytes 4096 | tf_op jit(solution)/shard_map/psum | solution.py:59
  192.6 41.1 %all-reduce.5 = (f32[128]{0:T(128)S(1)}, f32[128]{0:T(128)S(1)}, f32[128]{0:T(128)S(1)}, f32[128]{0:T(128)S(1)}) all-reduce(f32[128]{0:T(128)S(1)} %copy-done.178, f32[128]{0:T(128)S(1)} %multiply_reduce_fusion.7, f32[128]{0:T(128)S(1)} %multiply_reduce_fusion.9, ...), channel_id=1, replica_groups=mesh['lat'=8,'lon'=4] {'lat','lon'}, use_global_device_ids=true, to_apply=%region_27.28 | all-reduce | flops 512 | bytes 4096 | tf_op jit(solution)/shard_map/psum | solution.py:63
  271.7 15.6 %collective-permute-done.20 = f32[12,1,64,128]{3,0,2,1:T(8,128)S(1)} collective-permute-done((f32[12,1,64,128]{3,0,2,1:T(8,128)S(1)}, f32[12,1,64,128]{3,0,2,1:T(8,128)S(1)}, u32[]{:S(2)}, u32[]{:S(2)}) %collective-permute-start.20) | collective-permute-done | bytes 393248 | tf_op jit(solution)/shard_map/ppermute | solution.py:16
  293.7 16.1 %collective-permute-done.28 = f32[12,1,64,128]{3,0,2,1:T(8,128)S(1)} collective-permute-done((f32[12,1,64,128]{3,0,2,1:T(8,128)S(1)}, f32[12,1,64,128]{3,0,2,1:T(8,128)S(1)}, u32[]{:S(2)}, u32[]{:S(2)}) %collective-permute-start.28) | collective-permute-done | bytes 393248 | tf_op jit(solution)/shard_map/ppermute | solution.py:16
  311.0 10.0 %collective-permute-done.12 = f32[12,1,64,128]{3,0,2,1:T(8,128)S(1)} collective-permute-done((f32[12,1,64,128]{3,0,2,1:T(8,128)S(1)}, f32[12,1,64,128]{3,0,2,1:T(8,128)S(1)}, u32[]{:S(2)}, u32[]{:S(2)}) %collective-permute-start.12) | collective-permute-done | bytes 393248 | tf_op jit(solution)/shard_map/ppermute | solution.py:16
  336.9 9.5 fusion.345
  346.7 9.5 fusion.347
  356.3 10.1 %fusion.343 = (f32[128]{0:T(128)}, f32[12,2,64,128]{3,0,2,1:T(8,128)}) fusion(f32[128]{0:T(128)S(1)} %copy-done.195, f32[3,3,128,128]{3,2,1,0:T(8,128)S(1)} %copy-done, f32[12,4,1,128]{3,0,2,1:T(8,128)S(1)} %collective-permute-done.15, f32[12,1,64,128]{3,0,2,1:T(8,128)S(1)} %collective-permute-done.13, f32[12,2,64,128]{3,0,2,1:T(8,128)S(1)} %get-tuple-element.245, ...), kind=kOutput, calls=%fused_computation.573 | convolution fusion | flops 2720710656 | bytes 2999296 | tf_op jit(solution)/shard_map/conv_general_dilated | solution.py:30
  366.4 9.8 %fusion.341 = (f32[128]{0:T(128)}, f32[12,2,64,128]{3,0,2,1:T(8,128)}) fusion(f32[128]{0:T(128)S(1)} %copy-done.195, f32[3,3,128,128]{3,2,1,0:T(8,128)S(1)} %copy-done, f32[12,4,1,128]{3,0,2,1:T(8,128)S(1)} %collective-permute-done.7, f32[12,1,64,128]{3,0,2,1:T(8,128)S(1)} %collective-permute-done.5, f32[12,2,64,128]{3,0,2,1:T(8,128)S(1)} %get-tuple-element.244, ...), kind=kOutput, calls=%fused_computation.571 | convolution fusion | flops 2720710656 | bytes 2999296 | tf_op jit(solution)/shard_map/conv_general_dilated | solution.py:30
  376.2 39.8 %all-reduce.4 = (f32[128]{0:T(128)}, f32[128]{0:T(128)}, f32[128]{0:T(128)}, f32[128]{0:T(128)}) all-reduce(f32[128]{0:T(128)} %get-tuple-element.272, f32[128]{0:T(128)} %get-tuple-element.274, f32[128]{0:T(128)} %get-tuple-element.276, f32[128]{0:T(128)} %get-tuple-element.278), channel_id=1, replica_groups=mesh['lat'=8,'lon'=4] {'lat','lon'}, use_global_device_ids=true, to_apply=%region_29.30 | all-reduce | flops 512 | bytes 4096 | tf_op jit(solution)/shard_map/psum | solution.py:59
  424.8 41.5 %all-reduce.3 = (f32[128]{0:T(128)}, f32[128]{0:T(128)}, f32[128]{0:T(128)}, f32[128]{0:T(128)}) all-reduce(f32[128]{0:T(128)} %multiply_reduce_fusion.4, f32[128]{0:T(128)} %multiply_reduce_fusion.6, f32[128]{0:T(128)} %multiply_reduce_fusion.8, f32[128]{0:T(128)} %multiply_reduce_fusion.10), channel_id=1, replica_groups=mesh['lat'=8,'lon'=4] {'lat','lon'}, use_global_device_ids=true, to_apply=%region_31.32 | all-reduce | flops 512 | bytes 4096 | tf_op jit(solution)/shard_map/psum | solution.py:63
  475.6 39.9 %all-reduce.2 = (f32[128]{0:T(128)}, f32[128]{0:T(128)}, f32[128]{0:T(128)}, f32[128]{0:T(128)}, f32[128]{0:T(128)}, /*index=5*/f32[128]{0:T(128)}, f32[128]{0:T(128)}, f32[128]{0:T(128)}) all-reduce(f32[128]{0:T(128)} %fusion.214, f32[128]{0:T(128)} %get-tuple-element.23, ...), channel_id=1, replica_groups=mesh['lat'=8,'lon'=4] {'lat','lon'}, use_global_device_ids=true, to_apply=%region_59.60 | all-reduce | flops 1024 | bytes 8192 | tf_op jit(solution)/shard_map/psum | solution.py:70
  620.0 12.5 %collective-permute-done.40 = f32[12,1,64,128]{3,0,2,1:T(8,128)S(1)} collective-permute-done((f32[12,1,64,128]{3,0,2,1:T(8,128)S(1)}, f32[12,1,64,128]{3,0,2,1:T(8,128)S(1)}, u32[]{:S(2)}, u32[]{:S(2)}) %collective-permute-start.40) | collective-permute-done | bytes 393248 | tf_op jit(solution)/shard_map/ppermute | solution.py:16
  661.5 9.3 fusion.349
  680.0 44.7 %all-reduce.1 = (f32[128]{0:T(128)S(1)}, f32[128]{0:T(128)S(1)}, f32[128]{0:T(128)S(1)}, f32[128]{0:T(128)S(1)}, f32[128]{0:T(128)S(1)}, /*index=5*/f32[128]{0:T(128)S(1)}, f32[128]{0:T(128)S(1)}, f32[128]{0:T(128)S(1)}) all-reduce(f32[128]{0:T(128)S(1)} %get-tuple-element.31, ...), channel_id=1, replica_groups=mesh['lat'=8,'lon'=4] {'lat','lon'}, use_global_device_ids=true, to_apply=%region_63.64 | all-reduce | flops 1024 | bytes 8192 | tf_op jit(solution)/shard_map/psum | solution.py:70
  821.6 62.3 %all-reduce = (f32[128]{0:T(128)}, f32[128]{0:T(128)}, f32[128]{0:T(128)}, f32[128]{0:T(128)}, f32[128]{0:T(128)}, /*index=5*/f32[128]{0:T(128)}) all-reduce(f32[128]{0:T(128)S(1)} %add_add_fusion.5, f32[128]{0:T(128)S(1)} %add_add_fusion.4, f32[128]{0:T(128)S(1)} %add_add_fusion.3, ...), channel_id=1, replica_groups=mesh['lat'=8,'lon'=4] {'lat','lon'}, use_global_device_ids=true, to_apply=%region_69.70 | all-reduce | flops 768 | bytes 6144 | tf_op jit(solution)/shard_map/psum | solution.py:141
  893.5 9.7 %fusion.163 = f32[1,12,2,64,128]{4,1,3,2,0:T(8,128)S(1)} fusion(f32[3,3,128,128]{3,2,1,0:T(8,128)S(1)} %copy-done.193, f32[12,4,1,128]{3,0,2,1:T(8,128)S(1)} %collective-permute-done.63, f32[12,1,64,128]{3,0,2,1:T(8,128)} %collective-permute-done.61, f32[12,2,64,128]{3,0,2,1:T(8,128)S(1)} %copy-done.16, f32[12,1,64,128]{3,0,2,1:T(8,128)} %collective-permute-done.60, ...), kind=kOutput, calls=%fused_computation.179 | convolution fusion | flops 2719727616 | bytes 3784704 | tf_op jit(solution)/shard_map/conv_general_dilated | solution.py:30
  903.9 9.7 %fusion.169 = f32[1,12,2,64,128]{4,1,3,2,0:T(8,128)S(1)} fusion(f32[3,3,128,128]{3,2,1,0:T(8,128)S(1)} %copy-done.193, f32[12,4,1,128]{3,0,2,1:T(8,128)S(1)} %collective-permute-done.55, f32[12,1,64,128]{3,0,2,1:T(8,128)} %collective-permute-done.53, f32[12,2,64,128]{3,0,2,1:T(8,128)S(1)} %get-tuple-element.85, ...), kind=kOutput, calls=%fused_computation.181 | convolution fusion | flops 2719727616 | bytes 3784704 | tf_op jit(solution)/shard_map/conv_general_dilated | solution.py:30
  913.6 9.8 %fusion.175 = f32[1,12,2,64,128]{4,1,3,2,0:T(8,128)S(1)} fusion(f32[3,3,128,128]{3,2,1,0:T(8,128)S(1)} %copy-done.193, f32[12,4,1,128]{3,0,2,1:T(8,128)S(1)} %collective-permute-done.47, f32[12,1,64,128]{3,0,2,1:T(8,128)S(1)} %collective-permute-done.45, f32[12,2,64,128]{3,0,2,1:T(8,128)S(1)} %get-tuple-element.81, ...), kind=kOutput, calls=%fused_computation.183 | convolution fusion | flops 2719727616 | bytes 3784704 | tf_op jit(solution)/shard_map/conv_general_dilated | solution.py:30
  923.5 9.7 %fusion.181 = f32[1,12,2,64,128]{4,1,3,2,0:T(8,128)S(1)} fusion(f32[3,3,128,128]{3,2,1,0:T(8,128)S(1)} %copy-done.193, f32[12,4,1,128]{3,0,2,1:T(8,128)S(1)} %collective-permute-done.39, f32[12,1,64,128]{3,0,2,1:T(8,128)} %collective-permute-done.37, f32[12,2,64,128]{3,0,2,1:T(8,128)S(1)} %copy-done.14, f32[12,1,64,128]{3,0,2,1:T(8,128)} %collective-permute-done.36, ...), kind=kOutput, calls=%fused_computation.185 | convolution fusion | flops 2719727616 | bytes 3784704 | tf_op jit(solution)/shard_map/conv_general_dilated | solution.py:30
  936.1 19.2 %all-reduce.10.cloned.1.call-done = (f32[3,3,128,128]{3,2,1,0:T(8,128)}, f32[3,3,128,128]{3,2,1,0:T(8,128)}) async-done(((f32[3,3,128,128]{3,2,1,0:T(8,128)}, f32[3,3,128,128]{3,2,1,0:T(8,128)}), (f32[3,3,128,128]{3,2,1,0:T(8,128)}, f32[3,3,128,128]{3,2,1,0:T(8,128)})) %all-reduce.10.cloned.1.call-update) | async-done | bytes 1179664 | tf_op jit(solution)/shard_map/psum | solution.py:141
  (730 shorter events, 426.0 us)
Async XLA Ops:
  7.2 948.1 %all-reduce.10.cloned.1.call-start = ((), (), s32[]{:S(2)}) async-start(), calls=%async_computation | async-start | bytes 2359296 | tf_op jit(solution)/shard_map/psum | solution.py:141
  11.3 49.4 %collective-permute-start.24 = (f32[12,1,64,128]{3,0,2,1:T(8,128)S(1)}, f32[12,1,64,128]{3,0,2,1:T(8,128)S(1)}, u32[]{:S(2)}, u32[]{:S(2)}) collective-permute-start(f32[12,1,64,128]{3,0,2,1:T(8,128)S(1)} %get-tuple-element.242), channel_id=1, source_target_pairs={{0,4},{4,8},{8,12},{12,16},{16,20},{20,24},{24,28},{1,5},{5,9},{9,... | collective-permute-start | bytes 1179656 | tf_op jit(solution)/shard_map/ppermute | solution.py:16
  17.4 44.6 %collective-permute-start.17 = (f32[12,1,64,128]{3,0,2,1:T(8,128)S(1)}, f32[12,1,64,128]{3,0,2,1:T(8,128)S(1)}, u32[]{:S(2)}, u32[]{:S(2)}) collective-permute-start(f32[12,1,64,128]{3,0,2,1:T(8,128)S(1)} %get-tuple-element.241), channel_id=1, source_target_pairs={{4,0},{8,4},{12,8},{16,12},{20,16},{24,20},{28,24},{5,1},{9,5},{13... | collective-permute-start | bytes 1179656 | tf_op jit(solution)/shard_map/ppermute | solution.py:19
  18.9 64.2 %collective-permute-start.16 = (f32[12,1,64,128]{3,0,2,1:T(8,128)S(1)}, f32[12,1,64,128]{3,0,2,1:T(8,128)S(1)}, u32[]{:S(2)}, u32[]{:S(2)}) collective-permute-start(f32[12,1,64,128]{3,0,2,1:T(8,128)S(1)} %get-tuple-element.240), channel_id=1, source_target_pairs={{0,4},{4,8},{8,12},{12,16},{16,20},{20,24},{24,28},{1,5},{5,9},{9,... | collective-permute-start | bytes 1179656 | tf_op jit(solution)/shard_map/ppermute | solution.py:16
  24.9 59.3 %collective-permute-start.9 = (f32[12,1,64,128]{3,0,2,1:T(8,128)S(1)}, f32[12,1,64,128]{3,0,2,1:T(8,128)S(1)}, u32[]{:S(2)}, u32[]{:S(2)}) collective-permute-start(f32[12,1,64,128]{3,0,2,1:T(8,128)S(1)} %get-tuple-element.239), channel_id=1, source_target_pairs={{4,0},{8,4},{12,8},{16,12},{20,16},{24,20},{28,24},{5,1},{9,5},{13... | collective-permute-start | bytes 1179656 | tf_op jit(solution)/shard_map/ppermute | solution.py:19
  29.2 65.2 %collective-permute-start.8 = (f32[12,1,64,128]{3,0,2,1:T(8,128)S(1)}, f32[12,1,64,128]{3,0,2,1:T(8,128)S(1)}, u32[]{:S(2)}, u32[]{:S(2)}) collective-permute-start(f32[12,1,64,128]{3,0,2,1:T(8,128)S(1)} %get-tuple-element.238), channel_id=1, source_target_pairs={{0,4},{4,8},{8,12},{12,16},{16,20},{20,24},{24,28},{1,5},{5,9},{9,... | collective-permute-start | bytes 1179656 | tf_op jit(solution)/shard_map/ppermute | solution.py:16
  62.0 43.5 %collective-permute-start = (f32[12,1,64,128]{3,0,2,1:T(8,128)S(1)}, f32[12,1,64,128]{3,0,2,1:T(8,128)S(1)}, u32[]{:S(2)}, u32[]{:S(2)}) collective-permute-start(f32[12,1,64,128]{3,0,2,1:T(8,128)S(1)} %get-tuple-element.236), channel_id=1, source_target_pairs={{0,4},{4,8},{8,12},{12,16},{16,20},{20,24},{24,28},{1,5},{5,9},{9,... | collective-permute-start | bytes 1179656 | tf_op jit(solution)/shard_map/ppermute | solution.py:16
  240.4 46.9 %collective-permute-start.20 = (f32[12,1,64,128]{3,0,2,1:T(8,128)S(1)}, f32[12,1,64,128]{3,0,2,1:T(8,128)S(1)}, u32[]{:S(2)}, u32[]{:S(2)}) collective-permute-start(f32[12,1,64,128]{3,0,2,1:T(8,128)S(1)} %get-tuple-element.232), channel_id=1, source_target_pairs={{0,4},{4,8},{8,12},{12,16},{16,20},{20,24},{24,28},{1,5},{5,9},{9,... | collective-permute-start | bytes 1179656 | tf_op jit(solution)/shard_map/ppermute | solution.py:16
  246.6 63.2 %collective-permute-start.28 = (f32[12,1,64,128]{3,0,2,1:T(8,128)S(1)}, f32[12,1,64,128]{3,0,2,1:T(8,128)S(1)}, u32[]{:S(2)}, u32[]{:S(2)}) collective-permute-start(f32[12,1,64,128]{3,0,2,1:T(8,128)S(1)} %get-tuple-element.234), channel_id=1, source_target_pairs={{0,4},{4,8},{8,12},{12,16},{16,20},{20,24},{24,28},{1,5},{5,9},{9,... | collective-permute-start | bytes 1179656 | tf_op jit(solution)/shard_map/ppermute | solution.py:16
  252.2 58.7 %collective-permute-start.13 = (f32[12,1,64,128]{3,0,2,1:T(8,128)S(1)}, f32[12,1,64,128]{3,0,2,1:T(8,128)S(1)}, u32[]{:S(2)}, u32[]{:S(2)}) collective-permute-start(f32[12,1,64,128]{3,0,2,1:T(8,128)S(1)} %get-tuple-element.231), channel_id=1, source_target_pairs={{4,0},{8,4},{12,8},{16,12},{20,16},{24,20},{28,24},{5,1},{9,5},{13... | collective-permute-start | bytes 1179656 | tf_op jit(solution)/shard_map/ppermute | solution.py:19
  266.2 54.8 %collective-permute-start.12 = (f32[12,1,64,128]{3,0,2,1:T(8,128)S(1)}, f32[12,1,64,128]{3,0,2,1:T(8,128)S(1)}, u32[]{:S(2)}, u32[]{:S(2)}) collective-permute-start(f32[12,1,64,128]{3,0,2,1:T(8,128)S(1)} %get-tuple-element.230), channel_id=1, source_target_pairs={{0,4},{4,8},{8,12},{12,16},{16,20},{20,24},{24,28},{1,5},{5,9},{9,... | collective-permute-start | bytes 1179656 | tf_op jit(solution)/shard_map/ppermute | solution.py:16
  527.3 76.3 %collective-permute-start.57 = (f32[12,1,64,128]{3,0,2,1:T(8,128)S(1)}, f32[12,1,64,128]{3,0,2,1:T(8,128)S(1)}, u32[]{:S(2)}, u32[]{:S(2)}) collective-permute-start(f32[12,1,64,128]{3,0,2,1:T(8,128)S(1)} %get-tuple-element.227), channel_id=1, source_target_pairs={{4,0},{8,4},{12,8},{16,12},{20,16},{24,20},{28,24},{5,1},{9,5},{13... | collective-permute-start | bytes 1179656 | tf_op jit(solution)/shard_map/ppermute | solution.py:19
  528.6 80.5 %collective-permute-start.56 = (f32[12,1,64,128]{3,0,2,1:T(8,128)S(1)}, f32[12,1,64,128]{3,0,2,1:T(8,128)S(1)}, u32[]{:S(2)}, u32[]{:S(2)}) collective-permute-start(f32[12,1,64,128]{3,0,2,1:T(8,128)S(1)} %get-tuple-element.226), channel_id=1, source_target_pairs={{0,4},{4,8},{8,12},{12,16},{16,20},{20,24},{24,28},{1,5},{5,9},{9,... | collective-permute-start | bytes 1179656 | tf_op jit(solution)/shard_map/ppermute | solution.py:16
  533.4 76.9 %collective-permute-start.49 = (f32[12,1,64,128]{3,0,2,1:T(8,128)S(1)}, f32[12,1,64,128]{3,0,2,1:T(8,128)S(1)}, u32[]{:S(2)}, u32[]{:S(2)}) collective-permute-start(f32[12,1,64,128]{3,0,2,1:T(8,128)S(1)} %get-tuple-element.225), channel_id=1, source_target_pairs={{4,0},{8,4},{12,8},{16,12},{20,16},{24,20},{28,24},{5,1},{9,5},{13... | collective-permute-start | bytes 1179656 | tf_op jit(solution)/shard_map/ppermute | solution.py:19
  534.7 84.7 %collective-permute-start.48 = (f32[12,1,64,128]{3,0,2,1:T(8,128)S(1)}, f32[12,1,64,128]{3,0,2,1:T(8,128)S(1)}, u32[]{:S(2)}, u32[]{:S(2)}) collective-permute-start(f32[12,1,64,128]{3,0,2,1:T(8,128)S(1)} %get-tuple-element.224), channel_id=1, source_target_pairs={{0,4},{4,8},{8,12},{12,16},{16,20},{20,24},{24,28},{1,5},{5,9},{9,... | collective-permute-start | bytes 1179656 | tf_op jit(solution)/shard_map/ppermute | solution.py:16
  540.2 79.3 %collective-permute-start.41 = (f32[12,1,64,128]{3,0,2,1:T(8,128)S(1)}, f32[12,1,64,128]{3,0,2,1:T(8,128)S(1)}, u32[]{:S(2)}, u32[]{:S(2)}) collective-permute-start(f32[12,1,64,128]{3,0,2,1:T(8,128)S(1)} %get-tuple-element.223), channel_id=1, source_target_pairs={{4,0},{8,4},{12,8},{16,12},{20,16},{24,20},{28,24},{5,1},{9,5},{13... | collective-permute-start | bytes 1179656 | tf_op jit(solution)/shard_map/ppermute | solution.py:19
  733.1 76.1 %collective-permute-start.61 = (f32[12,1,64,128]{3,0,2,1:T(8,128)}, f32[12,1,64,128]{3,0,2,1:T(8,128)}, u32[]{:S(2)}, u32[]{:S(2)}) collective-permute-start(f32[12,1,64,128]{3,0,2,1:T(8,128)} %get-tuple-element.219), channel_id=1, source_target_pairs={{4,0},{8,4},{12,8},{16,12},{20,16},{24,20},{28,24},{5,1},{9,5},{13... | collective-permute-start | bytes 1179656 | tf_op jit(solution)/shard_map/ppermute | solution.py:19
  734.6 80.2 %collective-permute-start.60 = (f32[12,1,64,128]{3,0,2,1:T(8,128)}, f32[12,1,64,128]{3,0,2,1:T(8,128)}, u32[]{:S(2)}, u32[]{:S(2)}) collective-permute-start(f32[12,1,64,128]{3,0,2,1:T(8,128)} %get-tuple-element.218), channel_id=1, source_target_pairs={{0,4},{4,8},{8,12},{12,16},{16,20},{20,24},{24,28},{1,5},{5,9},{9,... | collective-permute-start | bytes 1179656 | tf_op jit(solution)/shard_map/ppermute | solution.py:16
  740.2 75.9 %collective-permute-start.53 = (f32[12,1,64,128]{3,0,2,1:T(8,128)}, f32[12,1,64,128]{3,0,2,1:T(8,128)}, u32[]{:S(2)}, u32[]{:S(2)}) collective-permute-start(f32[12,1,64,128]{3,0,2,1:T(8,128)} %get-tuple-element.217), channel_id=1, source_target_pairs={{4,0},{8,4},{12,8},{16,12},{20,16},{24,20},{28,24},{5,1},{9,5},{13... | collective-permute-start | bytes 1179656 | tf_op jit(solution)/shard_map/ppermute | solution.py:19
  741.5 143.2 %collective-permute-start.52 = (f32[12,1,64,128]{3,0,2,1:T(8,128)}, f32[12,1,64,128]{3,0,2,1:T(8,128)}, u32[]{:S(2)}, u32[]{:S(2)}) collective-permute-start(f32[12,1,64,128]{3,0,2,1:T(8,128)} %get-tuple-element.216), channel_id=1, source_target_pairs={{0,4},{4,8},{8,12},{12,16},{16,20},{20,24},{24,28},{1,5},{5,9},{9,... | collective-permute-start | bytes 1179656 | tf_op jit(solution)/shard_map/ppermute | solution.py:16
  747.0 138.9 %collective-permute-start.45 = (f32[12,1,64,128]{3,0,2,1:T(8,128)}, f32[12,1,64,128]{3,0,2,1:T(8,128)S(1)}, u32[]{:S(2)}, u32[]{:S(2)}) collective-permute-start(f32[12,1,64,128]{3,0,2,1:T(8,128)} %get-tuple-element.215), channel_id=1, source_target_pairs={{4,0},{8,4},{12,8},{16,12},{20,16},{24,20},{28,24},{5,1},{9,5},{13... | collective-permute-start | bytes 1179656 | tf_op jit(solution)/shard_map/ppermute | solution.py:19
  809.3 76.8 %collective-permute-start.44 = (f32[12,1,64,128]{3,0,2,1:T(8,128)}, f32[12,1,64,128]{3,0,2,1:T(8,128)}, u32[]{:S(2)}, u32[]{:S(2)}) collective-permute-start(f32[12,1,64,128]{3,0,2,1:T(8,128)} %get-tuple-element.214), channel_id=1, source_target_pairs={{0,4},{4,8},{8,12},{12,16},{16,20},{20,24},{24,28},{1,5},{5,9},{9,... | collective-permute-start | bytes 1179656 | tf_op jit(solution)/shard_map/ppermute | solution.py:16
  814.7 74.2 %collective-permute-start.37 = (f32[12,1,64,128]{3,0,2,1:T(8,128)}, f32[12,1,64,128]{3,0,2,1:T(8,128)}, u32[]{:S(2)}, u32[]{:S(2)}) collective-permute-start(f32[12,1,64,128]{3,0,2,1:T(8,128)} %get-tuple-element.213), channel_id=1, source_target_pairs={{4,0},{8,4},{12,8},{16,12},{20,16},{24,20},{28,24},{5,1},{9,5},{13... | collective-permute-start | bytes 1179656 | tf_op jit(solution)/shard_map/ppermute | solution.py:19
  816.0 73.1 %collective-permute-start.36 = (f32[12,1,64,128]{3,0,2,1:T(8,128)}, f32[12,1,64,128]{3,0,2,1:T(8,128)}, u32[]{:S(2)}, u32[]{:S(2)}) collective-permute-start(f32[12,1,64,128]{3,0,2,1:T(8,128)} %get-tuple-element.212), channel_id=1, source_target_pairs={{0,4},{4,8},{8,12},{12,16},{16,20},{20,24},{24,28},{1,5},{5,9},{9,... | collective-permute-start | bytes 1179656 | tf_op jit(solution)/shard_map/ppermute | solution.py:16
  (237 other events, 3988.0 us)
Sparse Core Ops, SparseCore 0:
  809.4 145.8 all-reduce.9
where the time goes:
time: 973 us; the launch traced here: 966 us
  blocking collectives  310 us (32%)
  matrix products  262 us (27%)
  waiting for transfers between devices  144 us (15%)
  starting transfers between devices  129 us (13%)
  other arithmetic  63.7 us (7%)
  local copies, waits for them, and re-layouts  39.3 us (4%)
  between operations  17.6 us (2%)
    conv_general_dilated x16, matrix products, correlate(): lax.conv_general_dilated(extended, kernel, (1, 1), 'VALID', dimension_num...  150 us
    ppermute x32, waiting for transfers between devices, padded_2(): lax.ppermute(lax.slice_in_dim(block, block.shape[dim] - width, None, axis...  125 us
    dot_general x72, matrix products, kernel_grad(): jnp.einsum('bhwc,bhwd->cd', window, slope, precision=lax.Precision.HIGHEST)  113 us
    ppermute x32, starting transfers between devices, padded_2(): lax.ppermute(lax.slice_in_dim(block, block.shape[dim] - width, None, axis...  89.7 us
    psum x2, blocking collectives, norm_back(): dgain, dshift = lax.psum((local_gain, local_shift), ('lat', 'lon'))  84.6 us
    psum x2, blocking collectives, moments(): squares = lax.psum(local_squares, ('lat', 'lon'))  82.6 us
    psum x2, blocking collectives, moments(): total = lax.psum(local_total, ('lat', 'lon'))  80.4 us
    psum x1, blocking collectives, shards(): lax.psum((grad_w1, grad_b1, grad_g1, grad_s1, grad_w2, grad_b2, grad_g2,...  62.3 us
  transfers between devices with their start and end apart: 65, of which 11 were waited for; matrix products, arithmetic and copies ran while one was open for 29% of the time, Pallas kernels for 0%

commit v1 on v0

v1 whole, which is shorter than its diff:
```python
import functools

import jax
import jax.numpy as jnp
from jax import lax
from jax.experimental import pallas as pl
from jax.experimental.pallas import tpu as pltpu
from jax.sharding import PartitionSpec as P


EPSILON = 1e-05
F32 = jnp.float32
BF16 = jnp.bfloat16
AXES = ("lat", "lon")
STEP = 2
VMEM_LIMIT = 48 << 20


def permute(value, target):
    rows, cols = lax.axis_size("lat"), lax.axis_size("lon")
    pairs = []
    for row in range(rows):
        for col in range(cols):
            to = target(row, col)
            if 0 <= to[0] < rows and 0 <= to[1] < cols:
                pairs.append((row * cols + col, to[0] * cols + to[1]))
    return lax.ppermute(value, AXES, pairs)


def to_core(row, col):
    return row, col ^ 1


def to_side(row, col):
    return row ^ 1, col


def to_cross(row, col):
    return row ^ 1, col ^ 1


def to_east(row, col):
    return row, col ^ 2


def to_pair(row, col):
    return row ^ 2, col


def to_next(row, col):
    return (row + 2 if (row // 2) % 2 else row - 2), col


def group_steps():
    steps = []
    bit = 2
    while bit < lax.axis_size("lon"):
        steps.append(functools.partial(lambda bit, row, col: (row, col ^ bit), bit))
        bit *= 2
    bit = 2
    while bit < lax.axis_size("lat"):
        steps.append(functools.partial(lambda bit, row, col: (row ^ bit, col), bit))
        bit *= 2
    return steps


def exchange_rows(pair_row, next_row):
    return permute(pair_row, to_pair), permute(next_row, to_next)


def split(value):
    high = value.astype(BF16)
    return high, (value - high.astype(F32)).astype(BF16)


def sigmoid(value):
    return 1.0 / (1.0 + jnp.exp(-value))


def cost(flops, moved):
    return pl.CostEstimate(flops=int(flops), bytes_accessed=int(moved), transcendentals=0)


def call(body, grid, scalars, inputs, outputs, scratch, name, flops=0.0):
    moved = sum(a.size * a.dtype.itemsize for a, _, _ in inputs)
    moved += sum(4 * functools.reduce(lambda x, y: x * y, o[0], 1) for o in outputs)
    return pl.pallas_call(
        body,
        grid_spec=pltpu.PrefetchScalarGridSpec(
            num_scalar_prefetch=1,
            grid=(grid,),
            in_specs=[pl.BlockSpec(block, index) for _, block, index in inputs],
            out_specs=[pl.BlockSpec(o[2], o[3]) for o in outputs],
            scratch_shapes=scratch,
        ),
        out_shape=[jax.ShapeDtypeStruct(o[0], o[1]) for o in outputs],
        compiler_params=pltpu.CompilerParams(vmem_limit_bytes=VMEM_LIMIT),
        cost_estimate=cost(flops, moved),
        name=name,
    )(scalars, *[a for a, _, _ in inputs])


def by_sample(array, step=STEP):
    rest = (0,) * (array.ndim - 1)
    return array, (step,) + array.shape[1:], lambda i, s: (i,) + rest


def whole(array):
    rest = (0,) * array.ndim
    return array, array.shape, lambda i, s: rest


def out_by_sample(shape, step=STEP):
    rest = (0,) * (len(shape) - 1)
    return shape, F32, (step,) + shape[1:], lambda i, s: (i,) + rest


def out_whole(shape):
    rest = (0,) * len(shape)
    return shape, F32, shape, lambda i, s: rest


def pack_kernel(s_ref, to_side, to_cross, to_core, side_edge, cross_edge, core, side_inner, cross_inner):
    lx = s_ref[0]
    side_edge[...] = to_side[0, :, lx]
    cross_edge[...] = to_cross[0, :, lx]
    core[...] = to_core[0]
    side_inner[...] = to_side[0, :, 1 - lx]
    cross_inner[...] = to_cross[0, :, 1 - lx]


def pack(scalars, field, name):
    _, _, batch, rows, cols, chans = field.shape
    flat = field.reshape((-1,) + field.shape[2:])
    step = batch // 2
    block = (1, step, rows, cols, chans)
    one = (batch, cols, chans)
    return call(
        pack_kernel,
        batch // step,
        scalars,
        [
            (flat, block, lambda i, s: (2 * (1 - s[0]) + s[1], i, 0, 0, 0)),
            (flat, block, lambda i, s: (2 * (1 - s[0]) + 1 - s[1], i, 0, 0, 0)),
            (flat, block, lambda i, s: (2 * s[0] + 1 - s[1], i, 0, 0, 0)),
        ],
        [out_by_sample(shape, step) for shape in (one, one, (batch, rows, cols, chans), one, one)],
        [],
        name,
    )


def join_kernel(edge, s_ref, home, core, side, cross, rows_ref, tile_ref):
    lx, nc = s_ref[0], s_ref[1]
    half = home.shape[3]
    here = pl.ds(pl.multiple_of(nc * half, half), half)
    there = pl.ds(pl.multiple_of((1 - nc) * half, half), half)
    rows_ref[:, lx, here, :] = home[0, :, 0]
    rows_ref[:, lx, there, :] = core[:, 0]
    rows_ref[:, 1 - lx, here, :] = side[...]
    rows_ref[:, 1 - lx, there, :] = cross[...]
    wide = 2 * half
    tile_ref[...] = jnp.concatenate([rows_ref[:, :, 0:4, :], rows_ref[:, :, wide - 4 : wide, :]], axis=2)


def join(scalars, field, core, side, cross, edge, name):
    _, _, batch, rows, cols, chans = field.shape
    flat = field.reshape((-1,) + field.shape[2:])

    def row_of(s):
        return s[0] if edge else 1 - s[0]

    step = batch // 2
    return call(
        functools.partial(join_kernel, edge),
        batch // step,
        scalars,
        [
            (flat, (1, step, 1, cols, chans), lambda i, s: (2 * s[0] + s[1], i, row_of(s), 0, 0)),
            (core, (step, 1, cols, chans), lambda i, s: (i, row_of(s), 0, 0)),
            by_sample(side, step),
            by_sample(cross, step),
        ],
        [out_by_sample((batch, 2, 2 * cols, chans), step), out_by_sample((batch, 2, 8, chans), step)],
        [],
        name,
    )


def edges_kernel(s_ref, pair, pair_tile, following, following_tile, pair_out, next_out):
    wide = pair.shape[2]
    pair_out[:, 0:wide, :] = pair[:, 0]
    pair_out[:, wide : wide + 8, :] = pair_tile[:, 0]
    next_out[:, 0:wide, :] = following[:, 0]
    next_out[:, wide : wide + 8, :] = following_tile[:, 0]


def edges(scalars, rows, tile, name):
    batch, _, wide, chans = rows.shape
    step = batch // 2
    shape = (batch, wide + 8, chans)
    return call(
        edges_kernel,
        batch // step,
        scalars,
        [
            (rows, (step, 1, wide, chans), lambda i, s: (i, 1 - s[2], 0, 0)),
            (tile, (step, 1, 8, chans), lambda i, s: (i, 1 - s[2], 0, 0)),
            (rows, (step, 1, wide, chans), lambda i, s: (i, s[2], 0, 0)),
            (tile, (step, 1, 8, chans), lambda i, s: (i, s[2], 0, 0)),
        ],
        [out_by_sample(shape, step), out_by_sample(shape, step)],
        [],
        name,
    )


def gather(scalars, field, name):
    side_edge, cross_edge, core, side_inner, cross_inner = pack(scalars, field, name + "_pack")
    side_edge = permute(side_edge, to_side)
    cross_edge = permute(cross_edge, to_cross)
    core = permute(core, to_core)
    side_inner = permute(side_inner, to_side)
    cross_inner = permute(cross_inner, to_cross)
    edge, tile = join(scalars, field, core, side_edge, cross_edge, True, name + "_edge")
    edge_tile = permute(tile, to_east)
    halos = exchange_rows(*edges(scalars, edge, edge_tile, name + "_halo"))
    inner, tile = join(scalars, field, core, side_inner, cross_inner, False, name + "_inner")
    inner_tile = permute(tile, to_east)
    return (edge, edge_tile, inner, inner_tile), halos


def row_of_parts(parts, row):
    edge, edge_tile, inner, inner_tile = parts
    rows, tiles = (edge, edge_tile) if row in (0, 3) else (inner, inner_tile)
    slot = 0 if row < 2 else 1
    return rows[:, slot], tiles[:, slot]


def ring_row(values, pad, row, high, low):
    step, wide, chans = values.shape
    pad[row, :, 8 : 8 + wide, :] = values
    pad[row, :, 0:8, :] = values[:, wide - 8 : wide]
    pad[row, :, 8 + wide : 16 + wide, :] = values[:, 0:8]
    for tap in range(3):
        shifted = values if tap == 1 else pad[row, :, 7 + tap : 7 + tap + wide, :]
        at = (row * 3 + tap) * chans
        high[:, at : at + chans], low[:, at : at + chans] = split(shifted.reshape(step * wide, chans))


def pair_of_rows(pair, high, low, weight_high, weight_low):
    chans = weight_high.shape[1] // 2
    at = slice(pair * 6 * chans, (pair * 6 + 12) * chans)
    total = jnp.dot(high[:, at], weight_high[...], preferred_element_type=F32)
    total += jnp.dot(low[:, at], weight_high[...], preferred_element_type=F32)
    total += jnp.dot(high[:, at], weight_low[...], preferred_element_type=F32)
    return total[:, :chans], total[:, chans:]


def north_south(s_ref, pair, following):
    odd = s_ref[2] == 1
    first, second = pair[...], following[...]
    return jnp.where(odd, first, second), jnp.where(odd, second, first)


def put_edges(s_ref, top, bottom, pair_out, next_out):
    odd = s_ref[2] == 1
    pair_out[...] = jnp.where(odd, top, bottom)
    next_out[...] = jnp.where(odd, bottom, top)


def lanes(values):
    return jnp.sum(values.reshape(-1, 8, values.shape[-1]), axis=0)


def fold(total):
    return jnp.sum(total, axis=0, keepdims=True)


def add_moments(active, first, shift, sums, others):
    @pl.when(first)
    def _():
        mean = jnp.mean(active[0].reshape(-1, active[0].shape[-1]), axis=0, keepdims=True)
        shift[...] = jnp.broadcast_to(mean, shift.shape)
        sums[...] = jnp.zeros_like(sums)

    base = shift[0:1, :]
    for at, values in enumerate(active):
        distance = values - base
        sums[0] += lanes(distance)
        sums[1] += lanes(distance * distance)
        if others is not None:
            sums[2] += lanes(others[at])
            sums[3] += lanes(others[at] * distance)


def put_moments(out_ref, shift, sums, count, others):
    total, squares = fold(sums[0]), fold(sums[1])
    offset = total / count
    out_ref[...] = jnp.zeros_like(out_ref)
    out_ref[0:1, :] = shift[0:1, :] + offset
    out_ref[1:2, :] = squares - total * offset
    if others:
        weight = fold(sums[2])
        out_ref[2:3, :] = weight
        out_ref[3:4, :] = fold(sums[3]) - weight * offset


def conv_scratch(wide, chans):
    return [
        pltpu.VMEM((6, STEP, wide + 16, chans), F32),
        pltpu.VMEM((STEP * wide, 18 * chans), BF16),
        pltpu.VMEM((STEP * wide, 18 * chans), BF16),
    ]


def first_kernel(
    count, s_ref, edge, edge_tile, inner, inner_tile, pair, following, weight_high, weight_low, bias,
    z_ref, pair_out, next_out, six_ref, stat_ref, pad, high, low, shift, sums,
):
    step = pl.program_id(0)
    own = edge.shape[2]
    wide = own + 8
    north, south = north_south(s_ref, pair, following)
    parts = (edge, edge_tile, inner, inner_tile)
    for row in range(6):
        if row in (0, 5):
            values = north if row == 0 else south
        else:
            values = jnp.concatenate(row_of_parts(parts, row - 1), axis=1)
        six_ref[:, row] = values
        ring_row(values, pad, row, high, low)
    active = []
    rows = []
    for two in range(2):
        for total in pair_of_rows(two, high, low, weight_high, weight_low):
            z = (total + bias[0:1, :]).reshape(-1, wide, total.shape[-1])
            z_ref[:, len(rows)] = z
            rows.append(z)
            active.append(z[:, :own] * sigmoid(z[:, :own]))
    put_edges(s_ref, rows[0], rows[3], pair_out, next_out)
    add_moments(active, step == 0, shift, sums, None)

    @pl.when(step == pl.num_programs(0) - 1)
    def _():
        put_moments(stat_ref, shift, sums, count, False)


def first_conv(scalars, parts, halos, weight, bias):
    batch, _, own, chans = parts[0].shape
    wide = own + 8
    return call(
        functools.partial(first_kernel, float(batch * 4 * own)),
        batch // STEP,
        scalars,
        [by_sample(a) for a in parts + halos] + [whole(a) for a in weight + (bias,)],
        [
            out_by_sample((batch, 4, wide, chans)),
            out_by_sample((batch, wide, chans)),
            out_by_sample((batch, wide, chans)),
            out_by_sample((batch, 6, wide, chans)),
            out_whole((8, chans)),
        ],
        conv_scratch(wide, chans) + [pltpu.VMEM((8, chans), F32), pltpu.VMEM((4, 8, chans), F32)],
        "conv_one",
        1.2e10,
    )


def second_kernel(
    count, s_ref, z1, pair, following, g_edge, g_inner, coef, weight_high, weight_low, bias,
    z_ref, pair_out, next_out, six_ref, stat_ref, pad, high, low, shift, sums,
):
    step = pl.program_id(0)
    own = g_edge.shape[2]
    wide = own + 8
    center, scale, offset = coef[0:1, :], coef[1:2, :], coef[2:3, :]
    north, south = north_south(s_ref, pair, following)
    for row in range(6):
        values = north if row == 0 else south if row == 5 else z1[:, row - 1]
        hidden = (values * sigmoid(values) - center) * scale + offset
        if row in (0, 5):
            hidden = jnp.where(s_ref[3 if row == 0 else 4] == 1, 0.0, hidden)
        six_ref[:, row] = hidden
        ring_row(hidden, pad, row, high, low)
    active = []
    rows = []
    for two in range(2):
        for total in pair_of_rows(two, high, low, weight_high, weight_low):
            z = (total + bias[0:1, :]).reshape(-1, wide, total.shape[-1])
            z_ref[:, len(rows)] = z
            rows.append(z)
            active.append(z[:, :own] * sigmoid(z[:, :own]))
    put_edges(s_ref, rows[0], rows[3], pair_out, next_out)
    others = [g_edge[:, 0], g_inner[:, 0], g_inner[:, 1], g_edge[:, 1]]
    add_moments(active, step == 0, shift, sums, others)

    @pl.when(step == pl.num_programs(0) - 1)
    def _():
        put_moments(stat_ref, shift, sums, count, True)


def second_conv(scalars, z1, halos, g_parts, coef, weight, bias):
    batch, _, wide, chans = z1.shape
    own = wide - 8
    return call(
        functools.partial(second_kernel, float(batch * 4 * own)),
        batch // STEP,
        scalars,
        [by_sample(a) for a in (z1,) + halos + (g_parts[0], g_parts[2])]
        + [whole(a) for a in (coef,) + weight + (bias,)],
        [
            out_by_sample((batch, 4, wide, chans)),
            out_by_sample((batch, wide, chans)),
            out_by_sample((batch, wide, chans)),
            out_by_sample((batch, 6, wide, chans)),
            out_whole((8, chans)),
        ],
        conv_scratch(wide, chans) + [pltpu.VMEM((8, chans), F32), pltpu.VMEM((4, 8, chans), F32)],
        "conv_two",
        1.2e10,
    )


def put_pieces(s_ref, rows, pieces):
    lx, nc = s_ref[0], s_ref[1]
    half = rows.shape[2] // 2
    here = pl.ds(pl.multiple_of(nc * half, half), half)
    there = pl.ds(pl.multiple_of((1 - nc) * half, half), half)
    for row in range(2):
        pieces[0][:, row] = rows[2 * lx + row, :, here, :]
        pieces[1][:, row] = rows[2 * lx + row, :, there, :]
        pieces[2][:, row] = rows[2 - 2 * lx + row, :, here, :]
        pieces[3][:, row] = rows[2 - 2 * lx + row, :, there, :]


def output_kernel(s_ref, z2, six, coef, home, core, side, cross, rows):
    own = rows.shape[2]
    center, scale, offset = coef[0:1, :], coef[1:2, :], coef[2:3, :]
    for row in range(4):
        z = z2[:, row, :own]
        rows[row] = six[:, row + 1, :own] + ((z * sigmoid(z) - center) * scale + offset)
    put_pieces(s_ref, rows, (home, core, side, cross))


def output_pieces(scalars, z2, six, coef):
    batch, _, wide, chans = z2.shape
    own = wide - 8
    piece = (batch, 2, own // 2, chans)
    return call(
        output_kernel,
        batch // STEP,
        scalars,
        [by_sample(z2), by_sample(six), whole(coef)],
        [out_by_sample(piece)] * 4,
        [pltpu.VMEM((4, STEP, own, chans), F32)],
        "output",
    )


def send_home(pieces):
    home, core, side, cross = pieces
    side, cross = permute(side, to_side), permute(cross, to_cross)
    return home, permute(core, to_core), side, cross


def place_kernel(s_ref, home, core, side, cross, out):
    part = pl.program_id(0)
    for at, piece in enumerate((home, core, side, cross)):

        @pl.when(part == at)
        def _(piece=piece):
            out[0] = piece[...]


def place(scalars, pieces, name):
    shape = pieces[0].shape

    def to(i, s):
        return 2 * (s[0] ^ (i // 2)) + (s[1] ^ (i % 2)), 0, 0, 0, 0

    return call(
        place_kernel,
        4,
        scalars,
        [whole(a) for a in pieces],
        [((4,) + shape, F32, (1,) + shape, to)],
        [],
        name,
    )[0]


def silu_and_slope(z):
    sigma = sigmoid(z)
    return z * sigma, sigma * (1.0 + z * (1.0 - sigma))


def third_kernel(
    s_ref, z2, pair, following, g_edge, g_edge_tile, g_inner, g_inner_tile, g_pair, g_following, z1, coef,
    weight_high, weight_low, dh_ref, pair_out, next_out, dz_ref, stat_ref, pad, high, low, sums,
):
    step = pl.program_id(0)
    own = g_edge.shape[2]
    wide = own + 8
    center, inverse, scale = coef[0:1, :], coef[1:2, :], coef[2:3, :]
    mean_shift, mean_gain = coef[3:4, :], coef[4:5, :]
    center_one, inverse_one = coef[5:6, :], coef[6:7, :]

    @pl.when(step == 0)
    def _():
        sums[...] = jnp.zeros_like(sums)

    north, south = north_south(s_ref, pair, following)
    g_north, g_south = north_south(s_ref, g_pair, g_following)
    parts = (g_edge, g_edge_tile, g_inner, g_inner_tile)
    for row in range(6):
        if row in (0, 5):
            z, g = (north, g_north) if row == 0 else (south, g_south)
        else:
            z, g = z2[:, row - 1], jnp.concatenate(row_of_parts(parts, row - 1), axis=1)
        active, slope = silu_and_slope(z)
        normed = (active - center) * inverse
        dz = scale * (g - mean_shift - normed * mean_gain) * slope
        if row in (0, 5):
            dz = jnp.where(s_ref[3 if row == 0 else 4] == 1, 0.0, dz)
        else:
            dz_ref[:, row - 1] = dz[:, :own]
            sums[2] += lanes(dz[:, :own])
        ring_row(dz, pad, row, high, low)
    rows = []
    for two in range(2):
        for total in pair_of_rows(two, high, low, weight_high, weight_low):
            dh = total.reshape(-1, wide, total.shape[-1])
            row = len(rows)
            dh_ref[:, row] = dh
            rows.append(dh)
            z = z1[:, row, :own]
            sums[0] += lanes(dh[:, :own])
            sums[1] += lanes(dh[:, :own] * ((z * sigmoid(z) - center_one) * inverse_one))
    put_edges(s_ref, rows[0], rows[3], pair_out, next_out)

    @pl.when(step == pl.num_programs(0) - 1)
    def _():
        stat_ref[...] = jnp.zeros_like(stat_ref)
        for at in range(3):
            stat_ref[at : at + 1, :] = fold(sums[at])


def third_conv(scalars, z2, halos, g_parts, g_halos, z1, coef, weight):
    batch, _, wide, chans = z2.shape
    own = wide - 8
    return call(
        third_kernel,
        batch // STEP,
        scalars,
        [by_sample(a) for a in (z2,) + halos + g_parts + g_halos + (z1,)]
        + [whole(a) for a in (coef,) + weight],
        [
            out_by_sample((batch, 4, wide, chans)),
            out_by_sample((batch, wide, chans)),
            out_by_sample((batch, wide, chans)),
            out_by_sample((batch, 4, own, chans)),
            out_whole((8, chans)),
        ],
        conv_scratch(wide, chans) + [pltpu.VMEM((3, 8, chans), F32)],
        "conv_three",
        1.2e10,
    )


def fourth_kernel(
    s_ref, dh, pair, following, z1, z_pair, z_following, g_edge, g_inner, coef, weight_high, weight_low,
    home, core, side, cross, dz_ref, stat_ref, pad, high, low, sums, grads,
):
    step = pl.program_id(0)
    own = g_edge.shape[2]
    wide = own + 8
    center, inverse, scale = coef[0:1, :], coef[1:2, :], coef[2:3, :]
    mean_shift, mean_gain = coef[3:4, :], coef[4:5, :]

    @pl.when(step == 0)
    def _():
        sums[...] = jnp.zeros_like(sums)

    north, south = north_south(s_ref, pair, following)
    z_north, z_south = north_south(s_ref, z_pair, z_following)
    for row in range(6):
        if row in (0, 5):
            z, q = (z_north, north) if row == 0 else (z_south, south)
        else:
            z, q = z1[:, row - 1], dh[:, row - 1]
        active, slope = silu_and_slope(z)
        normed = (active - center) * inverse
        dz = scale * (q - mean_shift - normed * mean_gain) * slope
        if row in (0, 5):
            dz = jnp.where(s_ref[3 if row == 0 else 4] == 1, 0.0, dz)
        else:
            dz_ref[:, row - 1] = dz[:, :own]
            sums[0] += lanes(dz[:, :own])
        ring_row(dz, pad, row, high, low)
    others = [g_edge[:, 0], g_inner[:, 0], g_inner[:, 1], g_edge[:, 1]]
    row = 0
    for two in range(2):
        for total in pair_of_rows(two, high, low, weight_high, weight_low):
            grads[row] = others[row] + total.reshape(-1, wide, total.shape[-1])[:, :own]
            row += 1
    put_pieces(s_ref, grads, (home, core, side, cross))

    @pl.when(step == pl.num_programs(0) - 1)
    def _():
        stat_ref[...] = jnp.zeros_like(stat_ref)
        stat_ref[0:1, :] = fold(sums[0])


def fourth_conv(scalars, dh, halos, z1, z_halos, g_parts, coef, weight):
    batch, _, wide, chans = dh.shape
    own = wide - 8
    piece = (batch, 2, own // 2, chans)
    return call(
        fourth_kernel,
        batch // STEP,
        scalars,
        [by_sample(a) for a in (dh,) + halos + (z1,) + z_halos + (g_parts[0], g_parts[2])]
        + [whole(a) for a in (coef,) + weight],
        [out_by_sample(piece)] * 4 + [out_by_sample((batch, 4, own, chans)), out_whole((8, chans))],
        conv_scratch(wide, chans) + [pltpu.VMEM((1, 8, chans), F32), pltpu.VMEM((4, STEP, own, chans), F32)],
        "conv_four",
        1.2e10,
    )


def weight_kernel(s_ref, six, dz, out_ref, pad, high, low, total):
    step = pl.program_id(0)
    own, chans = dz.shape[2], dz.shape[3]
    wide = own + 8
    for row in range(6):
        values = six[:, row]
        pad[row, :, 8 : 8 + wide, :] = values
        pad[row, :, 0:8, :] = values[:, own:wide]
        for tap in range(3):
            shifted = values[:, :own] if tap == 1 else pad[row, :, 7 + tap : 7 + tap + own, :]
            at = (row * 3 + tap) * chans
            high[:, at : at + chans], low[:, at : at + chans] = split(shifted.reshape(-1, chans))

    @pl.when(step == 0)
    def _():
        total[...] = jnp.zeros_like(total)

    def product(left, right):
        return lax.dot_general(left, right, (((0,), (0,)), ((), ())), preferred_element_type=F32)

    sums = None
    for two in range(2):
        at = slice(two * 6 * chans, (two * 6 + 12) * chans)
        slope = jnp.concatenate(
            [dz[:, 2 * two].reshape(-1, chans), dz[:, 2 * two + 1].reshape(-1, chans)], axis=1
        )
        slope_high, slope_low = split(slope)
        part = product(high[:, at], slope_high)
        part += product(low[:, at], slope_high)
        part += product(high[:, at], slope_low)
        sums = part if sums is None else sums + part
    total[...] += sums

    @pl.when(step == pl.num_programs(0) - 1)
    def _():
        line = 3 * chans
        for row in range(3):
            out_ref[row * line : (row + 1) * line, :] = (
                total[row * line : (row + 1) * line, :chans] + total[(row + 1) * line : (row + 2) * line, chans:]
            )


def weight_grad(scalars, six, dz, name):
    batch, _, own, chans = dz.shape
    return call(
        weight_kernel,
        batch // STEP,
        scalars,
        [by_sample(six), by_sample(dz)],
        [out_whole((9 * chans, chans))],
        [
            pltpu.VMEM((6, STEP, own + 16, chans), F32),
            pltpu.VMEM((STEP * own, 18 * chans), BF16),
            pltpu.VMEM((STEP * own, 18 * chans), BF16),
            pltpu.VMEM((12 * chans, 2 * chans), F32),
        ],
        name,
        1.5e10,
    )[0]


def pack_weight(kernel):
    nothing = jnp.zeros_like(kernel[:1])
    both = jnp.stack(
        [jnp.concatenate([kernel, nothing], axis=0), jnp.concatenate([nothing, kernel], axis=0)], axis=3
    )
    both = both.reshape(4 * 3 * kernel.shape[2], 2 * kernel.shape[3])
    high = lax.reduce_precision(both, exponent_bits=8, mantissa_bits=7)
    return high.astype(BF16), (both - high).astype(BF16)


def flipped(kernel):
    return jnp.transpose(kernel[::-1, ::-1], (0, 1, 3, 2))


def rows_of(*vectors):
    filled = [jnp.reshape(v, (1, -1)) for v in vectors]
    nothing = jnp.zeros((8 - len(filled), filled[0].shape[1]), F32)
    return jnp.concatenate(filled + [nothing], axis=0)


def all_moments(stats, here):
    count = here
    for target in group_steps():
        other = permute(stats, target)
        mean = 0.5 * (stats[0] + other[0])
        gap = stats[0] - other[0]
        squares = stats[1] + other[1] + gap * gap * (0.5 * count)
        weight = stats[2] + other[2]
        product = (stats[3] + (stats[0] - mean) * stats[2]) + (other[3] + (other[0] - mean) * other[2])
        stats = rows_of(mean, squares, weight, product)
        count = 2.0 * count
    return stats


def all_sums(stats):
    for target in group_steps():
        stats = stats + permute(stats, target)
    return stats


def shards(
    fields, weight_one, bias_one, gain_one, shift_one, weight_two, bias_two, gain_two, shift_two, cotangent
):
    parts_here, batch, rows_here, cols_here, chans = fields.shape
    lat, lon = lax.axis_index("lat"), lax.axis_index("lon")
    lats, lons = lax.axis_size("lat"), lax.axis_size("lon")
    assert (parts_here, rows_here, lons) == (4, 2, 4)
    here = float(batch * 4 * 2 * cols_here)
    members = float(lats * lons // 4)
    count = here * members
    pair = lat // 2
    scalars = jnp.stack([lat % 2, lon % 2, pair % 2, pair == 0, pair == lats // 2 - 1]).astype(jnp.int32)
    cells = fields.reshape((2, 2) + fields.shape[1:])
    slopes = cotangent.reshape((2, 2) + cotangent.shape[1:])

    x_parts, x_halos = gather(scalars, cells, "x")
    tied = lax.optimization_barrier((slopes, x_parts[3]))
    g_parts, g_halos = gather(scalars, tied[0], "g")

    z1, pair_row, next_row, x_six, stats = first_conv(
        scalars, x_parts, x_halos, pack_weight(weight_one), rows_of(bias_one)
    )
    z1_halos = exchange_rows(pair_row, next_row)
    stats = all_moments(stats, here)
    center_one, spread_one = stats[0], stats[1] / count
    inv_one = lax.rsqrt(spread_one + EPSILON)

    z2, pair_row, next_row, h_six, stats = second_conv(
        scalars, z1, z1_halos, g_parts, rows_of(center_one, gain_one * inv_one, shift_one),
        pack_weight(weight_two), rows_of(bias_two),
    )
    z2_halos = exchange_rows(pair_row, next_row)
    stats = all_moments(stats, here)
    center_two, spread_two, dshift_two = stats[0], stats[1] / count, stats[2]
    inv_two = lax.rsqrt(spread_two + EPSILON)
    dgain_two = stats[3] * inv_two

    pieces = output_pieces(scalars, z2, x_six, rows_of(center_two, gain_two * inv_two, shift_two))
    output = place(scalars, send_home(pieces), "output_place")

    dh1, pair_row, next_row, dz2, stats = third_conv(
        scalars, z2, z2_halos, g_parts, g_halos, z1,
        rows_of(
            center_two, inv_two, gain_two * inv_two, dshift_two / count, dgain_two / count, center_one, inv_one
        ),
        pack_weight(flipped(weight_two)),
    )
    dh1_halos = exchange_rows(pair_row, next_row)
    dbias_two = stats[2]
    grad_w2 = weight_grad(scalars, h_six, dz2, "weight_two")
    stats = all_sums(stats)
    dshift_one, dgain_one = stats[0], stats[1]

    *pieces, dz1, stats = fourth_conv(
        scalars, dh1, dh1_halos, z1, z1_halos, g_parts,
        rows_of(center_one, inv_one, gain_one * inv_one, dshift_one / count, dgain_one / count),
        pack_weight(flipped(weight_one)),
    )
    input_grad = place(scalars, send_home(pieces), "grad_place")
    dbias_one = stats[0]
    grad_w1 = weight_grad(scalars, x_six, dz1, "weight_one")

    small = jnp.stack([
        dbias_one, dgain_one / members, dshift_one / members,
        dbias_two, dgain_two / members, dshift_two / members,
    ])
    grad_w1, grad_w2, small = lax.psum((grad_w1, grad_w2, small), AXES)
    return (
        output.reshape(fields.shape),
        input_grad.reshape(fields.shape),
        grad_w1.reshape(weight_one.shape),
        small[0],
        small[1],
        small[2],
        grad_w2.reshape(weight_two.shape),
        small[3],
        small[4],
        small[5],
    )


def solution(mesh):
    field = P(None, None, "lat", "lon", None)
    return jax.shard_map(
        shards,
        mesh=mesh,
        in_specs=(field,) + (P(),) * 8 + (field,),
        out_specs=(field, field) + (P(),) * 8,
        check_vma=False,
    )
```

time: 973 us -> 430 us (0.44)
  matrix products: 262 us -> 0 us
  blocking collectives: 310 us -> 50.6 us
  Pallas kernels: 0 us -> 119 us
  starting transfers between devices: 129 us -> 55.3 us
  other arithmetic: 63.7 us -> 14.6 us
    psum x7 -> x1, blocking collectives: 310 us -> 50.6 us  [shards(): grad_w1, grad_w2, small = lax.psum((grad_w1, grad_w2, small), AXES)]
    conv_general_dilated x16 -> x0, matrix products: 150 us -> none  [correlate(): lax.conv_general_dilated(extended, kernel, (1, 1), 'VALID', dimension_num...]
    pallas_call x0 -> x17, Pallas kernels: none -> 119 us  [call(): pl.pallas_call(body, grid_spec=pltpu.PrefetchScalarGridSpec(num_scalar_pr...]
    dot_general x72 -> x0, matrix products: 113 us -> none  [kernel_grad(): jnp.einsum('bhwc,bhwd->cd', window, slope, precision=lax.Precision.HIGHEST)]
    ppermute x64 -> x39, starting transfers between devices: 129 us -> 55.2 us  [permute(): return lax.ppermute(value, AXES, pairs)]
    ppermute x64 -> x39, waiting for transfers between devices: 125 us -> 68.8 us  [permute(): return lax.ppermute(value, AXES, pairs)]
    psum x1, waiting for transfers between devices: 19.2 us -> 71.5 us  [shards(): grad_w1, grad_w2, small = lax.psum((grad_w1, grad_w2, small), AXES)]
    reduce_sum x19 -> x0, other arithmetic: 30.6 us -> none  [the longest x8 9.41 us: moments(): local_squares = jnp.sum(deviate * deviate, axis=(0, 1, 2))]
  transfers between devices with their start and end apart: 65 -> 40, of which waited for: 11 -> 16; matrix products, arithmetic and copies ran while one was open for 29% -> 8% of each run, Pallas kernels for 0% -> 20%
where the time goes in v1:
time: 430 us; the launch traced here: 429 us
  waiting for transfers between devices  140 us (33%)
  Pallas kernels  119 us (28%)
  starting transfers between devices  55.3 us (13%)
  blocking collectives  50.6 us (12%)
  local copies, waits for them, and re-layouts  34.4 us (8%)
  other arithmetic  14.6 us (3%)
  between operations  14.6 us (3%)
    pallas_call x17, Pallas kernels, call(): pl.pallas_call(body, grid_spec=pltpu.PrefetchScalarGridSpec(num_scalar_pr...  119 us
    psum x1, waiting for transfers between devices, shards(): grad_w1, grad_w2, small = lax.psum((grad_w1, grad_w2, small), AXES)  71.5 us
    ppermute x39, waiting for transfers between devices, permute(): return lax.ppermute(value, AXES, pairs)  68.8 us
    ppermute x39, starting transfers between devices, permute(): return lax.ppermute(value, AXES, pairs)  55.2 us
    psum x1, blocking collectives, shards(): grad_w1, grad_w2, small = lax.psum((grad_w1, grad_w2, small), AXES)  50.6 us
    another operation x8, local copies, waits for them, and re-layouts, pack_weight(): jnp.stack([jnp.concatenate([kernel, nothing], axis=0), jnp.concatenate([n...  16.2 us
    unnamed x98, local copies, waits for them, and re-layouts  13.9 us
  transfers between devices with their start and end apart: 40, of which 16 were waited for; matrix products, arithmetic and copies ran while one was open for 8% of the time, Pallas kernels for 20%

profile of v1, /device:TPU:0, one launch (start us, length us, event | category | flops | bytes accessed | tf_op | source)
XLA Modules:
  0.0 429.2 jit_solution(4731531617949408733)
XLA Ops:
  17.1 3.7 copy.22
  24.0 8.1 %collective-permute-done.2.cross = f32[12,64,128]{2,1,0:T(8,128)S(1)} collective-permute-done((f32[12,64,128]{2,1,0:T(8,128)}, f32[12,64,128]{2,1,0:T(8,128)S(1)}, u32[]{:S(2)}, u32[]{:S(2)}) %collective-permute-start.2) | collective-permute-done | bytes 393248 | tf_op jit(solution)/shard_map/ppermute | solution.py:27
  43.9 5.1 %collective-permute-done.5.cross = f32[12,64,128]{2,1,0:T(8,128)S(1)} collective-permute-done((f32[12,64,128]{2,1,0:T(8,128)S(1)}, f32[12,64,128]{2,1,0:T(8,128)S(1)}, u32[]{:S(2)}, u32[]{:S(2)}) %collective-permute-start.5) | collective-permute-done | bytes 393248 | tf_op jit(solution)/shard_map/ppermute | solution.py:27
  52.9 2.8 collective-permute-done.6.inner_tile
  60.3 13.4 %conv_one.1 = (f32[12,4,136,128]{3,2,1,0:T(8,128)}, f32[12,136,128]{2,1,0:T(8,128)S(1)}, f32[12,136,128]{2,1,0:T(8,128)S(1)}, f32[12,6,136,128]{3,2,1,0:T(8,128)}, f32[8,128]{1,0:T(8,128)S(1)}) custom-call(s32[5]{0:T(128)S(1)} %stack.74.s_ref, f32[12,2,128,128]{3,2,1,0:T(8,128)} %copy-done.4, ...), custom_call_target="tpu_custom_call" | custom-call | flops 12000000000 | bytes 16621568 | tf_op jit(solution)/shard_map/conv_one/pallas_call | solution.py:87
  78.0 4.7 %collective-permute-start.17 = (f32[8,128]{1,0:T(8,128)S(1)}, f32[8,128]{1,0:T(8,128)S(1)}, u32[]{:S(2)}, u32[]{:S(2)}) collective-permute-start(f32[8,128]{1,0:T(8,128)S(1)} %concatenate.57), channel_id=1, source_target_pairs={{0,8},{1,9},{2,10},{3,11},{4,12},{5,13},{6,14},{7,15},{8,0},{9,1},... | collective-permute-start | bytes 12296 | tf_op jit(solution)/shard_map/ppermute | solution.py:27
  88.7 4.6 %collective-permute-start.9 = (f32[12,136,128]{2,1,0:T(8,128)}, f32[12,136,128]{2,1,0:T(8,128)S(1)}, u32[]{:S(2)}, u32[]{:S(2)}) collective-permute-start(f32[12,136,128]{2,1,0:T(8,128)} %copy-done.15), channel_id=1, source_target_pairs={{0,8},{1,9},{2,10},{3,11},{4,12},{5,13},{6,14},{7,15},{8,0},{9,1},... | collective-permute-start | bytes 2506760 | tf_op jit(solution)/shard_map/ppermute | solution.py:27
  93.3 2.9 collective-permute-done.15.cross
  97.0 7.3 %collective-permute-start.18 = (f32[8,128]{1,0:T(8,128)S(1)}, f32[8,128]{1,0:T(8,128)S(1)}, u32[]{:S(2)}, u32[]{:S(2)}) collective-permute-start(f32[8,128]{1,0:T(8,128)S(1)} %concatenate.58), channel_id=1, source_target_pairs={{0,16},{1,17},{2,18},{3,19},{4,20},{5,21},{6,22},{7,23},{8,24},{9,... | collective-permute-start | bytes 12296 | tf_op jit(solution)/shard_map/ppermute | solution.py:27
  113.6 10.2 %collective-permute-done.18 = f32[8,128]{1,0:T(8,128)S(1)} collective-permute-done((f32[8,128]{1,0:T(8,128)S(1)}, f32[8,128]{1,0:T(8,128)S(1)}, u32[]{:S(2)}, u32[]{:S(2)}) %collective-permute-start.18) | collective-permute-done | bytes 4128 | tf_op jit(solution)/shard_map/ppermute | solution.py:27
  124.4 16.1 %conv_two.1 = (f32[12,4,136,128]{3,2,1,0:T(8,128)}, f32[12,136,128]{2,1,0:T(8,128)S(1)}, f32[12,136,128]{2,1,0:T(8,128)S(1)}, f32[12,6,136,128]{3,2,1,0:T(8,128)}, f32[8,128]{1,0:T(8,128)S(1)}) custom-call(s32[5]{0:T(128)S(1)} %stack.74.s_ref, f32[12,4,136,128]{3,2,1,0:T(8,128)} %get-tuple-element.69.z1, ...), custom_call_target="tpu_custom_call" | custom-call | flops 12000000000 | bytes 19771392 | tf_op jit(solution)/shard_map/conv_two/pallas_call | solution.py:87
  160.8 2.7 pad_maximum_fusion.3
  163.4 3.8 copy.23
  167.2 24.2 %collective-permute-done.21 = f32[8,128]{1,0:T(8,128)S(1)} collective-permute-done((f32[8,128]{1,0:T(8,128)S(1)}, f32[8,128]{1,0:T(8,128)S(1)}, u32[]{:S(2)}, u32[]{:S(2)}) %collective-permute-start.21) | collective-permute-done | bytes 4128 | tf_op jit(solution)/shard_map/ppermute | solution.py:27
  196.7 17.2 %conv_three.1 = (f32[12,4,136,128]{3,2,1,0:T(8,128)}, f32[12,136,128]{2,1,0:T(8,128)}, f32[12,136,128]{2,1,0:T(8,128)}, f32[12,4,128,128]{3,2,1,0:T(8,128)}, f32[8,128]{1,0:T(8,128)S(1)}) custom-call(s32[5]{0:T(128)S(1)} %stack.74.s_ref, f32[12,4,136,128]{3,2,1,0:T(8,128)} %get-tuple-element.81.z2, f32[12,136,128]{2,1,0:T(8,128)} %collective-permute-done.25.pair, ...), custom_call_target="tpu_custom_call" | custom-call | flops 12000000000 | bytes 23109632 | tf_op jit(solution)/shard_map/conv_three/pallas_call | solution.py:87
  217.7 7.4 %output.1 = (f32[12,2,64,128]{3,2,1,0:T(8,128)S(1)}, f32[12,2,64,128]{3,2,1,0:T(8,128)}, f32[12,2,64,128]{3,2,1,0:T(8,128)}, f32[12,2,64,128]{3,2,1,0:T(8,128)}) custom-call(s32[5]{0:T(128)S(1)} %stack.74.s_ref, f32[12,4,136,128]{3,2,1,0:T(8,128)} %get-tuple-element.81.z2, f32[12,6,136,128]{3,2,1,0:T(8,128)} %get-tuple-element.82.six, ...), custom_call_target="tpu_custom_call" | custom-call | bytes 11505664 | tf_op jit(solution)/shard_map/output/pallas_call | solution.py:87
  230.9 13.5 %weight_two.1 = f32[1152,128]{1,0:T(8,128)S(1)} custom-call(s32[5]{0:T(128)S(1)} %stack.74.s_ref, f32[12,6,136,128]{3,2,1,0:T(8,128)} %get-tuple-element.104.six, f32[12,4,128,128]{3,2,1,0:T(8,128)S(1)} %copy-done.16), custom_call_target="tpu_custom_call" | custom-call | flops 15000000512 | bytes 8749056 | tf_op jit(solution)/shard_map/weight_two/pallas_call | solution.py:87
  245.2 4.6 %collective-permute-done.35 = f32[8,128]{1,0:T(8,128)S(1)} collective-permute-done((f32[8,128]{1,0:T(8,128)S(1)}, f32[8,128]{1,0:T(8,128)S(1)}, u32[]{:S(2)}, u32[]{:S(2)}) %collective-permute-start.35) | collective-permute-done | bytes 4128 | tf_op jit(solution)/shard_map/ppermute | solution.py:27
  252.5 16.8 %conv_four.1 = (f32[12,2,64,128]{3,2,1,0:T(8,128)S(1)}, f32[12,2,64,128]{3,2,1,0:T(8,128)}, f32[12,2,64,128]{3,2,1,0:T(8,128)}, f32[12,2,64,128]{3,2,1,0:T(8,128...) custom-call(s32[5]{0:T(128)S(1)} %stack.74.s_ref, f32[12,4,136,128]{3,2,1,0:T(8,128)} %get-tuple-element.94.dh, ...), custom_call_target="tpu_custom_call" | custom-call | flops 12000000000 | bytes 21045248 | tf_op jit(solution)/shard_map/conv_four/pallas_call | solution.py:87
  274.2 13.5 %weight_one.1 = f32[1152,128]{1,0:T(8,128)S(1)} custom-call(s32[5]{0:T(128)S(1)} %stack.74.s_ref, f32[12,6,136,128]{3,2,1,0:T(8,128)} %get-tuple-element.82.six, f32[12,4,128,128]{3,2,1,0:T(8,128)S(1)} %copy-done.17), custom_call_target="tpu_custom_call" | custom-call | flops 15000000512 | bytes 8749056 | tf_op jit(solution)/shard_map/weight_one/pallas_call | solution.py:87
  288.6 3.9 output_place.1
  292.5 50.6 %psum.22 = f32[6,128]{1,0:T(8,128)S(1)} all-reduce(f32[6,128]{1,0:T(8,128)S(1)} %stack.87), channel_id=1, replica_groups=mesh['lat'=8,'lon'=4] {'lat','lon'}, use_global_device_ids=true, to_apply=%region_1.2 | all-reduce | flops 768 | bytes 6144 | tf_op jit(solution)/shard_map/psum | solution.py:799
  343.7 4.4 %grad_place.1 = f32[4,12,2,64,128]{4,3,2,1,0:T(8,128)} custom-call(s32[5]{0:T(128)S(1)} %stack.74.s_ref, f32[12,2,64,128]{3,2,1,0:T(8,128)S(1)} %get-tuple-element.98.home, f32[12,2,64,128]{3,2,1,0:T(8,128)} %collective-permute-done.36.core, f32[12,2,64,128]{3,2,1,0:T(8,128)} %collective-permute-done.37.side, f32[12,2,64,128]{3,2,1,0:T(8,128)} %collective-permute-done.38.cross), custom_call_target="tpu_custom_call" | custom-call | bytes 6291456 | tf_op jit(solution)/shard_map/grad_place/pallas_call | solution.py:87
  348.0 71.5 %all-reduce.13.cloned.1.call-done = (f32[3,3,128,128]{3,2,1,0:T(8,128)}, f32[3,3,128,128]{3,2,1,0:T(8,128)}) async-done(((f32[3,3,128,128]{3,2,1,0:T(8,128)}, f32[3,3,128,128]{3,2,1,0:T(8,128)}), (f32[3,3,128,128]{3,2,1,0:T(8,128)}, f32[3,3,128,128]{3,2,1,0:T(8,128)})) %all-reduce.13.cloned.1.call-update) | async-done | bytes 1179664 | tf_op jit(solution)/shard_map/psum | solution.py:799
  (224 shorter events, 101.8 us)
Async XLA Ops:
  7.2 412.3 %all-reduce.13.cloned.1.call-start = ((), (), s32[]{:S(2)}) async-start(), calls=%async_computation | async-start | bytes 2359296 | tf_op jit(solution)/shard_map/psum | solution.py:799
  10.9 21.2 %collective-permute-start = (f32[12,2,64,128]{3,2,1,0:T(8,128)S(1)}, f32[12,2,64,128]{3,2,1,0:T(8,128)S(1)}, u32[]{:S(2)}, u32[]{:S(2)}) collective-permute-start(f32[12,2,64,128]{3,2,1,0:T(8,128)S(1)} %get-tuple-element.58), channel_id=1, source_target_pairs={{0,1},{1,0},{2,3},{3,2},{4,5},{5,4},{6,7},{7,6},{8,9},{9,8},{10,11... | collective-permute-start | bytes 2359304 | tf_op jit(solution)/shard_map/ppermute | solution.py:27
  14.0 29.9 %collective-permute-start.4 = (f32[12,64,128]{2,1,0:T(8,128)}, f32[12,64,128]{2,1,0:T(8,128)S(1)}, u32[]{:S(2)}, u32[]{:S(2)}) collective-permute-start(f32[12,64,128]{2,1,0:T(8,128)} %get-tuple-element.63), channel_id=1, source_target_pairs={{0,4},{1,5},{2,6},{3,7},{4,0},{5,1},{6,2},{7,3},{8,12},{9,13},{10,... | collective-permute-start | bytes 1179656 | tf_op jit(solution)/shard_map/ppermute | solution.py:27
  15.7 33.2 %collective-permute-start.5 = (f32[12,64,128]{2,1,0:T(8,128)S(1)}, f32[12,64,128]{2,1,0:T(8,128)S(1)}, u32[]{:S(2)}, u32[]{:S(2)}) collective-permute-start(f32[12,64,128]{2,1,0:T(8,128)S(1)} %get-tuple-element.64), channel_id=1, source_target_pairs={{0,5},{1,4},{2,7},{3,6},{4,1},{5,0},{6,3},{7,2},{8,13},{9,12},{10,... | collective-permute-start | bytes 1179656 | tf_op jit(solution)/shard_map/ppermute | solution.py:27
  57.8 39.2 %collective-permute-start.11 = (f32[12,2,64,128]{3,2,1,0:T(8,128)}, f32[12,2,64,128]{3,2,1,0:T(8,128)S(1)}, u32[]{:S(2)}, u32[]{:S(2)}) collective-permute-start(f32[12,2,64,128]{3,2,1,0:T(8,128)} %get-tuple-element.73), channel_id=1, source_target_pairs={{0,1},{1,0},{2,3},{3,2},{4,5},{5,4},{6,7},{7,6},{8,9},{9,8},{10,11... | collective-permute-start | bytes 2359304 | tf_op jit(solution)/shard_map/ppermute | solution.py:27
  86.4 22.6 %collective-permute-start.12 = (f32[12,64,128]{2,1,0:T(8,128)}, f32[12,64,128]{2,1,0:T(8,128)S(1)}, u32[]{:S(2)}, u32[]{:S(2)}) collective-permute-start(f32[12,64,128]{2,1,0:T(8,128)} %get-tuple-element.74), channel_id=1, source_target_pairs={{0,4},{1,5},{2,6},{3,7},{4,0},{5,1},{6,2},{7,3},{8,12},{9,13},{10,... | collective-permute-start | bytes 1179656 | tf_op jit(solution)/shard_map/ppermute | solution.py:27
  87.4 23.3 %collective-permute-start.13 = (f32[12,64,128]{2,1,0:T(8,128)}, f32[12,64,128]{2,1,0:T(8,128)S(1)}, u32[]{:S(2)}, u32[]{:S(2)}) collective-permute-start(f32[12,64,128]{2,1,0:T(8,128)} %get-tuple-element.75), channel_id=1, source_target_pairs={{0,5},{1,4},{2,7},{3,6},{4,1},{5,0},{6,3},{7,2},{8,13},{9,12},{10,... | collective-permute-start | bytes 1179656 | tf_op jit(solution)/shard_map/ppermute | solution.py:27
  88.7 35.7 %collective-permute-start.9 = (f32[12,136,128]{2,1,0:T(8,128)}, f32[12,136,128]{2,1,0:T(8,128)S(1)}, u32[]{:S(2)}, u32[]{:S(2)}) collective-permute-start(f32[12,136,128]{2,1,0:T(8,128)} %copy-done.15), channel_id=1, source_target_pairs={{0,8},{1,9},{2,10},{3,11},{4,12},{5,13},{6,14},{7,15},{8,0},{9,1},... | collective-permute-start | bytes 2506760 | tf_op jit(solution)/shard_map/ppermute | solution.py:27
  96.3 28.1 %collective-permute-start.10 = (f32[12,136,128]{2,1,0:T(8,128)S(1)}, f32[12,136,128]{2,1,0:T(8,128)S(1)}, u32[]{:S(2)}, u32[]{:S(2)}) collective-permute-start(f32[12,136,128]{2,1,0:T(8,128)S(1)} %get-tuple-element.71), channel_id=1, source_target_pairs={{8,16},{9,17},{10,18},{11,19},{12,20},{13,21},{14,22},{15,23},{16,... | collective-permute-start | bytes 2506760 | tf_op jit(solution)/shard_map/ppermute | solution.py:27
  97.0 26.8 %collective-permute-start.18 = (f32[8,128]{1,0:T(8,128)S(1)}, f32[8,128]{1,0:T(8,128)S(1)}, u32[]{:S(2)}, u32[]{:S(2)}) collective-permute-start(f32[8,128]{1,0:T(8,128)S(1)} %concatenate.58), channel_id=1, source_target_pairs={{0,16},{1,17},{2,18},{3,19},{4,20},{5,21},{6,22},{7,23},{8,24},{9,... | collective-permute-start | bytes 12296 | tf_op jit(solution)/shard_map/ppermute | solution.py:27
  150.6 46.1 %collective-permute-start.29 = (f32[12,136,128]{2,1,0:T(8,128)}, f32[12,136,128]{2,1,0:T(8,128)}, u32[]{:S(2)}, u32[]{:S(2)}) collective-permute-start(f32[12,136,128]{2,1,0:T(8,128)} %get-tuple-element.92), channel_id=1, source_target_pairs={{0,8},{1,9},{2,10},{3,11},{4,12},{5,13},{6,14},{7,15},{8,0},{9,1},... | collective-permute-start | bytes 2506760 | tf_op jit(solution)/shard_map/ppermute | solution.py:27
  152.6 44.0 %collective-permute-start.30 = (f32[12,136,128]{2,1,0:T(8,128)}, f32[12,136,128]{2,1,0:T(8,128)}, u32[]{:S(2)}, u32[]{:S(2)}) collective-permute-start(f32[12,136,128]{2,1,0:T(8,128)} %get-tuple-element.93), channel_id=1, source_target_pairs={{8,16},{9,17},{10,18},{11,19},{12,20},{13,21},{14,22},{15,23},{16,... | collective-permute-start | bytes 2506760 | tf_op jit(solution)/shard_map/ppermute | solution.py:27
  154.2 42.5 %collective-permute-start.25 = (f32[12,136,128]{2,1,0:T(8,128)S(1)}, f32[12,136,128]{2,1,0:T(8,128)}, u32[]{:S(2)}, u32[]{:S(2)}) collective-permute-start(f32[12,136,128]{2,1,0:T(8,128)S(1)} %get-tuple-element.88), channel_id=1, source_target_pairs={{0,8},{1,9},{2,10},{3,11},{4,12},{5,13},{6,14},{7,15},{8,0},{9,1},... | collective-permute-start | bytes 2506760 | tf_op jit(solution)/shard_map/ppermute | solution.py:27
  156.4 40.3 %collective-permute-start.26 = (f32[12,136,128]{2,1,0:T(8,128)S(1)}, f32[12,136,128]{2,1,0:T(8,128)}, u32[]{:S(2)}, u32[]{:S(2)}) collective-permute-start(f32[12,136,128]{2,1,0:T(8,128)S(1)} %get-tuple-element.89), channel_id=1, source_target_pairs={{8,16},{9,17},{10,18},{11,19},{12,20},{13,21},{14,22},{15,23},{16,... | collective-permute-start | bytes 2506760 | tf_op jit(solution)/shard_map/ppermute | solution.py:27
  158.7 32.8 %collective-permute-start.21 = (f32[8,128]{1,0:T(8,128)S(1)}, f32[8,128]{1,0:T(8,128)S(1)}, u32[]{:S(2)}, u32[]{:S(2)}) collective-permute-start(f32[8,128]{1,0:T(8,128)S(1)} %concatenate.64), channel_id=1, source_target_pairs={{0,16},{1,17},{2,18},{3,19},{4,20},{5,21},{6,22},{7,23},{8,24},{9,... | collective-permute-start | bytes 12296 | tf_op jit(solution)/shard_map/ppermute | solution.py:27
  225.1 46.1 %collective-permute-start.22 = (f32[12,2,64,128]{3,2,1,0:T(8,128)}, f32[12,2,64,128]{3,2,1,0:T(8,128)S(1)}, u32[]{:S(2)}, u32[]{:S(2)}) collective-permute-start(f32[12,2,64,128]{3,2,1,0:T(8,128)} %get-tuple-element.85), channel_id=1, source_target_pairs={{0,1},{1,0},{2,3},{3,2},{4,5},{5,4},{6,7},{7,6},{8,9},{9,8},{10,11... | collective-permute-start | bytes 2359304 | tf_op jit(solution)/shard_map/ppermute | solution.py:27
  225.1 63.5 %collective-permute-start.23 = (f32[12,2,64,128]{3,2,1,0:T(8,128)}, f32[12,2,64,128]{3,2,1,0:T(8,128)S(1)}, u32[]{:S(2)}, u32[]{:S(2)}) collective-permute-start(f32[12,2,64,128]{3,2,1,0:T(8,128)} %get-tuple-element.86), channel_id=1, source_target_pairs={{0,4},{1,5},{2,6},{3,7},{4,0},{5,1},{6,2},{7,3},{8,12},{9,13},{10,... | collective-permute-start | bytes 2359304 | tf_op jit(solution)/shard_map/ppermute | solution.py:27
  225.4 24.9 %collective-permute-start.31 = (f32[12,136,128]{2,1,0:T(8,128)}, f32[12,136,128]{2,1,0:T(8,128)}, u32[]{:S(2)}, u32[]{:S(2)}) collective-permute-start(f32[12,136,128]{2,1,0:T(8,128)} %get-tuple-element.95), channel_id=1, source_target_pairs={{0,8},{1,9},{2,10},{3,11},{4,12},{5,13},{6,14},{7,15},{8,0},{9,1},... | collective-permute-start | bytes 2506760 | tf_op jit(solution)/shard_map/ppermute | solution.py:27
  227.4 22.9 %collective-permute-start.32 = (f32[12,136,128]{2,1,0:T(8,128)}, f32[12,136,128]{2,1,0:T(8,128)}, u32[]{:S(2)}, u32[]{:S(2)}) collective-permute-start(f32[12,136,128]{2,1,0:T(8,128)} %get-tuple-element.96), channel_id=1, source_target_pairs={{8,16},{9,17},{10,18},{11,19},{12,20},{13,21},{14,22},{15,23},{16,... | collective-permute-start | bytes 2506760 | tf_op jit(solution)/shard_map/ppermute | solution.py:27
  229.0 20.8 %collective-permute-start.35 = (f32[8,128]{1,0:T(8,128)S(1)}, f32[8,128]{1,0:T(8,128)S(1)}, u32[]{:S(2)}, u32[]{:S(2)}) collective-permute-start(f32[8,128]{1,0:T(8,128)S(1)} %add.378), channel_id=1, source_target_pairs={{0,16},{1,17},{2,18},{3,19},{4,20},{5,21},{6,22},{7,23},{8,24},{9,... | collective-permute-start | bytes 12296 | tf_op jit(solution)/shard_map/ppermute | solution.py:27
  249.8 38.7 %collective-permute-start.24 = (f32[12,2,64,128]{3,2,1,0:T(8,128)}, f32[12,2,64,128]{3,2,1,0:T(8,128)}, u32[]{:S(2)}, u32[]{:S(2)}) collective-permute-start(f32[12,2,64,128]{3,2,1,0:T(8,128)} %get-tuple-element.87), channel_id=1, source_target_pairs={{0,5},{1,4},{2,7},{3,6},{4,1},{5,0},{6,3},{7,2},{8,13},{9,12},{10,... | collective-permute-start | bytes 2359304 | tf_op jit(solution)/shard_map/ppermute | solution.py:27
  269.3 74.3 %collective-permute-start.36 = (f32[12,2,64,128]{3,2,1,0:T(8,128)}, f32[12,2,64,128]{3,2,1,0:T(8,128)}, u32[]{:S(2)}, u32[]{:S(2)}) collective-permute-start(f32[12,2,64,128]{3,2,1,0:T(8,128)} %get-tuple-element.99), channel_id=1, source_target_pairs={{0,1},{1,0},{2,3},{3,2},{4,5},{5,4},{6,7},{7,6},{8,9},{9,8},{10,11... | collective-permute-start | bytes 2359304 | tf_op jit(solution)/shard_map/ppermute | solution.py:27
  270.9 72.8 %collective-permute-start.37 = (f32[12,2,64,128]{3,2,1,0:T(8,128)}, f32[12,2,64,128]{3,2,1,0:T(8,128)}, u32[]{:S(2)}, u32[]{:S(2)}) collective-permute-start(f32[12,2,64,128]{3,2,1,0:T(8,128)} %get-tuple-element.100), channel_id=1, source_target_pairs={{0,4},{1,5},{2,6},{3,7},{4,0},{5,1},{6,2},{7,3},{8,12},{9,13},{10,... | collective-permute-start | bytes 2359304 | tf_op jit(solution)/shard_map/ppermute | solution.py:27
  271.2 72.5 %collective-permute-start.38 = (f32[12,2,64,128]{3,2,1,0:T(8,128)}, f32[12,2,64,128]{3,2,1,0:T(8,128)}, u32[]{:S(2)}, u32[]{:S(2)}) collective-permute-start(f32[12,2,64,128]{3,2,1,0:T(8,128)} %get-tuple-element.101), channel_id=1, source_target_pairs={{0,5},{1,4},{2,7},{3,6},{4,1},{5,0},{6,3},{7,2},{8,13},{9,12},{10,... | collective-permute-start | bytes 2359304 | tf_op jit(solution)/shard_map/ppermute | solution.py:27
  (64 other events, 574.0 us)
Sparse Core Ops, SparseCore 0:
  288.7 130.8 all-reduce.12

commit v2 on v0

v2 whole, which is shorter than its diff:
```python
import functools

import jax
import jax.numpy as jnp
from jax import lax
from jax.experimental import pallas as pl
from jax.experimental.pallas import tpu as pltpu
from jax.sharding import PartitionSpec as P


EPSILON = 1e-05
F32 = jnp.float32
BF16 = jnp.bfloat16
AXES = ("lat", "lon")
STEP = 2
VMEM_LIMIT = 32 << 20
CHUNKS = 2


def permute(value, target):
    rows, cols = lax.axis_size("lat"), lax.axis_size("lon")
    pairs = []
    for row in range(rows):
        for col in range(cols):
            to = target(row, col)
            if 0 <= to[0] < rows and 0 <= to[1] < cols:
                pairs.append((row * cols + col, to[0] * cols + to[1]))
    return lax.ppermute(value, AXES, pairs)


def to_core(row, col):
    return row, col ^ 1


def to_side(row, col):
    return row ^ 1, col


def to_east(row, col):
    return row, col ^ 2


def to_east_side(row, col):
    return row ^ 1, col ^ 2


def to_pair(row, col):
    return row ^ 2, col


def to_next(row, col):
    return (row + 2 if (row // 2) % 2 else row - 2), col


def group_steps():
    steps = []
    bit = 2
    while bit < lax.axis_size("lon"):
        steps.append(functools.partial(lambda bit, row, col: (row, col ^ bit), bit))
        bit *= 2
    bit = 2
    while bit < lax.axis_size("lat"):
        steps.append(functools.partial(lambda bit, row, col: (row ^ bit, col), bit))
        bit *= 2
    return steps


def exchange_rows(pair_row, next_row):
    return permute(pair_row, to_pair), permute(next_row, to_next)


def after(value, *others):
    return lax.optimization_barrier((value,) + others)[0]


def split(value):
    high = value.astype(BF16)
    return high, (value - high.astype(F32)).astype(BF16)


def sigmoid(value):
    return 1.0 / (1.0 + jnp.exp(-value))


VMEM = pl.BlockSpec(memory_space=pltpu.VMEM)
SMEM = pl.BlockSpec(memory_space=pltpu.SMEM)
HBM = pl.BlockSpec(memory_space=pltpu.HBM)


def in_hbm(array):
    return pltpu.with_memory_space_constraint(array, pltpu.HBM)


class Stream:
    def __init__(self, array, first=0, count=None, group=0):
        self.array = array
        self.first = first
        self.count = array.shape[0] if count is None else count
        self.group = group


class Result:
    def __init__(self, *shape):
        self.shape = shape


class Flow:
    def __init__(self, ins, outs, sems):
        self.ins, self.outs, self.sems = ins, outs, sems

    def copy_in(self, k, i):
        _, far, near, first = self.ins[k]
        source = far.at[pl.ds(first + i * STEP, STEP)]
        return pltpu.make_async_copy(source, near.at[pl.ds(i * STEP, STEP)], self.sems.at[k, i])

    def copy_out(self, k, i):
        far, near = self.outs[k]
        at = pl.ds(i * STEP, STEP)
        return pltpu.make_async_copy(near.at[at], far.at[at], self.sems.at[len(self.ins) + k, i])

    def start(self):
        for group in sorted({stream[0] for stream in self.ins}):
            members = [k for k, stream in enumerate(self.ins) if stream[0] == group]
            for i in range(max(self.ins[k][2].shape[0] for k in members) // STEP):
                for k in members:
                    self.copy_in(k, i).start()

    def steps(self, samples, body, group=0):
        def one(i, carry):
            for k, stream in enumerate(self.ins):
                if stream[0] == group:
                    self.copy_in(k, i).wait()
            body(pl.ds(pl.multiple_of(i * STEP, STEP), STEP), i)
            for k in range(len(self.outs)):
                self.copy_out(k, i).start()
            return carry

        lax.fori_loop(0, samples // STEP, one, 0)

    def finish(self):
        for k, (_, near) in enumerate(self.outs):
            for i in range(near.shape[0] // STEP):
                self.copy_out(k, i).wait()


def call(body, scalars, inputs, outputs, scratch, name):
    streams = [a for a in inputs if isinstance(a, Stream)]
    results = [o for o in outputs if isinstance(o, Result)]
    buffers = [pltpu.VMEM((a.count,) + a.array.shape[1:], F32) for a in streams]
    buffers += [pltpu.VMEM(o.shape, F32) for o in results]
    most = max([a.count // STEP for a in streams] + [o.shape[0] // STEP for o in results] + [1])

    def kernel(s_ref, *refs):
        refs = list(refs)
        in_refs, out_refs = refs[: len(inputs)], refs[len(inputs) : len(inputs) + len(outputs)]
        rest = refs[len(inputs) + len(outputs) :]
        near, rest = rest[: len(buffers)], rest[len(buffers) :]
        sems, rest = rest[0], rest[1:]
        ins, outs = [], []
        for at, a in enumerate(inputs):
            if isinstance(a, Stream):
                ins.append((a.group, in_refs[at], near[len(ins)], a.first))
                in_refs[at] = ins[-1][2]
        for at, o in enumerate(outputs):
            if isinstance(o, Result):
                outs.append((out_refs[at], near[len(ins) + len(outs)]))
                out_refs[at] = outs[-1][1]
        flow = Flow(ins, outs, sems)
        flow.start()
        body(flow, s_ref, *in_refs, *out_refs, *rest)
        flow.finish()

    return pl.pallas_call(
        kernel,
        in_specs=[SMEM] + [HBM if isinstance(a, Stream) else VMEM for a in inputs],
        out_specs=[HBM if isinstance(o, Result) else VMEM for o in outputs],
        out_shape=[pltpu.HBM(o.shape, F32) if isinstance(o, Result) else jax.ShapeDtypeStruct(o, F32) for o in outputs],
        scratch_shapes=buffers + [pltpu.SemaphoreType.DMA((max(len(buffers), 1), most))] + list(scratch),
        compiler_params=pltpu.CompilerParams(vmem_limit_bytes=VMEM_LIMIT),
        cost_estimate=pl.CostEstimate(flops=0, bytes_accessed=0, transcendentals=0),
        name=name,
    )(scalars, *[in_hbm(a.array) if isinstance(a, Stream) else a for a in inputs])


def pack_kernel(other_core, s_ref, field, out, sem):
    core = 1 - s_ref[1] if other_core else s_ref[1]
    copy = pltpu.make_async_copy(field.at[:, core], out, sem)
    copy.start()
    copy.wait()


def pack(scalars, field, other_core, name):
    return pl.pallas_call(
        functools.partial(pack_kernel, other_core),
        in_specs=[SMEM, HBM],
        out_specs=VMEM,
        out_shape=jax.ShapeDtypeStruct((2,) + field.shape[2:], F32),
        scratch_shapes=[pltpu.SemaphoreType.DMA],
        compiler_params=pltpu.CompilerParams(vmem_limit_bytes=VMEM_LIMIT),
        name=name,
    )(scalars, in_hbm(field))


def wide_rows(nc, own, other, out):
    half = own.shape[1]
    out[:, pl.ds(pl.multiple_of(nc * half, half), half), :] = own
    out[:, pl.ds(pl.multiple_of((1 - nc) * half, half), half), :] = other


def ends(nc, own, other):
    cols = own.shape[1]
    west, east = jnp.where(nc == 0, own[:, 0:8], other[:, 0:8]), jnp.where(nc == 0, other[:, -8:], own[:, -8:])
    del cols
    return jnp.concatenate([west[:, 0:4], east[:, 4:8]], axis=1)


def rows_kernel(flow, s_ref, own, other, home, edge, inner, *tiles):
    lx, nc = s_ref[0], s_ref[1]
    for row in range(2):
        wide_rows(nc, own[lx, :, row], other[lx, :, row], home.at[:, row])
    wide_rows(nc, own[1 - lx, :, lx], other[1 - lx, :, lx], edge)
    wide_rows(nc, own[1 - lx, :, 1 - lx], other[1 - lx, :, 1 - lx], inner)
    for part, tile in zip((lx, 1 - lx), tiles):
        for row in range(2):
            tile[:, row] = ends(nc, own[part, :, row], other[part, :, row])


def rows(scalars, own, other, name):
    _, batch, _, cols, chans = own.shape
    row = (batch, 2 * cols, chans)
    tile = (batch, 2, 8, chans)
    return call(rows_kernel, scalars, [own, other], [(batch, 2) + row[1:], row, row, tile, tile], [], name)


def join_kernel(edge, flow, s_ref, home, foreign, tiles, foreign_tiles, rows_ref, pair_ref, next_ref):
    lx, odd = s_ref[0], s_ref[2]
    wide = home.shape[2]
    row = lx if edge else 1 - lx
    rows_ref[:, lx, 0:wide, :] = home[:, row]
    rows_ref[:, lx, wide : wide + 8, :] = tiles[:, row]
    rows_ref[:, 1 - lx, 0:wide, :] = foreign[...]
    rows_ref[:, 1 - lx, wide : wide + 8, :] = foreign_tiles[:, 1 - row]
    pair_ref[...] = rows_ref[:, 1 - odd]
    next_ref[...] = rows_ref[:, odd]


def join(scalars, home, foreign, tiles, foreign_tiles, edge, name):
    batch, _, wide, chans = home.shape
    row = (batch, wide + 8, chans)
    return call(
        functools.partial(join_kernel, edge),
        scalars,
        [home, foreign, tiles, foreign_tiles],
        [(batch, 2) + row[1:], row, row],
        [],
        name,
    )


def chunk_rows_kernel(flow, s_ref, own, other, home, tiles, other_tiles, *others):
    lx, nc = s_ref[0], s_ref[1]
    part = others[0].shape[0]
    for row in range(2):
        wide_rows(nc, own[lx, :, row], other[lx, :, row], home.at[:, row])
        for chunk, out in enumerate(others):
            at = slice(chunk * part, (chunk + 1) * part)
            wide_rows(nc, own[1 - lx, at, row], other[1 - lx, at, row], out.at[:, row])
        for side, tile in zip((lx, 1 - lx), (tiles, other_tiles)):
            tile[:, row] = ends(nc, own[side, :, row], other[side, :, row])


def chunk_rows(scalars, own, other, name):
    _, batch, _, cols, chans = own.shape
    tile = (batch, 2, 8, chans)
    row = (2, 2 * cols, chans)
    return call(
        chunk_rows_kernel,
        scalars,
        [own, other],
        [(batch,) + row, tile, tile] + [(batch // CHUNKS,) + row] * CHUNKS,
        [],
        name,
    )


def cell_kernel(first, flow, s_ref, home, foreign, tiles, foreign_tiles, rows_ref, pair_ref, next_ref):
    lx, odd = s_ref[0], s_ref[2]
    part, _, wide, _ = foreign.shape
    at = slice(first, first + part)
    for row in range(2):
        for side, rows, ends_of in ((2 * lx, home[at, row], tiles), (2 - 2 * lx, foreign[:, row], foreign_tiles)):
            rows_ref[:, side + row, 0:wide, :] = rows
            rows_ref[:, side + row, wide : wide + 8, :] = ends_of[at, row]
    pair_ref[...] = rows_ref[:, 3 - 3 * odd]
    next_ref[...] = rows_ref[:, 3 * odd]
    flow.steps(part, lambda here, i: None)


def cell_rows(scalars, home, foreign, tiles, chunk, name):
    part, _, wide, chans = foreign.shape
    row = (part, wide + 8, chans)
    return call(
        functools.partial(cell_kernel, chunk * part),
        scalars,
        [home, foreign, *tiles],
        [Result(part, 4, *row[1:]), row, row],
        [],
        name,
    )


def row_of_parts(parts, row, at):
    edge, inner = parts
    return (edge if row in (0, 3) else inner)[at, 0 if row < 2 else 1]


def ring_row(values, pad, row, high, low):
    step, wide, chans = values.shape
    pad[row, :, 8 : 8 + wide, :] = values
    pad[row, :, 0:8, :] = values[:, wide - 8 : wide]
    pad[row, :, 8 + wide : 16 + wide, :] = values[:, 0:8]
    for tap in range(3):
        shifted = values if tap == 1 else pad[row, :, 7 + tap : 7 + tap + wide, :]
        at = (row * 3 + tap) * chans
        high[:, at : at + chans], low[:, at : at + chans] = split(shifted.reshape(step * wide, chans))


def put_weight(weight, turned, high, low):
    chans = weight.shape[1]
    nothing = jnp.zeros((chans, chans), BF16)
    for row in range(3):
        for tap in range(3):
            block = weight[(2 - row) * 3 + 2 - tap].T if turned else weight[row * 3 + tap]
            parts = split(block)
            for out in range(2):
                at = ((row + out) * 3 + tap) * chans
                for ref, part in zip((high, low), parts):
                    ref[at : at + chans, out * chans : (out + 1) * chans] = part
    for tap in range(3):
        for ref in (high, low):
            ref[(9 + tap) * chans : (10 + tap) * chans, 0:chans] = nothing
            ref[tap * chans : (tap + 1) * chans, chans : 2 * chans] = nothing


def pair_of_rows(pair, high, low, weight_high, weight_low):
    chans = weight_high.shape[1] // 2
    at = slice(pair * 6 * chans, (pair * 6 + 12) * chans)
    total = jnp.dot(high[:, at], weight_high[...], preferred_element_type=F32)
    total += jnp.dot(low[:, at], weight_high[...], preferred_element_type=F32)
    total += jnp.dot(high[:, at], weight_low[...], preferred_element_type=F32)
    return total[:, :chans], total[:, chans:]


def north_south(s_ref, pair, following, at):
    odd = s_ref[2] == 1
    first, second = pair[at], following[at]
    return jnp.where(odd, first, second), jnp.where(odd, second, first)


def put_edges(s_ref, top, bottom, pair_out, next_out, at):
    odd = s_ref[2] == 1
    pair_out[at] = jnp.where(odd, top, bottom)
    next_out[at] = jnp.where(odd, bottom, top)


def lanes(values):
    return jnp.sum(values.reshape(-1, 8, values.shape[-1]), axis=0)


def fold(total):
    return jnp.sum(total, axis=0, keepdims=True)


def add_moments(active, first, shift, sums, others):
    @pl.when(first)
    def _():
        mean = jnp.mean(active[0].reshape(-1, active[0].shape[-1]), axis=0, keepdims=True)
        shift[...] = jnp.broadcast_to(mean, shift.shape)
        sums[...] = jnp.zeros_like(sums)

    base = shift[0:1, :]
    for at, values in enumerate(active):
        distance = values - base
        sums[0] += lanes(distance)
        sums[1] += lanes(distance * distance)
        if others is not None:
            sums[2] += lanes(others[at])
            sums[3] += lanes(others[at] * distance)


def put_moments(out_ref, shift, sums, count, others):
    total, squares = fold(sums[0]), fold(sums[1])
    offset = total / count
    out_ref[...] = jnp.zeros_like(out_ref)
    out_ref[0:1, :] = shift[0:1, :] + offset
    out_ref[1:2, :] = squares - total * offset
    if others:
        weight = fold(sums[2])
        out_ref[2:3, :] = weight
        out_ref[3:4, :] = fold(sums[3]) - weight * offset


def conv_scratch(wide, chans):
    return [
        pltpu.VMEM((6, STEP, wide + 16, chans), F32),
        pltpu.VMEM((STEP * wide, 18 * chans), BF16),
        pltpu.VMEM((STEP * wide, 18 * chans), BF16),
        pltpu.VMEM((12 * chans, 2 * chans), BF16),
        pltpu.VMEM((12 * chans, 2 * chans), BF16),
    ]


def first_kernel(
    flow, s_ref, edge, inner, pair, following, weight, bias, z_ref, stat_ref,
    pad, high, low, weight_high, weight_low, shift, sums,
):
    batch, _, wide, _ = z_ref.shape
    own = wide - 8
    put_weight(weight, False, weight_high, weight_low)

    def step(at, i):
        north, south = north_south(s_ref, pair, following, at)
        for row in range(6):
            values = north if row == 0 else south if row == 5 else row_of_parts((edge, inner), row - 1, at)
            ring_row(values, pad, row, high, low)
        active = []
        for two in range(2):
            for total in pair_of_rows(two, high, low, weight_high, weight_low):
                z = (total + bias[0:1, :]).reshape(-1, wide, total.shape[-1])
                z_ref[at, len(active)] = z
                active.append(z[:, :own] * sigmoid(z[:, :own]))
        add_moments(active, i == 0, shift, sums, None)

    flow.steps(batch, step)
    put_moments(stat_ref, shift, sums, float(batch * 4 * own), False)


def first_conv(scalars, parts, halos, weight, bias):
    batch, _, wide, chans = parts[0].shape
    return call(
        first_kernel,
        scalars,
        parts + halos + (weight, bias),
        [Result(batch, 4, wide, chans), (8, chans)],
        conv_scratch(wide, chans) + [pltpu.VMEM((8, chans), F32), pltpu.VMEM((4, 8, chans), F32)],
        "conv_one",
    )


def first_halo_kernel(
    flow, s_ref, edge, pair, following, pair_inner, following_inner, weight, bias, north_ref, south_ref,
    pad, high, low, weight_high, weight_low,
):
    batch, wide, chans = north_ref.shape
    for tap in range(9):
        taps = slice(tap * chans, (tap + 1) * chans)
        weight_high[taps, :], weight_low[taps, :] = split(weight[tap])

    def step(at, i):
        north, south = north_south(s_ref, pair, following, at)
        far_north, far_south = north_south(s_ref, pair_inner, following_inner, at)
        rows = (far_north, north, edge[at, 0], edge[at, 1], south, far_south)
        for row, values in enumerate(rows):
            ring_row(values, pad, row, high, low)
        for side, ref in enumerate((north_ref, south_ref)):
            taps = slice(side * 9 * chans, (side + 1) * 9 * chans)
            total = jnp.dot(high[:, taps], weight_high[...], preferred_element_type=F32)
            total += jnp.dot(low[:, taps], weight_high[...], preferred_element_type=F32)
            total += jnp.dot(high[:, taps], weight_low[...], preferred_element_type=F32)
            ref[at] = (total + bias[0:1, :]).reshape(-1, wide, chans)

    flow.steps(batch, step)


def first_halo_conv(scalars, edge, halos, far_halos, weight, bias):
    batch, _, wide, chans = edge.shape
    return call(
        first_halo_kernel,
        scalars,
        [Stream(edge), *[Stream(a) for a in halos + far_halos], weight, bias],
        [(batch, wide, chans)] * 2,
        conv_scratch(wide, chans)[:3] + [pltpu.VMEM((9 * chans, chans), BF16)] * 2,
        "conv_one_halo",
    )


def hidden_row(s_ref, z1, north, south, coef, at, there, row):
    center, scale, offset = coef[0:1, :], coef[1:2, :], coef[2:3, :]
    values = north[there] if row == 0 else south[there] if row == 5 else z1[at, row - 1]
    hidden = (values * sigmoid(values) - center) * scale + offset
    if row in (0, 5):
        hidden = jnp.where(s_ref[3 if row == 0 else 4] == 1, 0.0, hidden)
    return hidden


def second_kernel(
    first, flow, s_ref, z1, g_rows, north, south, coef, weight, bias,
    z_ref, pair_out, next_out, stat_ref, pad, high, low, weight_high, weight_low, shift, sums,
):
    part, _, wide, _ = z_ref.shape
    own = wide - 8
    put_weight(weight, False, weight_high, weight_low)

    def step(at, i):
        there = pl.ds(i * STEP + first, STEP)
        for row in range(6):
            ring_row(hidden_row(s_ref, z1, north, south, coef, at, there, row), pad, row, high, low)
        active = []
        rows = []
        for two in range(2):
            for total in pair_of_rows(two, high, low, weight_high, weight_low):
                z = (total + bias[0:1, :]).reshape(-1, wide, total.shape[-1])
                z_ref[at, len(rows)] = z
                rows.append(z)
                active.append(z[:, :own] * sigmoid(z[:, :own]))
        put_edges(s_ref, rows[0], rows[3], pair_out, next_out, at)
        add_moments(active, i == 0, shift, sums, [g_rows[at, row, :own] for row in range(4)])

    flow.steps(part, step)
    put_moments(stat_ref, shift, sums, float(part * 4 * own), True)


def second_conv(scalars, z1, halos, g_rows, coef, weight, bias, chunk):
    part, _, wide, chans = g_rows.shape
    return call(
        functools.partial(second_kernel, chunk * part),
        scalars,
        [Stream(z1, chunk * part, part), Stream(g_rows), *halos, coef, weight, bias],
        [Result(part, 4, wide, chans), (part, wide, chans), (part, wide, chans), (8, chans)],
        conv_scratch(wide, chans) + [pltpu.VMEM((8, chans), F32), pltpu.VMEM((4, 8, chans), F32)],
        "conv_two",
    )


def put_pieces(s_ref, rows, home, other, at):
    lx = s_ref[0]
    for row in range(2):
        home[at, row] = rows[2 * lx + row]
        other[at, row] = rows[2 - 2 * lx + row]


def halves_kernel(flow, s_ref, home, foreign, out):
    cols = out.shape[3]
    there = pl.ds(pl.multiple_of((1 - s_ref[1]) * cols, cols), cols)
    for at, rows in enumerate((home, foreign)):
        for row in range(2):
            out[at, :, row] = rows[:, row, there, :]


def send_side(home, other):
    return home, permute(other, to_side)


def send_core(scalars, home, foreign, name):
    part, _, wide, chans = home.shape
    payload = call(halves_kernel, scalars, [home, foreign], [(2, part, 2, wide // 2, chans)], [], name)[0]
    return home, foreign, permute(payload, to_core)


def place_kernel(chunk, s_ref, home, foreign, core, *refs):
    out, sems = refs[-2:]
    lx, nc = s_ref[0], s_ref[1]
    part, cols = core.shape[1], core.shape[3]
    at = pl.ds(chunk * part, part)
    here = pl.ds(pl.multiple_of(nc * cols, cols), cols)
    copies = [
        pltpu.make_async_copy(home.at[:, :, here, :], out.at[lx, nc, at], sems.at[0]),
        pltpu.make_async_copy(foreign.at[:, :, here, :], out.at[1 - lx, nc, at], sems.at[1]),
        pltpu.make_async_copy(core.at[0], out.at[lx, 1 - nc, at], sems.at[2]),
        pltpu.make_async_copy(core.at[1], out.at[1 - lx, 1 - nc, at], sems.at[3]),
    ]
    for copy in copies:
        copy.start()
    for copy in copies:
        copy.wait()


def place(scalars, pieces, chunk, filled, name):
    _, part, rows_here, cols, chans = pieces[2].shape
    shape = (2, 2, part * CHUNKS, rows_here, cols, chans)
    earlier = [] if filled is None else [filled]
    return pl.pallas_call(
        functools.partial(place_kernel, chunk),
        in_specs=[SMEM] + [VMEM] * 3 + [HBM] * len(earlier),
        out_specs=HBM,
        out_shape=jax.ShapeDtypeStruct(shape, F32),
        scratch_shapes=[pltpu.SemaphoreType.DMA((4,))],
        input_output_aliases={4: 0} if earlier else {},
        compiler_params=pltpu.CompilerParams(vmem_limit_bytes=VMEM_LIMIT),
        name=name,
    )(scalars, *pieces, *earlier)


def silu_and_slope(z):
    sigma = sigmoid(z)
    return z * sigma, sigma * (1.0 + z * (1.0 - sigma))


def third_kernel(
    flow, s_ref, z2, g_rows, z1, x_edge, x_inner, pair, following, g_pair, g_following, coef, weight,
    dh_ref, dz_ref, pair_out, next_out, stat_ref, home, other,
    pad, high, low, weight_high, weight_low, sums, results,
):
    part, _, wide, _ = dh_ref.shape
    own = wide - 8
    center, inverse, scale = coef[0:1, :], coef[1:2, :], coef[2:3, :]
    mean_shift, mean_gain = coef[3:4, :], coef[4:5, :]
    center_one, inverse_one, shift_two = coef[5:6, :], coef[6:7, :], coef[7:8, :]
    put_weight(weight, True, weight_high, weight_low)
    sums[...] = jnp.zeros_like(sums)

    def step(at, i):
        north, south = north_south(s_ref, pair, following, at)
        g_north, g_south = north_south(s_ref, g_pair, g_following, at)
        for row in range(6):
            if row in (0, 5):
                z, g = (north, g_north) if row == 0 else (south, g_south)
            else:
                z, g = z2[at, row - 1], g_rows[at, row - 1]
            active, slope = silu_and_slope(z)
            distance = active - center
            dz = scale * (g - mean_shift - distance * inverse * mean_gain) * slope
            if row in (0, 5):
                dz = jnp.where(s_ref[3 if row == 0 else 4] == 1, 0.0, dz)
            else:
                dz_ref[at, row - 1] = dz[:, :own]
                sums[2] += lanes(dz[:, :own])
                x = row_of_parts((x_edge, x_inner), row - 1, at)
                results[row - 1] = x[:, :own] + (distance[:, :own] * scale + shift_two)
            ring_row(dz, pad, row, high, low)
        rows = []
        for two in range(2):
            for total in pair_of_rows(two, high, low, weight_high, weight_low):
                dh = total.reshape(-1, wide, total.shape[-1])
                row = len(rows)
                dh_ref[at, row] = dh
                rows.append(dh)
                z = z1[at, row, :own]
                sums[0] += lanes(dh[:, :own])
                sums[1] += lanes(dh[:, :own] * ((z * sigmoid(z) - center_one) * inverse_one))
        put_edges(s_ref, rows[0], rows[3], pair_out, next_out, at)
        put_pieces(s_ref, results, home, other, at)

    flow.steps(part, step)
    stat_ref[...] = jnp.zeros_like(stat_ref)
    for row in range(3):
        stat_ref[row : row + 1, :] = fold(sums[row])


def third_conv(scalars, z2, halos, g_rows, g_halos, z1, x_parts, coef, weight, chunk):
    part, _, wide, chans = z2.shape
    own = wide - 8
    first = chunk * part
    return call(
        third_kernel,
        scalars,
        [Stream(z2), Stream(g_rows)]
        + [Stream(a, first, part) for a in (z1,) + x_parts]
        + [*halos, *g_halos, coef, weight],
        [Result(part, 4, wide, chans), Result(part, 4, own, chans)]
        + [(part, wide, chans), (part, wide, chans), (8, chans), (part, 2, own, chans), (part, 2, own, chans)],
        conv_scratch(wide, chans) + [pltpu.VMEM((3, 8, chans), F32), pltpu.VMEM((4, STEP, own, chans), F32)],
        "conv_three",
    )


def slope_one(z, q, coef):
    center, inverse, scale = coef[0:1, :], coef[1:2, :], coef[2:3, :]
    mean_shift, mean_gain = coef[3:4, :], coef[4:5, :]
    active, slope = silu_and_slope(z)
    return scale * (q - mean_shift - (active - center) * inverse * mean_gain) * slope


def fourth_kernel(
    flow, s_ref, dh, z1, z_north, z_south, g_rows, pair, following, coef, weight,
    home, other, pad, high, low, weight_high, weight_low, results,
):
    part, _, wide, _ = dh.shape
    own = wide - 8
    put_weight(weight, True, weight_high, weight_low)

    def step(at, i):
        north, south = north_south(s_ref, pair, following, at)
        for row in range(6):
            if row in (0, 5):
                z, q = (z_north[at], north) if row == 0 else (z_south[at], south)
            else:
                z, q = z1[at, row - 1], dh[at, row - 1]
            dz = slope_one(z, q, coef)
            if row in (0, 5):
                dz = jnp.where(s_ref[3 if row == 0 else 4] == 1, 0.0, dz)
            ring_row(dz, pad, row, high, low)
        row = 0
        for two in range(2):
            for total in pair_of_rows(two, high, low, weight_high, weight_low):
                results[row] = g_rows[at, row, :own] + total.reshape(-1, wide, total.shape[-1])[:, :own]
                row += 1
        put_pieces(s_ref, results, home, other, at)

    flow.steps(part, step)


def fourth_conv(scalars, dh, halos, z1, z_halos, g_rows, coef, weight, chunk):
    part, _, wide, chans = dh.shape
    own = wide - 8
    return call(
        fourth_kernel,
        scalars,
        [Stream(dh)]
        + [Stream(a, chunk * part, part) for a in (z1,) + z_halos]
        + [Stream(g_rows), *halos, coef, weight],
        [(part, 2, own, chans)] * 2,
        conv_scratch(wide, chans) + [pltpu.VMEM((4, STEP, own, chans), F32)],
        "conv_four",
    )


def weight_step(rows, slopes, pad, high, low, total):
    own, chans = slopes[0].shape[1], slopes[0].shape[2]
    wide = own + 8
    for row, values in enumerate(rows):
        pad[row, :, 8 : 8 + wide, :] = values
        pad[row, :, 0:8, :] = values[:, own:wide]
        for tap in range(3):
            shifted = values[:, :own] if tap == 1 else pad[row, :, 7 + tap : 7 + tap + own, :]
            at = (row * 3 + tap) * chans
            high[:, at : at + chans], low[:, at : at + chans] = split(shifted.reshape(-1, chans))

    def product(left, right):
        return lax.dot_general(left, right, (((0,), (0,)), ((), ())), preferred_element_type=F32)

    sums = None
    for two in range(2):
        at = slice(two * 6 * chans, (two * 6 + 12) * chans)
        slope = jnp.concatenate([s.reshape(-1, chans) for s in slopes[2 * two : 2 * two + 2]], axis=1)
        slope_high, slope_low = split(slope)
        part = product(high[:, at], slope_high)
        part += product(low[:, at], slope_high)
        part += product(high[:, at], slope_low)
        sums = part if sums is None else sums + part
    total[...] += sums


SMALL = 32


def weight_end(out_ref, total, small, bias):
    chans = out_ref.shape[1]
    line = 3 * chans
    for row in range(3):
        out_ref[row * line : (row + 1) * line, :] = (
            total[row * line : (row + 1) * line, :chans] + total[(row + 1) * line : (row + 2) * line, chans:]
        )
    out_ref[3 * line :, :] = jnp.zeros((SMALL, chans), F32)
    out_ref[3 * line : 3 * line + 8, :] = small[...]
    if bias is not None:
        out_ref[3 * line : 3 * line + 1, :] = fold(bias[...])


def weight_scratch(own, chans):
    return [
        pltpu.VMEM((6, STEP, own + 16, chans), F32),
        pltpu.VMEM((STEP * own, 18 * chans), BF16),
        pltpu.VMEM((STEP * own, 18 * chans), BF16),
        pltpu.VMEM((12 * chans, 2 * chans), F32),
    ]


def weight_two_kernel(flow, s_ref, *refs):
    chunks = [refs[4 * chunk : 4 * chunk + 4] for chunk in range(CHUNKS)]
    coef, small, out_ref, *scratch = refs[4 * CHUNKS :]
    scratch[-1][...] = jnp.zeros_like(scratch[-1])
    for chunk, (z1, north, south, dz) in enumerate(chunks):

        def step(at, i):
            rows = [hidden_row(s_ref, z1, north, south, coef, at, at, row) for row in range(6)]
            weight_step(rows, [dz[at, row] for row in range(4)], *scratch)

        flow.steps(dz.shape[0], step, chunk)
    weight_end(out_ref, scratch[-1], small, None)


def weight_two_grad(scalars, z1, halos, coef, dz, small):
    part, _, own, chans = dz[0].shape
    streams = []
    for chunk in range(CHUNKS):
        streams += [Stream(a, chunk * part, part, chunk) for a in (z1,) + halos]
        streams += [Stream(dz[chunk], group=chunk)]
    return call(
        weight_two_kernel,
        scalars,
        streams + [coef, small],
        [(9 * chans + SMALL, chans)],
        weight_scratch(own, chans),
        "weight_two",
    )[0]


def weight_one_kernel(flow, s_ref, *refs):
    chunks = [refs[6 * chunk : 6 * chunk + 6] for chunk in range(CHUNKS)]
    coef, small, out_ref, bias, *scratch = refs[6 * CHUNKS :]
    bias[...] = jnp.zeros_like(bias)
    scratch[-1][...] = jnp.zeros_like(scratch[-1])
    for chunk, (edge, inner, pair, following, z1, dh) in enumerate(chunks):
        part, _, wide, _ = dh.shape
        own = wide - 8

        def step(at, i):
            north, south = north_south(s_ref, pair, following, at)
            rows = [north] + [row_of_parts((edge, inner), row, at) for row in range(4)] + [south]
            slopes = [slope_one(z1[at, row, :own], dh[at, row, :own], coef) for row in range(4)]
            for slope in slopes:
                bias[...] += lanes(slope)
            weight_step(rows, slopes, *scratch)

        flow.steps(part, step, chunk)
    weight_end(out_ref, scratch[-1], small, bias)


def weight_one_grad(scalars, parts, halos, dh, z1, coef, small):
    part, _, wide, chans = dh[0].shape
    streams = []
    for chunk in range(CHUNKS):
        streams += [Stream(a, chunk * part, part, chunk) for a in parts + halos + (z1,)]
        streams += [Stream(dh[chunk], group=chunk)]
    return call(
        weight_one_kernel,
        scalars,
        streams + [coef, small],
        [(9 * chans + SMALL, chans)],
        [pltpu.VMEM((8, chans), F32)] + weight_scratch(wide - 8, chans),
        "weight_one",
    )[0]


def rows_of(*vectors):
    filled = [jnp.reshape(v, (1, -1)) for v in vectors]
    if len(filled) < 8:
        filled.append(jnp.zeros((8 - len(filled), filled[0].shape[1]), F32))
    return jnp.concatenate(filled, axis=0)


def merge_moments(one, other, count):
    mean = 0.5 * (one[0] + other[0])
    gap = one[0] - other[0]
    squares = one[1] + other[1] + gap * gap * (0.5 * count)
    weight = one[2] + other[2]
    product = (one[3] + (one[0] - mean) * one[2]) + (other[3] + (other[0] - mean) * other[2])
    return rows_of(mean, squares, weight, product)


def all_moments(stats, here, *others):
    count = here
    partial = []
    for target in group_steps():
        stats = merge_moments(stats, permute(stats, target), count)
        if not partial and others:
            stats = after(stats, *others)
        partial.append(stats)
        count = 2.0 * count
    return partial


def all_sums(stats, *others):
    partial = []
    for target in group_steps():
        stats = stats + permute(stats, target)
        if not partial and others:
            stats = after(stats, *others)
        partial.append(stats)
    return partial


def quarters_kernel(flow, s_ref, value, own, *others):
    size = own.shape[0]
    here = 2 * s_ref[5] + s_ref[2]
    for bits, ref in zip((0, 2, 1, 3), (own,) + others):
        ref[...] = value[pl.ds(pl.multiple_of((here ^ bits) * size, 8), size), :]


def whole_kernel(flow, s_ref, own, *refs):
    others, out = refs[:-1], refs[-1]
    size = own.shape[0]
    here = 2 * s_ref[5] + s_ref[2]
    for bits, ref in zip((0, 2, 1, 3), (own,) + others):
        out[pl.ds(pl.multiple_of((here ^ bits) * size, 8), size), :] = ref[...]


def to_east_pair(row, col):
    return row ^ 2, col ^ 2


def sum_everywhere(scalars, one, two, lon, beside):
    west = lon % 2 == 0
    value = jnp.where(west, one, two) + permute(after(jnp.where(west, two, one), *beside[0]), to_core)
    size, chans = value.shape[0] // 4, value.shape[1]
    targets = (to_east, to_pair, to_east_pair)
    own, *others = call(quarters_kernel, scalars, [value], [(size, chans)] * 4, [], "quarters")
    others = [permute(v, target) for v, target in zip(others, targets)]
    own = after(own, *beside[1])
    own = (own + others[0]) + (others[1] + others[2])
    own = own + permute(own, to_side)
    last = beside[2](own)
    for target in group_steps()[2:]:
        own = own + permute(own, target)
    others = [permute(own, target) for target in targets]
    value = call(whole_kernel, scalars, [after(own, last), *others], [(4 * size, chans)], [], "whole")[0]
    other = permute(value, to_core)
    return jnp.where(west, value, other), jnp.where(west, other, value)


def shards(
    fields, weight_one, bias_one, gain_one, shift_one, weight_two, bias_two, gain_two, shift_two, cotangent
):
    parts_here, batch, rows_here, cols_here, chans = fields.shape
    lat, lon = lax.axis_index("lat"), lax.axis_index("lon")
    lats, lons = lax.axis_size("lat"), lax.axis_size("lon")
    assert (parts_here, rows_here, lons) == (4, 2, 4)
    here = float(batch * 4 * 2 * cols_here)
    members = float(lats * lons // 4)
    count = here * members
    pair = lat // 2
    scalars = jnp.stack([lat % 2, lon % 2, pair % 2, pair == 0, pair == lats // 2 - 1, lon // 2]).astype(jnp.int32)
    cells = fields.reshape((2, 2) + fields.shape[1:])
    slopes = cotangent.reshape((2, 2) + cotangent.shape[1:])
    taps_one = weight_one.reshape((9, chans, chans))
    taps_two = weight_two.reshape((9, chans, chans))

    other = pack(scalars, cells, True, "x_pack_other")
    core = permute(other, to_core)
    own = pack(scalars, after(cells, other), False, "x_pack_own")
    home, edge, inner, tiles, other_tiles = rows(scalars, own, core, "x_rows")
    edge = permute(edge, to_side)
    tiles = permute(tiles, to_east)
    foreign_tiles = permute(other_tiles, to_east_side)
    inner = permute(after(inner, tiles), to_side)
    x_edge, pair_row, next_row = join(scalars, home, edge, tiles, foreign_tiles, True, "x_edge")
    x_halos = exchange_rows(pair_row, next_row)
    slopes = after(slopes, x_edge)
    other = pack(scalars, slopes, True, "g_pack_other")
    core = permute(other, to_core)
    own = pack(scalars, after(slopes, other), False, "g_pack_own")
    g_home, g_tiles, g_other, *g_foreign = chunk_rows(scalars, own, core, "g_rows")
    g_foreign = [permute(part, to_side) for part in g_foreign]
    g_tiles = (permute(g_tiles, to_east), permute(g_other, to_east_side))
    x_inner, pair_row, next_row = join(scalars, after(home, g_home), inner, tiles, foreign_tiles, False, "x_inner")
    x_far = exchange_rows(pair_row, next_row)
    x_parts = (x_edge, x_inner)

    z1, stats = first_conv(scalars, x_parts, x_halos, taps_one, after(rows_of(bias_one), g_home))
    partial = all_moments(after(stats, *x_far, g_foreign[0]), here)
    z1_halos = tuple(
        first_halo_conv(scalars, after(x_edge, partial[-2]), x_halos, x_far, taps_one, rows_of(bias_one))
    )
    g_rows, g_edges = [], []
    for chunk in range(CHUNKS):
        foreign = after(g_foreign[chunk], z1_halos[0])
        four, pair_row, next_row = cell_rows(scalars, g_home, foreign, g_tiles, chunk, "g_cell")
        g_rows.append(four)
        g_edges.append((pair_row, next_row))
    stats = partial[-1]
    center_one, spread_one = stats[0], stats[1] / count
    inv_one = lax.rsqrt(spread_one + EPSILON)

    coef_one = rows_of(center_one, gain_one * inv_one, shift_one)
    g_halos = [exchange_rows(after(top, coef_one), bottom) for top, bottom in g_edges]
    z2, z2_edges, parts, earlier = [], [], [], []
    for chunk in range(CHUNKS):
        z, pair_row, next_row, stats = second_conv(
            scalars, z1, z1_halos, g_rows[chunk], after(coef_one, *earlier), taps_two, rows_of(bias_two), chunk
        )
        earlier = [z, *g_halos[0], *g_halos[1]]
        z2.append(z)
        z2_edges.append((pair_row, next_row))
        parts.append(stats)
    z2_halos = [exchange_rows(*z2_edges[0])]
    partial = all_moments(merge_moments(parts[0], parts[1], here / CHUNKS), here, *z2_halos[0])
    z2_halos.append(exchange_rows(after(z2_edges[1][0], partial[-2]), z2_edges[1][1]))
    stats = partial[-1]
    center_two, spread_two, dshift_two = stats[0], stats[1] / count, stats[2]
    inv_two = lax.rsqrt(spread_two + EPSILON)
    dgain_two = stats[3] * inv_two

    coef = rows_of(
        center_two, inv_two, gain_two * inv_two, dshift_two / count, dgain_two / count, center_one, inv_one,
        shift_two,
    )
    dh1, dz2, dh1_edges, parts, output = [], [], [], [], []
    for chunk in range(CHUNKS):
        dh, dz, pair_row, next_row, stats, *pieces = third_conv(
            scalars, z2[chunk], z2_halos[chunk], g_rows[chunk], g_halos[chunk], z1, x_parts, after(coef, *dh1),
            taps_two, chunk,
        )
        dh1.append(dh)
        dz2.append(dz)
        dh1_edges.append((pair_row, next_row))
        parts.append(stats)
        output.append(send_side(*pieces))
    stats = parts[0] + parts[1]
    dbias_two = stats[2]
    dh1_halos = [exchange_rows(*dh1_edges[0])]
    partial = all_sums(stats, *dh1_halos[0])
    dh1_halos.append(exchange_rows(after(dh1_edges[1][0], partial[-2]), dh1_edges[1][1]))
    small = rows_of(dbias_two, dgain_two / members, dshift_two / members)
    grad_w2 = weight_two_grad(scalars, z1, z1_halos, after(coef_one, partial[-2]), dz2, small)
    dshift_one, dgain_one = partial[-1][0], partial[-1][1]

    coef = rows_of(center_one, inv_one, gain_one * inv_one, dshift_one / count, dgain_one / count)
    small = rows_of(jnp.zeros_like(dgain_one), dgain_one / members, dshift_one / members)

    def input_slope(chunk, coef):
        return fourth_conv(
            scalars, dh1[chunk], dh1_halos[chunk], z1, z1_halos, g_rows[chunk], coef, taps_one, chunk
        )

    pieces = input_slope(0, after(coef, grad_w2, output[0][1], output[1][1]))
    grad_w1 = weight_one_grad(scalars, x_parts, x_halos, dh1, z1, after(coef, pieces[0]), small)
    input_grad = [send_side(*pieces)]
    pieces = input_slope(1, after(coef, grad_w1))
    out_whole = None
    for chunk in range(CHUNKS):
        out_whole = place(scalars, send_core(scalars, *output[chunk], "output_halves"), chunk, out_whole, "output_place")
    def send_last(summed):
        input_grad.append(send_side(pieces[0], after(pieces[1], summed)))
        return input_grad[1][1]

    beside = ([input_grad[0][1]], [pieces[0], out_whole], send_last)
    one, two = sum_everywhere(scalars, grad_w1, grad_w2, lon, beside)
    many = 9 * chans
    sums = (one[:many], one[many], one[many + 1], one[many + 2], two[:many], two[many], two[many + 1], two[many + 2])
    grad_whole = place(scalars, send_core(scalars, *input_grad[0], "grad_halves"), 0, None, "grad_place")
    home, grad_whole = lax.optimization_barrier((input_grad[1][0], grad_whole))
    pieces = send_core(scalars, home, input_grad[1][1], "grad_halves")
    home, *sums = lax.optimization_barrier((home, *sums))
    pieces = (home,) + pieces[1:]
    grad_whole = place(scalars, pieces, 1, grad_whole, "grad_place")
    return (
        out_whole.reshape(fields.shape),
        grad_whole.reshape(fields.shape),
        sums[0].reshape(weight_one.shape),
        *sums[1:4],
        sums[4].reshape(weight_two.shape),
        *sums[5:8],
    )


def solution(mesh):
    field = P(None, None, "lat", "lon", None)
    return jax.shard_map(
        shards,
        mesh=mesh,
        in_specs=(field,) + (P(),) * 8 + (field,),
        out_specs=(field, field) + (P(),) * 8,
        check_vma=False,
    )
```

time: 973 us -> 302 us (0.31)
  blocking collectives: 310 us -> 0 us
  matrix products: 262 us -> 0 us
  Pallas kernels: 0 us -> 137 us
  waiting for transfers between devices: 144 us -> 74 us
  other arithmetic: 63.7 us -> 0.59 us
  starting transfers between devices: 129 us -> 74.6 us
  local copies, waits for them, and re-layouts: 39.3 us -> 13.2 us
  between operations: 17.6 us -> 1.81 us
    psum x7 -> x0, blocking collectives: 310 us -> none  [the longest x2 84.6 us: norm_back(): dgain, dshift = lax.psum((local_gain, local_shift), ('lat', 'lon'))]
    conv_general_dilated x16 -> x0, matrix products: 150 us -> none  [correlate(): lax.conv_general_dilated(extended, kernel, (1, 1), 'VALID', dimension_num...]
    pallas_call x0 -> x30, Pallas kernels: none -> 137 us  [the longest x22 122 us: call(): pl.pallas_call(kernel, in_specs=[SMEM] + [HBM if isinstance(a, Stream) el...]
    dot_general x72 -> x0, matrix products: 113 us -> none  [kernel_grad(): jnp.einsum('bhwc,bhwd->cd', window, slope, precision=lax.Precision.HIGHEST)]
    ppermute x64 -> x53, starting transfers between devices: 129 us -> 74.6 us  [permute(): return lax.ppermute(value, AXES, pairs)]
    ppermute x64 -> x53, waiting for transfers between devices: 125 us -> 74 us  [permute(): return lax.ppermute(value, AXES, pairs)]
    reduce_sum x19 -> x0, other arithmetic: 30.6 us -> none  [the longest x8 9.41 us: moments(): local_squares = jnp.sum(deviate * deviate, axis=(0, 1, 2))]
    psum x1 -> x0, waiting for transfers between devices: 19.2 us -> none  [shards(): lax.psum((grad_w1, grad_b1, grad_g1, grad_s1, grad_w2, grad_b2, grad_g2,...]
  transfers between devices with their start and end apart: 65 -> 53, of which waited for: 11 -> 16; matrix products, arithmetic and copies ran while one was open for 29% -> 1% of each run, Pallas kernels for 0% -> 40%
where the time goes in v2:
time: 302 us
  Pallas kernels  137 us (45%)
  starting transfers between devices  74.6 us (25%)
  waiting for transfers between devices  74 us (25%)
  local copies, waits for them, and re-layouts  13.2 us (4%)
    pallas_call x22, Pallas kernels, call(): pl.pallas_call(kernel, in_specs=[SMEM] + [HBM if isinstance(a, Stream) el...  122 us
    ppermute x53, starting transfers between devices, permute(): return lax.ppermute(value, AXES, pairs)  74.6 us
    ppermute x53, waiting for transfers between devices, permute(): return lax.ppermute(value, AXES, pairs)  74 us
    unnamed x84, local copies, waits for them, and re-layouts  10.6 us
    pallas_call x4, Pallas kernels, place(): pl.pallas_call(functools.partial(place_kernel, chunk), in_specs=[SMEM] +...  8.07 us
    pallas_call x4, Pallas kernels, pack(): pl.pallas_call(functools.partial(pack_kernel, other_core), in_specs=[SMEM...  7.86 us
  transfers between devices with their start and end apart: 53, of which 16 were waited for; matrix products, arithmetic and copies ran while one was open for 1% of the time, Pallas kernels for 40%

profile of v2, /device:TPU:0, one launch (start us, length us, event | category | flops | bytes accessed | tf_op | source)
XLA Modules:
  0.0 301.6 jit_solution(3339704874647470889)
XLA Ops:
  14.7 16.5 %collective-permute-done.3.refs_3_ = f32[12,2,8,128]{3,2,1,0:T(8,128)S(1)} collective-permute-done((f32[12,2,8,128]{3,2,1,0:T(8,128)S(1)}, f32[12,2,8,128]{3,2,1,0:T(8,128)S(1)}, u32[]{:S(2)}, u32[]{:S(2)}) %collective-permute-start.3) | collective-permute-done | bytes 98336 | tf_op jit(solution)/shard_map/ppermute | solution.py:28
  42.8 11.2 %collective-permute-done.5.refs_1_ = f32[12,128,128]{2,1,0:T(8,128)S(1)} collective-permute-done((f32[12,128,128]{2,1,0:T(8,128)S(1)}, f32[12,128,128]{2,1,0:T(8,128)S(1)}, u32[]{:S(2)}, u32[]{:S(2)}) %collective-permute-start.5) | collective-permute-done | bytes 786464 | tf_op jit(solution)/shard_map/ppermute | solution.py:28
  55.5 4.4 %collective-permute-start.9 = (f32[12,136,128]{2,1,0:T(8,128)S(1)}, f32[12,136,128]{2,1,0:T(8,128)S(1)}, u32[]{:S(2)}, u32[]{:S(2)}) collective-permute-start(f32[12,136,128]{2,1,0:T(8,128)S(1)} %get-tuple-element.122), channel_id=1, source_target_pairs={{0,8},{1,9},{2,10},{3,11},{4,12},{5,13},{6,14},{7,15},{8,0},{9,1},... | collective-permute-start | bytes 2506760 | tf_op jit(solution)/shard_map/ppermute | solution.py:28
  62.0 11.7 %conv_one.1 = (f32[12,4,136,128]{3,2,1,0:T(8,128)}, f32[8,128]{1,0:T(8,128)S(1)}) custom-call(s32[6]{0:T(128)S(1)} %stack.35.s_ref, f32[12,2,136,128]{3,2,1,0:T(8,128)S(1)} %get-tuple-element.126.refs_0_.refs_3_.refs_6_, f32[12,2,136,128]{3,2,1,0:T(8,128)S(1)} %get-tuple-element.115.refs_1_.refs_4_.refs_7_, ...), custom_call_target="tpu_custom_call" | custom-call | tf_op jit(solution)/shard_map/conv_one/pallas_call | solution.py:173
  73.7 6.7 %collective-permute-done.11.refs_1_ = f32[6,2,128,128]{3,2,1,0:T(8,128)S(1)} collective-permute-done((f32[6,2,128,128]{3,2,1,0:T(8,128)S(1)}, f32[6,2,128,128]{3,2,1,0:T(8,128)S(1)}, u32[]{:S(2)}, u32[]{:S(2)}) %collective-permute-start.11) | collective-permute-done | bytes 786464 | tf_op jit(solution)/shard_map/ppermute | solution.py:28
  81.9 3.1 %collective-permute-done.12 = f32[8,128]{1,0:T(8,128)S(1)} collective-permute-done((f32[8,128]{1,0:T(8,128)S(1)}, f32[8,128]{1,0:T(8,128)S(1)}, u32[]{:S(2)}, u32[]{:S(2)}) %collective-permute-start.12) | collective-permute-done | bytes 4128 | tf_op jit(solution)/shard_map/ppermute | solution.py:28
  91.3 10.5 %conv_one_halo.1 = (f32[12,136,128]{2,1,0:T(8,128)S(1)}, f32[12,136,128]{2,1,0:T(8,128)S(1)}) custom-call(s32[6]{0:T(128)S(1)} %stack.35.s_ref, f32[12,2,136,128]{3,2,1,0:T(8,128)} %copy-done, f32[12,136,128]{2,1,0:T(8,128)} %copy-done.4, f32[12,136,128]{2,1,0:T(8,128)} %copy-done.5, f32[12,136,128]{2,1,0:T(8,128)} %copy-done.35, ...), custom_call_target="tpu_custom_call" | custom-call | tf_op jit(solution)/shard_map/conv_one_halo/pallas_call | solution.py:173
  108.1 5.1 %collective-permute-start.19 = (f32[6,136,128]{2,1,0:T(8,128)S(1)}, f32[6,136,128]{2,1,0:T(8,128)S(1)}, u32[]{:S(2)}, u32[]{:S(2)}) collective-permute-start(f32[6,136,128]{2,1,0:T(8,128)S(1)} %get-tuple-element.140), channel_id=1, source_target_pairs={{0,8},{1,9},{2,10},{3,11},{4,12},{5,13},{6,14},{7,15},{8,0},{9,1},... | collective-permute-start | bytes 1253384 | tf_op jit(solution)/shard_map/ppermute | solution.py:28
  113.3 9.5 %conv_two.2 = (f32[6,4,136,128]{3,2,1,0:T(8,128)}, f32[6,136,128]{2,1,0:T(8,128)}, f32[6,136,128]{2,1,0:T(8,128)}, f32[8,128]{1,0:T(8,128)S(1)}) custom-call(s32[6]{0:T(128)S(1)} %stack.35.s_ref, f32[12,4,136,128]{3,2,1,0:T(8,128)} %get-tuple-element.119.refs_0_.refs_2_.refs_4_.refs_1_.refs_10_, f32[6,4,136,128]{3,2,1,0:T(8,128)} %get-tuple-element.134.refs_1_.refs_4_, ...), custom_call_target="tpu_custom_call" | custom-call | tf_op jit(solution)/shard_map/conv_two/pallas_call | solution.py:173
  126.3 5.9 %collective-permute-done.17.refs_7_ = f32[6,136,128]{2,1,0:T(8,128)S(1)} collective-permute-done((f32[6,136,128]{2,1,0:T(8,128)S(1)}, f32[6,136,128]{2,1,0:T(8,128)S(1)}, u32[]{:S(2)}, u32[]{:S(2)}) %collective-permute-start.17) | collective-permute-done | bytes 417824 | tf_op jit(solution)/shard_map/ppermute | solution.py:28
  132.2 8.7 %conv_two.3 = (f32[6,4,136,128]{3,2,1,0:T(8,128)}, f32[6,136,128]{2,1,0:T(8,128)S(1)}, f32[6,136,128]{2,1,0:T(8,128)S(1)}, f32[8,128]{1,0:T(8,128)S(1)}) custom-call(s32[6]{0:T(128)S(1)} %stack.35.s_ref, f32[12,4,136,128]{3,2,1,0:T(8,128)} %get-tuple-element.119.refs_0_.refs_2_.refs_4_.refs_1_.refs_10_, ...), custom_call_target="tpu_custom_call" | custom-call | tf_op jit(solution)/shard_map/conv_two/pallas_call | solution.py:173
  143.0 3.1 %collective-permute-done.21 = f32[8,128]{1,0:T(8,128)S(1)} collective-permute-done((f32[8,128]{1,0:T(8,128)S(1)}, f32[8,128]{1,0:T(8,128)S(1)}, u32[]{:S(2)}, u32[]{:S(2)}) %collective-permute-start.21) | collective-permute-done | bytes 4128 | tf_op jit(solution)/shard_map/ppermute | solution.py:28
  156.7 11.6 %conv_three.2 = (f32[6,4,136,128]{3,2,1,0:T(8,128)}, f32[6,4,128,128]{3,2,1,0:T(8,128)}, f32[6,136,128]{2,1,0:T(8,128)S(1)}, f32[6,136,128]{2,1,0:T(8,128)S(1)},...) custom-call(s32[6]{0:T(128)S(1)} %stack.35.s_ref, ...), custom_call_target="tpu_custom_call" | custom-call | tf_op jit(solution)/shard_map/conv_three/pallas_call | solution.py:173
  171.3 11.0 %conv_three.3 = (f32[6,4,136,128]{3,2,1,0:T(8,128)}, f32[6,4,128,128]{3,2,1,0:T(8,128)}, f32[6,136,128]{2,1,0:T(8,128)S(1)}, f32[6,136,128]{2,1,0:T(8,128)S(1)},...) custom-call(s32[6]{0:T(128)S(1)} %stack.35.s_ref, ...), custom_call_target="tpu_custom_call" | custom-call | tf_op jit(solution)/shard_map/conv_three/pallas_call | solution.py:173
  189.5 3.2 %collective-permute-start.35 = (f32[8,128]{1,0:T(8,128)S(1)}, f32[8,128]{1,0:T(8,128)S(1)}, u32[]{:S(2)}, u32[]{:S(2)}) collective-permute-start(f32[8,128]{1,0:T(8,128)S(1)} %add.388), channel_id=1, source_target_pairs={{0,8},{1,9},{2,10},{3,11},{4,12},{5,13},{6,14},{7,15},{8,0},{9,1},... | collective-permute-start | bytes 12296 | tf_op jit(solution)/shard_map/ppermute | solution.py:28
  198.9 13.1 %weight_two.1 = f32[1184,128]{1,0:T(8,128)S(1)} custom-call(s32[6]{0:T(128)S(1)} %stack.35.s_ref, f32[12,4,136,128]{3,2,1,0:T(8,128)} %get-tuple-element.119.refs_0_.refs_2_.refs_4_.refs_1_.refs_10_, f32[12,136,128]{2,1,0:T(8,128)} %copy-done.2, f32[12,136,128]{2,1,0:T(8,128)} %copy-done.3, f32[6,4,128,128]{3,2,1,0:T(8,128)} %get-tuple-element.167.refs_3_, ...), custom_call_target="tpu_custom_call" | custom-call | tf_op jit(solution)/shard_map/weight_two/pallas_call | solution.py:173
  212.1 9.4 %conv_four.2 = (f32[6,2,128,128]{3,2,1,0:T(8,128)S(1)}, f32[6,2,128,128]{3,2,1,0:T(8,128)}) custom-call(s32[6]{0:T(128)S(1)} %stack.35.s_ref, f32[6,4,136,128]{3,2,1,0:T(8,128)} %get-tuple-element.152.refs_0_.refs_5_, f32[12,4,136,128]{3,2,1,0:T(8,128)} %get-tuple-element.119.refs_0_.refs_2_.refs_4_.refs_1_.refs_10_, f32[12,136,128]{2,1,0:T(8,128)} %copy-done.2, ...), custom_call_target="tpu_custom_call" | custom-call | tf_op jit(solution)/shard_map/conv_four/pallas_call | solution.py:173
  223.9 14.1 %weight_one.1 = f32[1184,128]{1,0:T(8,128)S(1)} custom-call(s32[6]{0:T(128)S(1)} %stack.35.s_ref, f32[12,2,136,128]{3,2,1,0:T(8,128)} %copy-done, f32[12,2,136,128]{3,2,1,0:T(8,128)} %copy-done.1, f32[12,136,128]{2,1,0:T(8,128)} %copy-done.4, f32[12,136,128]{2,1,0:T(8,128)} %copy-done.5, ...), custom_call_target="tpu_custom_call" | custom-call | tf_op jit(solution)/shard_map/weight_one/pallas_call | solution.py:173
  242.3 4.8 %collective-permute-start.36 = (f32[6,136,128]{2,1,0:T(8,128)S(1)}, f32[6,136,128]{2,1,0:T(8,128)S(1)}, u32[]{:S(2)}, u32[]{:S(2)}) collective-permute-start(f32[6,136,128]{2,1,0:T(8,128)S(1)} %copy-done.29), channel_id=1, source_target_pairs={{0,8},{1,9},{2,10},{3,11},{4,12},{5,13},{6,14},{7,15},{8,0},{9,1},... | collective-permute-start | bytes 1253384 | tf_op jit(solution)/shard_map/ppermute | solution.py:28
  248.3 8.7 %collective-permute-start.43 = (f32[296,128]{1,0:T(8,128)S(1)}, f32[296,128]{1,0:T(8,128)S(1)}, u32[]{:S(2)}, u32[]{:S(2)}) collective-permute-start(f32[296,128]{1,0:T(8,128)S(1)} %get-tuple-element.181), channel_id=1, source_target_pairs={{0,8},{1,9},{2,10},{3,11},{4,12},{5,13},{6,14},{7,15},{8,0},{9,1},... | collective-permute-start | bytes 454664 | tf_op jit(solution)/shard_map/ppermute | solution.py:28
  258.3 8.5 %conv_four.3 = (f32[6,2,128,128]{3,2,1,0:T(8,128)S(1)}, f32[6,2,128,128]{3,2,1,0:T(8,128)S(1)}) custom-call(s32[6]{0:T(128)S(1)} %stack.35.s_ref, f32[6,4,136,128]{3,2,1,0:T(8,128)} %get-tuple-element.158.refs_11_.refs_0_, f32[12,4,136,128]{3,2,1,0:T(8,128)} %get-tuple-element.119.refs_0_.refs_2_.refs_4_.refs_1_.refs_10_, f32[12,136,128]{2,1,0:T(8,128)} %copy-done.2, ...), custom_call_target="tpu_custom_call" | custom-call | tf_op jit(solution)/shard_map/conv_four/pallas_call | solution.py:173
  271.5 4.7 %collective-permute-done.45 = f32[296,128]{1,0:T(8,128)S(1)} collective-permute-done((f32[296,128]{1,0:T(8,128)S(1)}, f32[296,128]{1,0:T(8,128)S(1)}, u32[]{:S(2)}, u32[]{:S(2)}) %collective-permute-start.45) | collective-permute-done | bytes 151584 | tf_op jit(solution)/shard_map/ppermute | solution.py:28
  279.8 4.8 %collective-permute-done.46 = f32[296,128]{1,0:T(8,128)S(1)} collective-permute-done((f32[296,128]{1,0:T(8,128)S(1)}, f32[296,128]{1,0:T(8,128)S(1)}, u32[]{:S(2)}, u32[]{:S(2)}) %collective-permute-start.46) | collective-permute-done | bytes 151584 | tf_op jit(solution)/shard_map/ppermute | solution.py:28
  288.1 5.1 %collective-permute-done.47.refs_1_.foreign = f32[6,2,128,128]{3,2,1,0:T(8,128)S(1)} collective-permute-done((f32[6,2,128,128]{3,2,1,0:T(8,128)S(1)}, f32[6,2,128,128]{3,2,1,0:T(8,128)S(1)}, u32[]{:S(2)}, u32[]{:S(2)}) %collective-permute-start.47) | collective-permute-done | bytes 786464 | tf_op jit(solution)/shard_map/ppermute | solution.py:28
  (238 shorter events, 104.5 us)
Async XLA Ops:
  7.1 24.1 %collective-permute-start.1 = (f32[12,128,128]{2,1,0:T(8,128)S(1)}, f32[12,128,128]{2,1,0:T(8,128)S(1)}, u32[]{:S(2)}, u32[]{:S(2)}) collective-permute-start(f32[12,128,128]{2,1,0:T(8,128)S(1)} %get-tuple-element.105), channel_id=1, source_target_pairs={{0,4},{1,5},{2,6},{3,7},{4,0},{5,1},{6,2},{7,3},{8,12},{9,13},{10,... | collective-permute-start | bytes 2359304 | tf_op jit(solution)/shard_map/ppermute | solution.py:28
  11.6 19.6 %collective-permute-start.3 = (f32[12,2,8,128]{3,2,1,0:T(8,128)S(1)}, f32[12,2,8,128]{3,2,1,0:T(8,128)S(1)}, u32[]{:S(2)}, u32[]{:S(2)}) collective-permute-start(f32[12,2,8,128]{3,2,1,0:T(8,128)S(1)} %get-tuple-element.107), channel_id=1, source_target_pairs={{0,6},{1,7},{2,4},{3,5},{4,2},{5,3},{6,0},{7,1},{8,14},{9,15},{10,... | collective-permute-start | bytes 294920 | tf_op jit(solution)/shard_map/ppermute | solution.py:28
  34.1 20.0 %collective-permute-start.5 = (f32[12,128,128]{2,1,0:T(8,128)S(1)}, f32[12,128,128]{2,1,0:T(8,128)S(1)}, u32[]{:S(2)}, u32[]{:S(2)}) collective-permute-start(f32[12,128,128]{2,1,0:T(8,128)S(1)} %get-tuple-element.114), channel_id=1, source_target_pairs={{0,4},{1,5},{2,6},{3,7},{4,0},{5,1},{6,2},{7,3},{8,12},{9,13},{10,... | collective-permute-start | bytes 2359304 | tf_op jit(solution)/shard_map/ppermute | solution.py:28
  35.6 25.8 %collective-permute-start.6 = (f32[12,136,128]{2,1,0:T(8,128)S(1)}, f32[12,136,128]{2,1,0:T(8,128)S(1)}, u32[]{:S(2)}, u32[]{:S(2)}) collective-permute-start(f32[12,136,128]{2,1,0:T(8,128)S(1)} %get-tuple-element.116), channel_id=1, source_target_pairs={{0,8},{1,9},{2,10},{3,11},{4,12},{5,13},{6,14},{7,15},{8,0},{9,1},... | collective-permute-start | bytes 2506760 | tf_op jit(solution)/shard_map/ppermute | solution.py:28
  39.2 22.8 %collective-permute-start.7 = (f32[12,136,128]{2,1,0:T(8,128)S(1)}, f32[12,136,128]{2,1,0:T(8,128)S(1)}, u32[]{:S(2)}, u32[]{:S(2)}) collective-permute-start(f32[12,136,128]{2,1,0:T(8,128)S(1)} %get-tuple-element.117), channel_id=1, source_target_pairs={{8,16},{9,17},{10,18},{11,19},{12,20},{13,21},{14,22},{15,23},{16,... | collective-permute-start | bytes 2506760 | tf_op jit(solution)/shard_map/ppermute | solution.py:28
  54.8 26.5 %collective-permute-start.10 = (f32[12,136,128]{2,1,0:T(8,128)S(1)}, f32[12,136,128]{2,1,0:T(8,128)S(1)}, u32[]{:S(2)}, u32[]{:S(2)}) collective-permute-start(f32[12,136,128]{2,1,0:T(8,128)S(1)} %get-tuple-element.123), channel_id=1, source_target_pairs={{8,16},{9,17},{10,18},{11,19},{12,20},{13,21},{14,22},{15,23},{16,... | collective-permute-start | bytes 2506760 | tf_op jit(solution)/shard_map/ppermute | solution.py:28
  55.5 25.8 %collective-permute-start.9 = (f32[12,136,128]{2,1,0:T(8,128)S(1)}, f32[12,136,128]{2,1,0:T(8,128)S(1)}, u32[]{:S(2)}, u32[]{:S(2)}) collective-permute-start(f32[12,136,128]{2,1,0:T(8,128)S(1)} %get-tuple-element.122), channel_id=1, source_target_pairs={{0,8},{1,9},{2,10},{3,11},{4,12},{5,13},{6,14},{7,15},{8,0},{9,1},... | collective-permute-start | bytes 2506760 | tf_op jit(solution)/shard_map/ppermute | solution.py:28
  60.0 20.5 %collective-permute-start.11 = (f32[6,2,128,128]{3,2,1,0:T(8,128)S(1)}, f32[6,2,128,128]{3,2,1,0:T(8,128)S(1)}, u32[]{:S(2)}, u32[]{:S(2)}) collective-permute-start(f32[6,2,128,128]{3,2,1,0:T(8,128)S(1)} %get-tuple-element.124), channel_id=1, source_target_pairs={{0,4},{1,5},{2,6},{3,7},{4,0},{5,1},{6,2},{7,3},{8,12},{9,13},{10,... | collective-permute-start | bytes 2359304 | tf_op jit(solution)/shard_map/ppermute | solution.py:28
  61.5 40.3 %collective-permute-start.8 = (f32[6,2,128,128]{3,2,1,0:T(8,128)}, f32[6,2,128,128]{3,2,1,0:T(8,128)}, u32[]{:S(2)}, u32[]{:S(2)}) collective-permute-start(f32[6,2,128,128]{3,2,1,0:T(8,128)} %get-tuple-element.120), channel_id=1, source_target_pairs={{0,4},{1,5},{2,6},{3,7},{4,0},{5,1},{6,2},{7,3},{8,12},{9,13},{10,... | collective-permute-start | bytes 2359304 | tf_op jit(solution)/shard_map/ppermute | solution.py:28
  88.8 19.1 %collective-permute-start.16 = (f32[8,128]{1,0:T(8,128)S(1)}, f32[8,128]{1,0:T(8,128)S(1)}, u32[]{:S(2)}, u32[]{:S(2)}) collective-permute-start(f32[8,128]{1,0:T(8,128)S(1)} %concatenate.40), channel_id=1, source_target_pairs={{0,16},{1,17},{2,18},{3,19},{4,20},{5,21},{6,22},{7,23},{8,24},{9,... | collective-permute-start | bytes 12296 | tf_op jit(solution)/shard_map/ppermute | solution.py:28
  103.9 21.0 %collective-permute-start.18 = (f32[6,136,128]{2,1,0:T(8,128)S(1)}, f32[6,136,128]{2,1,0:T(8,128)S(1)}, u32[]{:S(2)}, u32[]{:S(2)}) collective-permute-start(f32[6,136,128]{2,1,0:T(8,128)S(1)} %get-tuple-element.138), channel_id=1, source_target_pairs={{8,16},{9,17},{10,18},{11,19},{12,20},{13,21},{14,22},{15,23},{16,... | collective-permute-start | bytes 1253384 | tf_op jit(solution)/shard_map/ppermute | solution.py:28
  107.3 19.0 %collective-permute-start.20 = (f32[6,136,128]{2,1,0:T(8,128)S(1)}, f32[6,136,128]{2,1,0:T(8,128)S(1)}, u32[]{:S(2)}, u32[]{:S(2)}) collective-permute-start(f32[6,136,128]{2,1,0:T(8,128)S(1)} %get-tuple-element.141), channel_id=1, source_target_pairs={{8,16},{9,17},{10,18},{11,19},{12,20},{13,21},{14,22},{15,23},{16,... | collective-permute-start | bytes 1253384 | tf_op jit(solution)/shard_map/ppermute | solution.py:28
  113.2 19.0 %collective-permute-start.17 = (f32[6,136,128]{2,1,0:T(8,128)S(1)}, f32[6,136,128]{2,1,0:T(8,128)S(1)}, u32[]{:S(2)}, u32[]{:S(2)}) collective-permute-start(f32[6,136,128]{2,1,0:T(8,128)S(1)} %get-tuple-element.137), channel_id=1, source_target_pairs={{0,8},{1,9},{2,10},{3,11},{4,12},{5,13},{6,14},{7,15},{8,0},{9,1},... | collective-permute-start | bytes 1253384 | tf_op jit(solution)/shard_map/ppermute | solution.py:28
  122.8 23.3 %collective-permute-start.22 = (f32[6,136,128]{2,1,0:T(8,128)}, f32[6,136,128]{2,1,0:T(8,128)}, u32[]{:S(2)}, u32[]{:S(2)}) collective-permute-start(f32[6,136,128]{2,1,0:T(8,128)} %get-tuple-element.147), channel_id=1, source_target_pairs={{0,8},{1,9},{2,10},{3,11},{4,12},{5,13},{6,14},{7,15},{8,0},{9,1},... | collective-permute-start | bytes 1253384 | tf_op jit(solution)/shard_map/ppermute | solution.py:28
  124.9 21.3 %collective-permute-start.23 = (f32[6,136,128]{2,1,0:T(8,128)}, f32[6,136,128]{2,1,0:T(8,128)}, u32[]{:S(2)}, u32[]{:S(2)}) collective-permute-start(f32[6,136,128]{2,1,0:T(8,128)} %get-tuple-element.148), channel_id=1, source_target_pairs={{8,16},{9,17},{10,18},{11,19},{12,20},{13,21},{14,22},{15,23},{16,... | collective-permute-start | bytes 1253384 | tf_op jit(solution)/shard_map/ppermute | solution.py:28
  151.7 19.6 %collective-permute-start.26 = (f32[6,136,128]{2,1,0:T(8,128)}, f32[6,136,128]{2,1,0:T(8,128)S(1)}, u32[]{:S(2)}, u32[]{:S(2)}) collective-permute-start(f32[6,136,128]{2,1,0:T(8,128)} %copy-done.33), channel_id=1, source_target_pairs={{8,16},{9,17},{10,18},{11,19},{12,20},{13,21},{14,22},{15,23},{16,... | collective-permute-start | bytes 1253384 | tf_op jit(solution)/shard_map/ppermute | solution.py:28
  168.4 19.6 %collective-permute-start.33 = (f32[6,136,128]{2,1,0:T(8,128)S(1)}, f32[6,136,128]{2,1,0:T(8,128)S(1)}, u32[]{:S(2)}, u32[]{:S(2)}) collective-permute-start(f32[6,136,128]{2,1,0:T(8,128)S(1)} %get-tuple-element.162), channel_id=1, source_target_pairs={{0,8},{1,9},{2,10},{3,11},{4,12},{5,13},{6,14},{7,15},{8,0},{9,1},... | collective-permute-start | bytes 1253384 | tf_op jit(solution)/shard_map/ppermute | solution.py:28
  169.0 19.7 %collective-permute-start.34 = (f32[6,136,128]{2,1,0:T(8,128)S(1)}, f32[6,136,128]{2,1,0:T(8,128)S(1)}, u32[]{:S(2)}, u32[]{:S(2)}) collective-permute-start(f32[6,136,128]{2,1,0:T(8,128)S(1)} %get-tuple-element.163), channel_id=1, source_target_pairs={{8,16},{9,17},{10,18},{11,19},{12,20},{13,21},{14,22},{15,23},{16,... | collective-permute-start | bytes 1253384 | tf_op jit(solution)/shard_map/ppermute | solution.py:28
  169.7 42.3 %collective-permute-start.30 = (f32[6,2,128,128]{3,2,1,0:T(8,128)}, f32[6,2,128,128]{3,2,1,0:T(8,128)}, u32[]{:S(2)}, u32[]{:S(2)}) collective-permute-start(f32[6,2,128,128]{3,2,1,0:T(8,128)} %get-tuple-element.157), channel_id=1, source_target_pairs={{0,4},{1,5},{2,6},{3,7},{4,0},{5,1},{6,2},{7,3},{8,12},{9,13},{10,... | collective-permute-start | bytes 2359304 | tf_op jit(solution)/shard_map/ppermute | solution.py:28
  183.9 28.2 %collective-permute-start.28 = (f32[6,2,128,128]{3,2,1,0:T(8,128)}, f32[6,2,128,128]{3,2,1,0:T(8,128)S(1)}, u32[]{:S(2)}, u32[]{:S(2)}) collective-permute-start(f32[6,2,128,128]{3,2,1,0:T(8,128)} %get-tuple-element.155), channel_id=1, source_target_pairs={{0,4},{1,5},{2,6},{3,7},{4,0},{5,1},{6,2},{7,3},{8,12},{9,13},{10,... | collective-permute-start | bytes 2359304 | tf_op jit(solution)/shard_map/ppermute | solution.py:28
  240.3 26.5 %collective-permute-start.31 = (f32[2,6,2,64,128]{4,3,2,1,0:T(8,128)S(1)}, f32[2,6,2,64,128]{4,3,2,1,0:T(8,128)S(1)}, u32[]{:S(2)}, u32[]{:S(2)}) collective-permute-start(f32[2,6,2,64,128]{4,3,2,1,0:T(8,128)S(1)} %output_halves.3), channel_id=1, source_target_pairs={{0,1},{1,0},{2,3},{3,2},{4,5},{5,4},{6,7},{7,6},{8,9},{9,8},{10,11... | collective-permute-start | bytes 2359304 | tf_op jit(solution)/shard_map/ppermute | solution.py:28
  241.0 28.1 %collective-permute-start.29 = (f32[2,6,2,64,128]{4,3,2,1,0:T(8,128)S(1)}, f32[2,6,2,64,128]{4,3,2,1,0:T(8,128)S(1)}, u32[]{:S(2)}, u32[]{:S(2)}) collective-permute-start(f32[2,6,2,64,128]{4,3,2,1,0:T(8,128)S(1)} %output_halves.2), channel_id=1, source_target_pairs={{0,1},{1,0},{2,3},{3,2},{4,5},{5,4},{6,7},{7,6},{8,9},{9,8},{10,11... | collective-permute-start | bytes 2359304 | tf_op jit(solution)/shard_map/ppermute | solution.py:28
  247.7 23.2 %collective-permute-start.42 = (f32[296,128]{1,0:T(8,128)S(1)}, f32[296,128]{1,0:T(8,128)S(1)}, u32[]{:S(2)}, u32[]{:S(2)}) collective-permute-start(f32[296,128]{1,0:T(8,128)S(1)} %get-tuple-element.180), channel_id=1, source_target_pairs={{0,2},{1,3},{2,0},{3,1},{4,6},{5,7},{6,4},{7,5},{8,10},{9,11},{10,... | collective-permute-start | bytes 454664 | tf_op jit(solution)/shard_map/ppermute | solution.py:28
  248.3 22.6 %collective-permute-start.43 = (f32[296,128]{1,0:T(8,128)S(1)}, f32[296,128]{1,0:T(8,128)S(1)}, u32[]{:S(2)}, u32[]{:S(2)}) collective-permute-start(f32[296,128]{1,0:T(8,128)S(1)} %get-tuple-element.181), channel_id=1, source_target_pairs={{0,8},{1,9},{2,10},{3,11},{4,12},{5,13},{6,14},{7,15},{8,0},{9,1},... | collective-permute-start | bytes 454664 | tf_op jit(solution)/shard_map/ppermute | solution.py:28
  (71 other events, 667.0 us)

commit v3 on v2

--- a/solution.py
+++ b/solution.py
@@ -904,9 +904,9 @@
     for target in group_steps()[2:]:
         own = own + permute(own, target)
     others = [permute(own, target) for target in targets]
-    value = call(whole_kernel, scalars, [after(own, last), *others], [(4 * size, chans)], [], "whole")[0]
+    value = call(whole_kernel, scalars, [after(own, last, *beside[3]), *others], [(4 * size, chans)], [], "whole")[0]
     other = permute(value, to_core)
-    return jnp.where(west, value, other), jnp.where(west, other, value)
+    return value, other
 
 
 def shards(
@@ -948,7 +948,7 @@
     x_parts = (x_edge, x_inner)
 
     z1, stats = first_conv(scalars, x_parts, x_halos, taps_one, after(rows_of(bias_one), g_home))
-    partial = all_moments(after(stats, *x_far, g_foreign[0]), here)
+    partial = all_moments(stats, here, *x_far, g_foreign[0])
     z1_halos = tuple(
         first_halo_conv(scalars, after(x_edge, partial[-2]), x_halos, x_far, taps_one, rows_of(bias_one))
     )
@@ -969,12 +969,13 @@
         z, pair_row, next_row, stats = second_conv(
             scalars, z1, z1_halos, g_rows[chunk], after(coef_one, *earlier), taps_two, rows_of(bias_two), chunk
         )
-        earlier = [z, *g_halos[0], *g_halos[1]]
+        earlier = [z, *g_halos[0]]
         z2.append(z)
         z2_edges.append((pair_row, next_row))
         parts.append(stats)
     z2_halos = [exchange_rows(*z2_edges[0])]
-    partial = all_moments(merge_moments(parts[0], parts[1], here / CHUNKS), here, *z2_halos[0])
+    stats = after(merge_moments(parts[0], parts[1], here / CHUNKS), *g_halos[1])
+    partial = all_moments(stats, here, *z2_halos[0])
     z2_halos.append(exchange_rows(after(z2_edges[1][0], partial[-2]), z2_edges[1][1]))
     stats = partial[-1]
     center_two, spread_two, dshift_two = stats[0], stats[1] / count, stats[2]
@@ -1013,7 +1014,7 @@
             scalars, dh1[chunk], dh1_halos[chunk], z1, z1_halos, g_rows[chunk], coef, taps_one, chunk
         )
 
-    pieces = input_slope(0, after(coef, grad_w2, output[0][1], output[1][1]))
+    pieces = input_slope(0, after(coef, grad_w2, output[0][1], output[1][1], *dh1_halos[1]))
     grad_w1 = weight_one_grad(scalars, x_parts, x_halos, dh1, z1, after(coef, pieces[0]), small)
     input_grad = [send_side(*pieces)]
     pieces = input_slope(1, after(coef, grad_w1))
@@ -1024,11 +1025,14 @@
         input_grad.append(send_side(pieces[0], after(pieces[1], summed)))
         return input_grad[1][1]
 
-    beside = ([input_grad[0][1]], [pieces[0], out_whole], send_last)
+    grad_whole = place(scalars, send_core(scalars, *input_grad[0], "grad_halves"), 0, None, "grad_place")
+    beside = ([input_grad[0][1]], pieces[:1], send_last, [out_whole, grad_whole])
     one, two = sum_everywhere(scalars, grad_w1, grad_w2, lon, beside)
-    many = 9 * chans
-    sums = (one[:many], one[many], one[many + 1], one[many + 2], two[:many], two[many], two[many + 1], two[many + 2])
-    grad_whole = place(scalars, send_core(scalars, *input_grad[0], "grad_halves"), 0, None, "grad_place")
+    many, west = 9 * chans, lon % 2 == 0
+    sums = []
+    for mine, its in ((one, two), (two, one)):
+        sums.append(jnp.where(west, mine[:many], its[:many]))
+        sums += [jnp.where(west, mine[many + row], its[many + row]) for row in range(3)]
     home, grad_whole = lax.optimization_barrier((input_grad[1][0], grad_whole))
     pieces = send_core(scalars, home, input_grad[1][1], "grad_halves")
     home, *sums = lax.optimization_barrier((home, *sums))

time: 302 us -> 279 us (0.924)
  waiting for transfers between devices: 74 us -> 60.2 us
  starting transfers between devices: 74.6 us -> 66.9 us
  local copies, waits for them, and re-layouts: 13.2 us -> 7.06 us
    ppermute x53, waiting for transfers between devices: 74 us -> 60.2 us  [permute(): return lax.ppermute(value, AXES, pairs)]
    ppermute x53, starting transfers between devices: 74.6 us -> 66.9 us  [permute(): return lax.ppermute(value, AXES, pairs)]
    unnamed x84 -> x62, local copies, waits for them, and re-layouts: 10.6 us -> 6.71 us
  transfers between devices with their start and end apart: 53 -> 53, of which waited for: 16 -> 14; matrix products, arithmetic and copies ran while one was open for 1% -> 1% of each run, Pallas kernels for 40% -> 44%
where the time goes in v3:
time: 279 us; the launch traced here: 278 us
  Pallas kernels  140 us (50%)
  starting transfers between devices  66.9 us (24%)
  waiting for transfers between devices  60.2 us (22%)
  local copies, waits for them, and re-layouts  7.06 us (3%)
    pallas_call x22, Pallas kernels, call(): pl.pallas_call(kernel, in_specs=[SMEM] + [HBM if isinstance(a, Stream) el...  124 us
    ppermute x53, starting transfers between devices, permute(): return lax.ppermute(value, AXES, pairs)  66.9 us
    ppermute x53, waiting for transfers between devices, permute(): return lax.ppermute(value, AXES, pairs)  60.2 us
    pallas_call x4, Pallas kernels, place(): pl.pallas_call(functools.partial(place_kernel, chunk), in_specs=[SMEM] +...  8.06 us
    pallas_call x4, Pallas kernels, pack(): pl.pallas_call(functools.partial(pack_kernel, other_core), in_specs=[SMEM...  7.87 us
    unnamed x62, local copies, waits for them, and re-layouts  6.71 us
  transfers between devices with their start and end apart: 53, of which 14 were waited for; matrix products, arithmetic and copies ran while one was open for 1% of the time, Pallas kernels for 44%

profile of v3, /device:TPU:0, one launch (start us, length us, event | category | flops | bytes accessed | tf_op | source)
XLA Modules:
  0.0 278.0 jit_solution(645668444810671400)
XLA Ops:
  7.1 2.9 %collective-permute-start.1 = (f32[12,128,128]{2,1,0:T(8,128)S(1)}, f32[12,128,128]{2,1,0:T(8,128)S(1)}, u32[]{:S(2)}, u32[]{:S(2)}) collective-permute-start(f32[12,128,128]{2,1,0:T(8,128)S(1)} %get-tuple-element.106), channel_id=1, source_target_pairs={{0,4},{1,5},{2,6},{3,7},{4,0},{5,1},{6,2},{7,3},{8,12},{9,13},{10,... | collective-permute-start | bytes 2359304 | tf_op jit(solution)/shard_map/ppermute | solution.py:28
  11.6 3.1 %collective-permute-done.2.refs_2_ = f32[12,2,8,128]{3,2,1,0:T(8,128)S(1)} collective-permute-done((f32[12,2,8,128]{3,2,1,0:T(8,128)S(1)}, f32[12,2,8,128]{3,2,1,0:T(8,128)S(1)}, u32[]{:S(2)}, u32[]{:S(2)}) %collective-permute-start.2) | collective-permute-done | bytes 98336 | tf_op jit(solution)/shard_map/ppermute | solution.py:28
  14.7 16.5 %collective-permute-done.3.refs_3_ = f32[12,2,8,128]{3,2,1,0:T(8,128)S(1)} collective-permute-done((f32[12,2,8,128]{3,2,1,0:T(8,128)S(1)}, f32[12,2,8,128]{3,2,1,0:T(8,128)S(1)}, u32[]{:S(2)}, u32[]{:S(2)}) %collective-permute-start.3) | collective-permute-done | bytes 98336 | tf_op jit(solution)/shard_map/ppermute | solution.py:28
  41.9 12.2 %collective-permute-done.5.refs_1_ = f32[12,128,128]{2,1,0:T(8,128)S(1)} collective-permute-done((f32[12,128,128]{2,1,0:T(8,128)S(1)}, f32[12,128,128]{2,1,0:T(8,128)S(1)}, u32[]{:S(2)}, u32[]{:S(2)}) %collective-permute-start.5) | collective-permute-done | bytes 786464 | tf_op jit(solution)/shard_map/ppermute | solution.py:28
  60.8 11.8 %conv_one.1 = (f32[12,4,136,128]{3,2,1,0:T(8,128)}, f32[8,128]{1,0:T(8,128)S(1)}) custom-call(s32[6]{0:T(128)S(1)} %stack.35.s_ref, f32[12,2,136,128]{3,2,1,0:T(8,128)S(1)} %get-tuple-element.127.refs_0_.refs_3_.refs_6_, f32[12,2,136,128]{3,2,1,0:T(8,128)S(1)} %get-tuple-element.116.refs_1_.refs_4_.refs_7_, ...), custom_call_target="tpu_custom_call" | custom-call | tf_op jit(solution)/shard_map/conv_one/pallas_call | solution.py:173
  73.2 3.1 %collective-permute-done.9 = f32[8,128]{1,0:T(8,128)S(1)} collective-permute-done((f32[8,128]{1,0:T(8,128)S(1)}, f32[8,128]{1,0:T(8,128)S(1)}, u32[]{:S(2)}, u32[]{:S(2)}) %collective-permute-start.9) | collective-permute-done | bytes 4128 | tf_op jit(solution)/shard_map/ppermute | solution.py:28
  78.2 3.3 %collective-permute-start.13 = (f32[8,128]{1,0:T(8,128)S(1)}, f32[8,128]{1,0:T(8,128)S(1)}, u32[]{:S(2)}, u32[]{:S(2)}) collective-permute-start(f32[8,128]{1,0:T(8,128)S(1)} %concatenate.39), channel_id=1, source_target_pairs={{0,8},{1,9},{2,10},{3,11},{4,12},{5,13},{6,14},{7,15},{8,0},{9,1},... | collective-permute-start | bytes 12296 | tf_op jit(solution)/shard_map/ppermute | solution.py:28
  88.7 10.4 %conv_one_halo.1 = (f32[12,136,128]{2,1,0:T(8,128)S(1)}, f32[12,136,128]{2,1,0:T(8,128)S(1)}) custom-call(s32[6]{0:T(128)S(1)} %stack.35.s_ref, f32[12,2,136,128]{3,2,1,0:T(8,128)} %copy-done, f32[12,136,128]{2,1,0:T(8,128)} %copy-done.4, f32[12,136,128]{2,1,0:T(8,128)} %copy-done.5, f32[12,136,128]{2,1,0:T(8,128)} %copy-done.24, ...), custom_call_target="tpu_custom_call" | custom-call | tf_op jit(solution)/shard_map/conv_one_halo/pallas_call | solution.py:173
  99.2 3.1 %g_cell.3 = (f32[6,4,136,128]{3,2,1,0:T(8,128)}, f32[6,136,128]{2,1,0:T(8,128)S(1)}, f32[6,136,128]{2,1,0:T(8,128)S(1)}) custom-call(s32[6]{0:T(128)S(1)} %stack.35.s_ref, f32[12,2,128,128]{3,2,1,0:T(8,128)S(1)} %copy-done.11, f32[6,2,128,128]{3,2,1,0:T(8,128)} %collective-permute-done.12.refs_1_, f32[12,2,8,128]{3,2,1,0:T(8,128)S(1)} %collective-permute-done.14.refs_2_, ...), custom_call_target="tpu_custom_call" | custom-call | tf_op jit(solution)/shard_map/g_cell/pallas_call | solution.py:173
  111.8 8.7 %conv_two.2 = (f32[6,4,136,128]{3,2,1,0:T(8,128)}, f32[6,136,128]{2,1,0:T(8,128)S(1)}, f32[6,136,128]{2,1,0:T(8,128)S(1)}, f32[8,128]{1,0:T(8,128)S(1)}) custom-call(s32[6]{0:T(128)S(1)} %stack.35.s_ref, f32[12,4,136,128]{3,2,1,0:T(8,128)} %get-tuple-element.120.refs_0_.refs_2_.refs_4_.refs_1_.refs_10_, ...), custom_call_target="tpu_custom_call" | custom-call | tf_op jit(solution)/shard_map/conv_two/pallas_call | solution.py:173
  122.1 8.8 %conv_two.3 = (f32[6,4,136,128]{3,2,1,0:T(8,128)}, f32[6,136,128]{2,1,0:T(8,128)S(1)}, f32[6,136,128]{2,1,0:T(8,128)S(1)}, f32[8,128]{1,0:T(8,128)S(1)}) custom-call(s32[6]{0:T(128)S(1)} %stack.35.s_ref, f32[12,4,136,128]{3,2,1,0:T(8,128)} %get-tuple-element.120.refs_0_.refs_2_.refs_4_.refs_1_.refs_10_, ...), custom_call_target="tpu_custom_call" | custom-call | tf_op jit(solution)/shard_map/conv_two/pallas_call | solution.py:173
  131.5 3.1 %collective-permute-done.21 = f32[8,128]{1,0:T(8,128)S(1)} collective-permute-done((f32[8,128]{1,0:T(8,128)S(1)}, f32[8,128]{1,0:T(8,128)S(1)}, u32[]{:S(2)}, u32[]{:S(2)}) %collective-permute-start.21) | collective-permute-done | bytes 4128 | tf_op jit(solution)/shard_map/ppermute | solution.py:28
  134.7 3.2 %collective-permute-start.24 = (f32[8,128]{1,0:T(8,128)S(1)}, f32[8,128]{1,0:T(8,128)S(1)}, u32[]{:S(2)}, u32[]{:S(2)}) collective-permute-start(f32[8,128]{1,0:T(8,128)S(1)} %concatenate.44), channel_id=1, source_target_pairs={{0,8},{1,9},{2,10},{3,11},{4,12},{5,13},{6,14},{7,15},{8,0},{9,1},... | collective-permute-start | bytes 12296 | tf_op jit(solution)/shard_map/ppermute | solution.py:28
  139.5 2.9 %collective-permute-start.27 = (f32[8,128]{1,0:T(8,128)S(1)}, f32[8,128]{1,0:T(8,128)S(1)}, u32[]{:S(2)}, u32[]{:S(2)}) collective-permute-start(f32[8,128]{1,0:T(8,128)S(1)} %concatenate.45), channel_id=1, source_target_pairs={{0,16},{1,17},{2,18},{3,19},{4,20},{5,21},{6,22},{7,23},{8,24},{9,... | collective-permute-start | bytes 12296 | tf_op jit(solution)/shard_map/ppermute | solution.py:28
  146.3 11.7 %conv_three.2 = (f32[6,4,136,128]{3,2,1,0:T(8,128)}, f32[6,4,128,128]{3,2,1,0:T(8,128)}, f32[6,136,128]{2,1,0:T(8,128)S(1)}, f32[6,136,128]{2,1,0:T(8,128)S(1)},...) custom-call(s32[6]{0:T(128)S(1)} %stack.35.s_ref, ...), custom_call_target="tpu_custom_call" | custom-call | tf_op jit(solution)/shard_map/conv_three/pallas_call | solution.py:173
  162.4 11.7 %conv_three.3 = (f32[6,4,136,128]{3,2,1,0:T(8,128)}, f32[6,4,128,128]{3,2,1,0:T(8,128)}, f32[6,136,128]{2,1,0:T(8,128)S(1)}, f32[6,136,128]{2,1,0:T(8,128)}, f32...) custom-call(s32[6]{0:T(128)S(1)} %stack.35.s_ref, ...), custom_call_target="tpu_custom_call" | custom-call | tf_op jit(solution)/shard_map/conv_three/pallas_call | solution.py:173
  175.2 3.1 %collective-permute-done.32 = f32[8,128]{1,0:T(8,128)S(1)} collective-permute-done((f32[8,128]{1,0:T(8,128)S(1)}, f32[8,128]{1,0:T(8,128)S(1)}, u32[]{:S(2)}, u32[]{:S(2)}) %collective-permute-start.32) | collective-permute-done | bytes 4128 | tf_op jit(solution)/shard_map/ppermute | solution.py:28
  179.8 3.6 %collective-permute-start.35 = (f32[8,128]{1,0:T(8,128)S(1)}, f32[8,128]{1,0:T(8,128)S(1)}, u32[]{:S(2)}, u32[]{:S(2)}) collective-permute-start(f32[8,128]{1,0:T(8,128)S(1)} %add.358), channel_id=1, source_target_pairs={{0,8},{1,9},{2,10},{3,11},{4,12},{5,13},{6,14},{7,15},{8,0},{9,1},... | collective-permute-start | bytes 12296 | tf_op jit(solution)/shard_map/ppermute | solution.py:28
  190.7 13.3 %weight_two.1 = f32[1184,128]{1,0:T(8,128)S(1)} custom-call(s32[6]{0:T(128)S(1)} %stack.35.s_ref, f32[12,4,136,128]{3,2,1,0:T(8,128)} %get-tuple-element.120.refs_0_.refs_2_.refs_4_.refs_1_.refs_10_, f32[12,136,128]{2,1,0:T(8,128)} %copy-done.2, f32[12,136,128]{2,1,0:T(8,128)} %copy-done.3, f32[6,4,128,128]{3,2,1,0:T(8,128)} %get-tuple-element.169.refs_3_, ...), custom_call_target="tpu_custom_call" | custom-call | tf_op jit(solution)/shard_map/weight_two/pallas_call | solution.py:173
  204.1 9.5 %conv_four.2 = (f32[6,2,128,128]{3,2,1,0:T(8,128)S(1)}, f32[6,2,128,128]{3,2,1,0:T(8,128)}) custom-call(s32[6]{0:T(128)S(1)} %stack.35.s_ref, f32[6,4,136,128]{3,2,1,0:T(8,128)} %get-tuple-element.154.refs_0_.refs_5_, f32[12,4,136,128]{3,2,1,0:T(8,128)} %get-tuple-element.120.refs_0_.refs_2_.refs_4_.refs_1_.refs_10_, f32[12,136,128]{2,1,0:T(8,128)} %copy-done.2, ...), custom_call_target="tpu_custom_call" | custom-call | tf_op jit(solution)/shard_map/conv_four/pallas_call | solution.py:173
  216.0 13.9 %weight_one.1 = f32[1184,128]{1,0:T(8,128)S(1)} custom-call(s32[6]{0:T(128)S(1)} %stack.35.s_ref, f32[12,2,136,128]{3,2,1,0:T(8,128)} %copy-done, f32[12,2,136,128]{3,2,1,0:T(8,128)} %copy-done.1, f32[12,136,128]{2,1,0:T(8,128)} %copy-done.4, f32[12,136,128]{2,1,0:T(8,128)} %copy-done.5, ...), custom_call_target="tpu_custom_call" | custom-call | tf_op jit(solution)/shard_map/weight_one/pallas_call | solution.py:173
  236.4 9.2 %conv_four.3 = (f32[6,2,128,128]{3,2,1,0:T(8,128)S(1)}, f32[6,2,128,128]{3,2,1,0:T(8,128)S(1)}) custom-call(s32[6]{0:T(128)S(1)} %stack.35.s_ref, f32[6,4,136,128]{3,2,1,0:T(8,128)} %get-tuple-element.160.refs_11_.refs_0_, f32[12,4,136,128]{3,2,1,0:T(8,128)} %get-tuple-element.120.refs_0_.refs_2_.refs_4_.refs_1_.refs_10_, f32[12,136,128]{2,1,0:T(8,128)} %copy-done.2, ...), custom_call_target="tpu_custom_call" | custom-call | tf_op jit(solution)/shard_map/conv_four/pallas_call | solution.py:173
  252.7 9.1 %collective-permute-done.46 = f32[296,128]{1,0:T(8,128)S(1)} collective-permute-done((f32[296,128]{1,0:T(8,128)S(1)}, f32[296,128]{1,0:T(8,128)S(1)}, u32[]{:S(2)}, u32[]{:S(2)}) %collective-permute-start.46) | collective-permute-done | bytes 151584 | tf_op jit(solution)/shard_map/ppermute | solution.py:28
  262.4 3.0 %collective-permute-start.50 = (f32[296,128]{1,0:T(8,128)S(1)}, f32[296,128]{1,0:T(8,128)S(1)}, u32[]{:S(2)}, u32[]{:S(2)}) collective-permute-start(f32[296,128]{1,0:T(8,128)S(1)} %add.366.refs_0_), channel_id=1, source_target_pairs={{0,10},{1,11},{2,8},{3,9},{4,14},{5,15},{6,12},{7,13},{8,2},{9,3},... | collective-permute-start | bytes 454664 | tf_op jit(solution)/shard_map/ppermute | solution.py:28
  (214 shorter events, 95.1 us)
Async XLA Ops:
  7.1 24.1 %collective-permute-start.1 = (f32[12,128,128]{2,1,0:T(8,128)S(1)}, f32[12,128,128]{2,1,0:T(8,128)S(1)}, u32[]{:S(2)}, u32[]{:S(2)}) collective-permute-start(f32[12,128,128]{2,1,0:T(8,128)S(1)} %get-tuple-element.106), channel_id=1, source_target_pairs={{0,4},{1,5},{2,6},{3,7},{4,0},{5,1},{6,2},{7,3},{8,12},{9,13},{10,... | collective-permute-start | bytes 2359304 | tf_op jit(solution)/shard_map/ppermute | solution.py:28
  11.6 19.6 %collective-permute-start.3 = (f32[12,2,8,128]{3,2,1,0:T(8,128)S(1)}, f32[12,2,8,128]{3,2,1,0:T(8,128)S(1)}, u32[]{:S(2)}, u32[]{:S(2)}) collective-permute-start(f32[12,2,8,128]{3,2,1,0:T(8,128)S(1)} %get-tuple-element.108), channel_id=1, source_target_pairs={{0,6},{1,7},{2,4},{3,5},{4,2},{5,3},{6,0},{7,1},{8,14},{9,15},{10,... | collective-permute-start | bytes 294920 | tf_op jit(solution)/shard_map/ppermute | solution.py:28
  34.1 20.0 %collective-permute-start.5 = (f32[12,128,128]{2,1,0:T(8,128)S(1)}, f32[12,128,128]{2,1,0:T(8,128)S(1)}, u32[]{:S(2)}, u32[]{:S(2)}) collective-permute-start(f32[12,128,128]{2,1,0:T(8,128)S(1)} %get-tuple-element.115), channel_id=1, source_target_pairs={{0,4},{1,5},{2,6},{3,7},{4,0},{5,1},{6,2},{7,3},{8,12},{9,13},{10,... | collective-permute-start | bytes 2359304 | tf_op jit(solution)/shard_map/ppermute | solution.py:28
  35.6 25.1 %collective-permute-start.6 = (f32[12,136,128]{2,1,0:T(8,128)S(1)}, f32[12,136,128]{2,1,0:T(8,128)S(1)}, u32[]{:S(2)}, u32[]{:S(2)}) collective-permute-start(f32[12,136,128]{2,1,0:T(8,128)S(1)} %get-tuple-element.117), channel_id=1, source_target_pairs={{0,8},{1,9},{2,10},{3,11},{4,12},{5,13},{6,14},{7,15},{8,0},{9,1},... | collective-permute-start | bytes 2506760 | tf_op jit(solution)/shard_map/ppermute | solution.py:28
  37.2 23.6 %collective-permute-start.7 = (f32[12,136,128]{2,1,0:T(8,128)S(1)}, f32[12,136,128]{2,1,0:T(8,128)S(1)}, u32[]{:S(2)}, u32[]{:S(2)}) collective-permute-start(f32[12,136,128]{2,1,0:T(8,128)S(1)} %get-tuple-element.118), channel_id=1, source_target_pairs={{8,16},{9,17},{10,18},{11,19},{12,20},{13,21},{14,22},{15,23},{16,... | collective-permute-start | bytes 2506760 | tf_op jit(solution)/shard_map/ppermute | solution.py:28
  56.0 22.2 %collective-permute-start.10 = (f32[12,136,128]{2,1,0:T(8,128)}, f32[12,136,128]{2,1,0:T(8,128)S(1)}, u32[]{:S(2)}, u32[]{:S(2)}) collective-permute-start(f32[12,136,128]{2,1,0:T(8,128)} %get-tuple-element.123), channel_id=1, source_target_pairs={{0,8},{1,9},{2,10},{3,11},{4,12},{5,13},{6,14},{7,15},{8,0},{9,1},... | collective-permute-start | bytes 2506760 | tf_op jit(solution)/shard_map/ppermute | solution.py:28
  57.6 20.6 %collective-permute-start.11 = (f32[12,136,128]{2,1,0:T(8,128)}, f32[12,136,128]{2,1,0:T(8,128)}, u32[]{:S(2)}, u32[]{:S(2)}) collective-permute-start(f32[12,136,128]{2,1,0:T(8,128)} %get-tuple-element.124), channel_id=1, source_target_pairs={{8,16},{9,17},{10,18},{11,19},{12,20},{13,21},{14,22},{15,23},{16,... | collective-permute-start | bytes 2506760 | tf_op jit(solution)/shard_map/ppermute | solution.py:28
  59.3 18.9 %collective-permute-start.12 = (f32[6,2,128,128]{3,2,1,0:T(8,128)S(1)}, f32[6,2,128,128]{3,2,1,0:T(8,128)}, u32[]{:S(2)}, u32[]{:S(2)}) collective-permute-start(f32[6,2,128,128]{3,2,1,0:T(8,128)S(1)} %get-tuple-element.125), channel_id=1, source_target_pairs={{0,4},{1,5},{2,6},{3,7},{4,0},{5,1},{6,2},{7,3},{8,12},{9,13},{10,... | collective-permute-start | bytes 2359304 | tf_op jit(solution)/shard_map/ppermute | solution.py:28
  81.5 17.6 %collective-permute-start.14 = (f32[12,2,8,128]{3,2,1,0:T(8,128)S(1)}, f32[12,2,8,128]{3,2,1,0:T(8,128)S(1)}, u32[]{:S(2)}, u32[]{:S(2)}) collective-permute-start(f32[12,2,8,128]{3,2,1,0:T(8,128)S(1)} %get-tuple-element.130), channel_id=1, source_target_pairs={{0,2},{1,3},{2,0},{3,1},{4,6},{5,7},{6,4},{7,5},{8,10},{9,11},{10,... | collective-permute-start | bytes 294920 | tf_op jit(solution)/shard_map/ppermute | solution.py:28
  82.0 17.1 %collective-permute-start.15 = (f32[12,2,8,128]{3,2,1,0:T(8,128)S(1)}, f32[12,2,8,128]{3,2,1,0:T(8,128)S(1)}, u32[]{:S(2)}, u32[]{:S(2)}) collective-permute-start(f32[12,2,8,128]{3,2,1,0:T(8,128)S(1)} %get-tuple-element.131), channel_id=1, source_target_pairs={{0,6},{1,7},{2,4},{3,5},{4,2},{5,3},{6,0},{7,1},{8,14},{9,15},{10,... | collective-permute-start | bytes 294920 | tf_op jit(solution)/shard_map/ppermute | solution.py:28
  84.5 18.7 %collective-permute-start.16 = (f32[8,128]{1,0:T(8,128)S(1)}, f32[8,128]{1,0:T(8,128)S(1)}, u32[]{:S(2)}, u32[]{:S(2)}) collective-permute-start(f32[8,128]{1,0:T(8,128)S(1)} %concatenate.40), channel_id=1, source_target_pairs={{0,16},{1,17},{2,18},{3,19},{4,20},{5,21},{6,22},{7,23},{8,24},{9,... | collective-permute-start | bytes 12296 | tf_op jit(solution)/shard_map/ppermute | solution.py:28
  86.1 19.5 %collective-permute-start.8 = (f32[6,2,128,128]{3,2,1,0:T(8,128)S(1)}, f32[6,2,128,128]{3,2,1,0:T(8,128)S(1)}, u32[]{:S(2)}, u32[]{:S(2)}) collective-permute-start(f32[6,2,128,128]{3,2,1,0:T(8,128)S(1)} %get-tuple-element.121), channel_id=1, source_target_pairs={{0,4},{1,5},{2,6},{3,7},{4,0},{5,1},{6,2},{7,3},{8,12},{9,13},{10,... | collective-permute-start | bytes 2359304 | tf_op jit(solution)/shard_map/ppermute | solution.py:28
  102.3 18.3 %collective-permute-start.18 = (f32[6,136,128]{2,1,0:T(8,128)S(1)}, f32[6,136,128]{2,1,0:T(8,128)S(1)}, u32[]{:S(2)}, u32[]{:S(2)}) collective-permute-start(f32[6,136,128]{2,1,0:T(8,128)S(1)} %get-tuple-element.139), channel_id=1, source_target_pairs={{8,16},{9,17},{10,18},{11,19},{12,20},{13,21},{14,22},{15,23},{16,... | collective-permute-start | bytes 1253384 | tf_op jit(solution)/shard_map/ppermute | solution.py:28
  103.3 18.8 %collective-permute-start.17 = (f32[6,136,128]{2,1,0:T(8,128)S(1)}, f32[6,136,128]{2,1,0:T(8,128)S(1)}, u32[]{:S(2)}, u32[]{:S(2)}) collective-permute-start(f32[6,136,128]{2,1,0:T(8,128)S(1)} %get-tuple-element.138), channel_id=1, source_target_pairs={{0,8},{1,9},{2,10},{3,11},{4,12},{5,13},{6,14},{7,15},{8,0},{9,1},... | collective-permute-start | bytes 1253384 | tf_op jit(solution)/shard_map/ppermute | solution.py:28
  108.4 22.5 %collective-permute-start.20 = (f32[6,136,128]{2,1,0:T(8,128)}, f32[6,136,128]{2,1,0:T(8,128)S(1)}, u32[]{:S(2)}, u32[]{:S(2)}) collective-permute-start(f32[6,136,128]{2,1,0:T(8,128)} %get-tuple-element.147), channel_id=1, source_target_pairs={{8,16},{9,17},{10,18},{11,19},{12,20},{13,21},{14,22},{15,23},{16,... | collective-permute-start | bytes 1253384 | tf_op jit(solution)/shard_map/ppermute | solution.py:28
  109.1 21.8 %collective-permute-start.19 = (f32[6,136,128]{2,1,0:T(8,128)}, f32[6,136,128]{2,1,0:T(8,128)}, u32[]{:S(2)}, u32[]{:S(2)}) collective-permute-start(f32[6,136,128]{2,1,0:T(8,128)} %get-tuple-element.146), channel_id=1, source_target_pairs={{0,8},{1,9},{2,10},{3,11},{4,12},{5,13},{6,14},{7,15},{8,0},{9,1},... | collective-permute-start | bytes 1253384 | tf_op jit(solution)/shard_map/ppermute | solution.py:28
  142.4 18.9 %collective-permute-start.26 = (f32[6,136,128]{2,1,0:T(8,128)S(1)}, f32[6,136,128]{2,1,0:T(8,128)S(1)}, u32[]{:S(2)}, u32[]{:S(2)}) collective-permute-start(f32[6,136,128]{2,1,0:T(8,128)S(1)} %get-tuple-element.153), channel_id=1, source_target_pairs={{8,16},{9,17},{10,18},{11,19},{12,20},{13,21},{14,22},{15,23},{16,... | collective-permute-start | bytes 1253384 | tf_op jit(solution)/shard_map/ppermute | solution.py:28
  143.3 18.1 %collective-permute-start.25 = (f32[6,136,128]{2,1,0:T(8,128)S(1)}, f32[6,136,128]{2,1,0:T(8,128)S(1)}, u32[]{:S(2)}, u32[]{:S(2)}) collective-permute-start(f32[6,136,128]{2,1,0:T(8,128)S(1)} %get-tuple-element.152), channel_id=1, source_target_pairs={{0,8},{1,9},{2,10},{3,11},{4,12},{5,13},{6,14},{7,15},{8,0},{9,1},... | collective-permute-start | bytes 1253384 | tf_op jit(solution)/shard_map/ppermute | solution.py:28
  158.0 20.3 %collective-permute-start.33 = (f32[6,136,128]{2,1,0:T(8,128)S(1)}, f32[6,136,128]{2,1,0:T(8,128)S(1)}, u32[]{:S(2)}, u32[]{:S(2)}) collective-permute-start(f32[6,136,128]{2,1,0:T(8,128)S(1)} %get-tuple-element.164), channel_id=1, source_target_pairs={{0,8},{1,9},{2,10},{3,11},{4,12},{5,13},{6,14},{7,15},{8,0},{9,1},... | collective-permute-start | bytes 1253384 | tf_op jit(solution)/shard_map/ppermute | solution.py:28
  159.1 19.9 %collective-permute-start.34 = (f32[6,136,128]{2,1,0:T(8,128)S(1)}, f32[6,136,128]{2,1,0:T(8,128)S(1)}, u32[]{:S(2)}, u32[]{:S(2)}) collective-permute-start(f32[6,136,128]{2,1,0:T(8,128)S(1)} %get-tuple-element.165), channel_id=1, source_target_pairs={{8,16},{9,17},{10,18},{11,19},{12,20},{13,21},{14,22},{15,23},{16,... | collective-permute-start | bytes 1253384 | tf_op jit(solution)/shard_map/ppermute | solution.py:28
  159.8 44.2 %collective-permute-start.30 = (f32[6,2,128,128]{3,2,1,0:T(8,128)}, f32[6,2,128,128]{3,2,1,0:T(8,128)}, u32[]{:S(2)}, u32[]{:S(2)}) collective-permute-start(f32[6,2,128,128]{3,2,1,0:T(8,128)} %get-tuple-element.159), channel_id=1, source_target_pairs={{0,4},{1,5},{2,6},{3,7},{4,0},{5,1},{6,2},{7,3},{8,12},{9,13},{10,... | collective-permute-start | bytes 2359304 | tf_op jit(solution)/shard_map/ppermute | solution.py:28
  174.1 30.0 %collective-permute-start.28 = (f32[6,2,128,128]{3,2,1,0:T(8,128)}, f32[6,2,128,128]{3,2,1,0:T(8,128)S(1)}, u32[]{:S(2)}, u32[]{:S(2)}) collective-permute-start(f32[6,2,128,128]{3,2,1,0:T(8,128)} %get-tuple-element.157), channel_id=1, source_target_pairs={{0,4},{1,5},{2,6},{3,7},{4,0},{5,1},{6,2},{7,3},{8,12},{9,13},{10,... | collective-permute-start | bytes 2359304 | tf_op jit(solution)/shard_map/ppermute | solution.py:28
  249.9 19.5 %collective-permute-start.40 = (f32[2,6,2,64,128]{4,3,2,1,0:T(8,128)S(1)}, f32[2,6,2,64,128]{4,3,2,1,0:T(8,128)S(1)}, u32[]{:S(2)}, u32[]{:S(2)}) collective-permute-start(f32[2,6,2,64,128]{4,3,2,1,0:T(8,128)S(1)} %grad_halves.2), channel_id=1, source_target_pairs={{0,1},{1,0},{2,3},{3,2},{4,5},{5,4},{6,7},{7,6},{8,9},{9,8},{10,11... | collective-permute-start | bytes 2359304 | tf_op jit(solution)/shard_map/ppermute | solution.py:28
  250.9 20.9 %collective-permute-start.47 = (f32[6,2,128,128]{3,2,1,0:T(8,128)S(1)}, f32[6,2,128,128]{3,2,1,0:T(8,128)S(1)}, u32[]{:S(2)}, u32[]{:S(2)}) collective-permute-start(f32[6,2,128,128]{3,2,1,0:T(8,128)S(1)} %get-tuple-element.186), channel_id=1, source_target_pairs={{0,4},{1,5},{2,6},{3,7},{4,0},{5,1},{6,2},{7,3},{8,12},{9,13},{10,... | collective-permute-start | bytes 2359304 | tf_op jit(solution)/shard_map/ppermute | solution.py:28
  (60 other events, 603.2 us)

commit v4 on v3

--- a/solution.py
+++ b/solution.py
@@ -656,7 +656,7 @@
         scalars,
         [Stream(z2), Stream(g_rows)]
         + [Stream(a, first, part) for a in (z1,) + x_parts]
-        + [*halos, *g_halos, coef, weight],
+        + [*halos, *[Stream(a) for a in g_halos], coef, weight],
         [Result(part, 4, wide, chans), Result(part, 4, own, chans)]
         + [(part, wide, chans), (part, wide, chans), (8, chans), (part, 2, own, chans), (part, 2, own, chans)],
         conv_scratch(wide, chans) + [pltpu.VMEM((3, 8, chans), F32), pltpu.VMEM((4, STEP, own, chans), F32)],
@@ -708,7 +708,7 @@
         scalars,
         [Stream(dh)]
         + [Stream(a, chunk * part, part) for a in (z1,) + z_halos]
-        + [Stream(g_rows), *halos, coef, weight],
+        + [Stream(g_rows), *[Stream(a) for a in halos], coef, weight],
         [(part, 2, own, chans)] * 2,
         conv_scratch(wide, chans) + [pltpu.VMEM((4, STEP, own, chans), F32)],
         "conv_four",
@@ -933,7 +933,7 @@
     edge = permute(edge, to_side)
     tiles = permute(tiles, to_east)
     foreign_tiles = permute(other_tiles, to_east_side)
-    inner = permute(after(inner, tiles), to_side)
+    inner = permute(after(inner, foreign_tiles), to_side)
     x_edge, pair_row, next_row = join(scalars, home, edge, tiles, foreign_tiles, True, "x_edge")
     x_halos = exchange_rows(pair_row, next_row)
     slopes = after(slopes, x_edge)

time: 279 us -> 274 us (0.982)
  local copies, waits for them, and re-layouts: 7.06 us -> 3.55 us
    unnamed x62 -> x54, local copies, waits for them, and re-layouts: 6.71 us -> 3.19 us
where the time goes in v4:
time: 274 us; the launch traced here: 273 us
  Pallas kernels  139 us (51%)
  starting transfers between devices  67 us (24%)
  waiting for transfers between devices  60.2 us (22%)
  local copies, waits for them, and re-layouts  3.55 us (1%)
    pallas_call x22, Pallas kernels, call(): pl.pallas_call(kernel, in_specs=[SMEM] + [HBM if isinstance(a, Stream) el...  123 us
    ppermute x53, starting transfers between devices, permute(): return lax.ppermute(value, AXES, pairs)  67 us
    ppermute x53, waiting for transfers between devices, permute(): return lax.ppermute(value, AXES, pairs)  60.2 us
    pallas_call x4, Pallas kernels, place(): pl.pallas_call(functools.partial(place_kernel, chunk), in_specs=[SMEM] +...  8.06 us
    pallas_call x4, Pallas kernels, pack(): pl.pallas_call(functools.partial(pack_kernel, other_core), in_specs=[SMEM...  7.87 us
  transfers between devices with their start and end apart: 53, of which 14 were waited for; matrix products, arithmetic and copies ran while one was open for 1% of the time, Pallas kernels for 44%

profile of v4, /device:TPU:0, one launch (start us, length us, event | category | flops | bytes accessed | tf_op | source)
XLA Modules:
  0.0 273.4 jit_solution(3095953304404801794)
XLA Ops:
  7.1 2.9 %collective-permute-start.1 = (f32[12,128,128]{2,1,0:T(8,128)S(1)}, f32[12,128,128]{2,1,0:T(8,128)S(1)}, u32[]{:S(2)}, u32[]{:S(2)}) collective-permute-start(f32[12,128,128]{2,1,0:T(8,128)S(1)} %get-tuple-element.106), channel_id=1, source_target_pairs={{0,4},{1,5},{2,6},{3,7},{4,0},{5,1},{6,2},{7,3},{8,12},{9,13},{10,... | collective-permute-start | bytes 2359304 | tf_op jit(solution)/shard_map/ppermute | solution.py:28
  11.6 3.1 %collective-permute-done.2.refs_2_ = f32[12,2,8,128]{3,2,1,0:T(8,128)S(1)} collective-permute-done((f32[12,2,8,128]{3,2,1,0:T(8,128)S(1)}, f32[12,2,8,128]{3,2,1,0:T(8,128)S(1)}, u32[]{:S(2)}, u32[]{:S(2)}) %collective-permute-start.2) | collective-permute-done | bytes 98336 | tf_op jit(solution)/shard_map/ppermute | solution.py:28
  14.7 16.5 %collective-permute-done.3.refs_3_ = f32[12,2,8,128]{3,2,1,0:T(8,128)S(1)} collective-permute-done((f32[12,2,8,128]{3,2,1,0:T(8,128)S(1)}, f32[12,2,8,128]{3,2,1,0:T(8,128)S(1)}, u32[]{:S(2)}, u32[]{:S(2)}) %collective-permute-start.3) | collective-permute-done | bytes 98336 | tf_op jit(solution)/shard_map/ppermute | solution.py:28
  41.9 12.2 %collective-permute-done.5.refs_1_ = f32[12,128,128]{2,1,0:T(8,128)S(1)} collective-permute-done((f32[12,128,128]{2,1,0:T(8,128)S(1)}, f32[12,128,128]{2,1,0:T(8,128)S(1)}, u32[]{:S(2)}, u32[]{:S(2)}) %collective-permute-start.5) | collective-permute-done | bytes 786464 | tf_op jit(solution)/shard_map/ppermute | solution.py:28
  60.8 11.8 %conv_one.1 = (f32[12,4,136,128]{3,2,1,0:T(8,128)}, f32[8,128]{1,0:T(8,128)S(1)}) custom-call(s32[6]{0:T(128)S(1)} %stack.35.s_ref, f32[12,2,136,128]{3,2,1,0:T(8,128)S(1)} %get-tuple-element.127.refs_0_.refs_3_.refs_6_, f32[12,2,136,128]{3,2,1,0:T(8,128)S(1)} %get-tuple-element.116.refs_1_.refs_4_.refs_7_, ...), custom_call_target="tpu_custom_call" | custom-call | tf_op jit(solution)/shard_map/conv_one/pallas_call | solution.py:173
  73.2 3.1 %collective-permute-done.9 = f32[8,128]{1,0:T(8,128)S(1)} collective-permute-done((f32[8,128]{1,0:T(8,128)S(1)}, f32[8,128]{1,0:T(8,128)S(1)}, u32[]{:S(2)}, u32[]{:S(2)}) %collective-permute-start.9) | collective-permute-done | bytes 4128 | tf_op jit(solution)/shard_map/ppermute | solution.py:28
  78.2 3.3 %collective-permute-start.13 = (f32[8,128]{1,0:T(8,128)S(1)}, f32[8,128]{1,0:T(8,128)S(1)}, u32[]{:S(2)}, u32[]{:S(2)}) collective-permute-start(f32[8,128]{1,0:T(8,128)S(1)} %concatenate.39), channel_id=1, source_target_pairs={{0,8},{1,9},{2,10},{3,11},{4,12},{5,13},{6,14},{7,15},{8,0},{9,1},... | collective-permute-start | bytes 12296 | tf_op jit(solution)/shard_map/ppermute | solution.py:28
  88.7 10.4 %conv_one_halo.1 = (f32[12,136,128]{2,1,0:T(8,128)S(1)}, f32[12,136,128]{2,1,0:T(8,128)S(1)}) custom-call(s32[6]{0:T(128)S(1)} %stack.35.s_ref, f32[12,2,136,128]{3,2,1,0:T(8,128)} %copy-done, f32[12,136,128]{2,1,0:T(8,128)} %copy-done.4, f32[12,136,128]{2,1,0:T(8,128)} %copy-done.5, f32[12,136,128]{2,1,0:T(8,128)} %copy-done.16, ...), custom_call_target="tpu_custom_call" | custom-call | tf_op jit(solution)/shard_map/conv_one_halo/pallas_call | solution.py:173
  99.2 3.1 %g_cell.3 = (f32[6,4,136,128]{3,2,1,0:T(8,128)}, f32[6,136,128]{2,1,0:T(8,128)S(1)}, f32[6,136,128]{2,1,0:T(8,128)S(1)}) custom-call(s32[6]{0:T(128)S(1)} %stack.35.s_ref, f32[12,2,128,128]{3,2,1,0:T(8,128)S(1)} %copy-done.11, f32[6,2,128,128]{3,2,1,0:T(8,128)} %collective-permute-done.12.refs_1_, f32[12,2,8,128]{3,2,1,0:T(8,128)S(1)} %collective-permute-done.14.refs_2_, ...), custom_call_target="tpu_custom_call" | custom-call | tf_op jit(solution)/shard_map/g_cell/pallas_call | solution.py:173
  111.8 8.7 %conv_two.2 = (f32[6,4,136,128]{3,2,1,0:T(8,128)}, f32[6,136,128]{2,1,0:T(8,128)S(1)}, f32[6,136,128]{2,1,0:T(8,128)S(1)}, f32[8,128]{1,0:T(8,128)S(1)}) custom-call(s32[6]{0:T(128)S(1)} %stack.35.s_ref, f32[12,4,136,128]{3,2,1,0:T(8,128)} %get-tuple-element.120.refs_0_.refs_2_.refs_4_.refs_1_.refs_10_, ...), custom_call_target="tpu_custom_call" | custom-call | tf_op jit(solution)/shard_map/conv_two/pallas_call | solution.py:173
  121.4 8.7 %conv_two.3 = (f32[6,4,136,128]{3,2,1,0:T(8,128)}, f32[6,136,128]{2,1,0:T(8,128)S(1)}, f32[6,136,128]{2,1,0:T(8,128)S(1)}, f32[8,128]{1,0:T(8,128)S(1)}) custom-call(s32[6]{0:T(128)S(1)} %stack.35.s_ref, f32[12,4,136,128]{3,2,1,0:T(8,128)} %get-tuple-element.120.refs_0_.refs_2_.refs_4_.refs_1_.refs_10_, ...), custom_call_target="tpu_custom_call" | custom-call | tf_op jit(solution)/shard_map/conv_two/pallas_call | solution.py:173
  130.8 3.1 %collective-permute-done.21 = f32[8,128]{1,0:T(8,128)S(1)} collective-permute-done((f32[8,128]{1,0:T(8,128)S(1)}, f32[8,128]{1,0:T(8,128)S(1)}, u32[]{:S(2)}, u32[]{:S(2)}) %collective-permute-start.21) | collective-permute-done | bytes 4128 | tf_op jit(solution)/shard_map/ppermute | solution.py:28
  134.0 3.9 %collective-permute-start.24 = (f32[8,128]{1,0:T(8,128)S(1)}, f32[8,128]{1,0:T(8,128)S(1)}, u32[]{:S(2)}, u32[]{:S(2)}) collective-permute-start(f32[8,128]{1,0:T(8,128)S(1)} %concatenate.44), channel_id=1, source_target_pairs={{0,8},{1,9},{2,10},{3,11},{4,12},{5,13},{6,14},{7,15},{8,0},{9,1},... | collective-permute-start | bytes 12296 | tf_op jit(solution)/shard_map/ppermute | solution.py:28
  139.5 2.9 %collective-permute-start.27 = (f32[8,128]{1,0:T(8,128)S(1)}, f32[8,128]{1,0:T(8,128)S(1)}, u32[]{:S(2)}, u32[]{:S(2)}) collective-permute-start(f32[8,128]{1,0:T(8,128)S(1)} %concatenate.45), channel_id=1, source_target_pairs={{0,16},{1,17},{2,18},{3,19},{4,20},{5,21},{6,22},{7,23},{8,24},{9,... | collective-permute-start | bytes 12296 | tf_op jit(solution)/shard_map/ppermute | solution.py:28
  145.3 11.2 %conv_three.2 = (f32[6,4,136,128]{3,2,1,0:T(8,128)}, f32[6,4,128,128]{3,2,1,0:T(8,128)}, f32[6,136,128]{2,1,0:T(8,128)S(1)}, f32[6,136,128]{2,1,0:T(8,128)S(1)},...) custom-call(s32[6]{0:T(128)S(1)} %stack.35.s_ref, ...), custom_call_target="tpu_custom_call" | custom-call | tf_op jit(solution)/shard_map/conv_three/pallas_call | solution.py:173
  159.9 11.4 %conv_three.3 = (f32[6,4,136,128]{3,2,1,0:T(8,128)}, f32[6,4,128,128]{3,2,1,0:T(8,128)}, f32[6,136,128]{2,1,0:T(8,128)S(1)}, f32[6,136,128]{2,1,0:T(8,128)}, f32...) custom-call(s32[6]{0:T(128)S(1)} %stack.35.s_ref, ...), custom_call_target="tpu_custom_call" | custom-call | tf_op jit(solution)/shard_map/conv_three/pallas_call | solution.py:173
  172.4 3.1 %collective-permute-done.32 = f32[8,128]{1,0:T(8,128)S(1)} collective-permute-done((f32[8,128]{1,0:T(8,128)S(1)}, f32[8,128]{1,0:T(8,128)S(1)}, u32[]{:S(2)}, u32[]{:S(2)}) %collective-permute-start.32) | collective-permute-done | bytes 4128 | tf_op jit(solution)/shard_map/ppermute | solution.py:28
  175.6 3.7 %collective-permute-start.35 = (f32[8,128]{1,0:T(8,128)S(1)}, f32[8,128]{1,0:T(8,128)S(1)}, u32[]{:S(2)}, u32[]{:S(2)}) collective-permute-start(f32[8,128]{1,0:T(8,128)S(1)} %add.358), channel_id=1, source_target_pairs={{0,8},{1,9},{2,10},{3,11},{4,12},{5,13},{6,14},{7,15},{8,0},{9,1},... | collective-permute-start | bytes 12296 | tf_op jit(solution)/shard_map/ppermute | solution.py:28
  186.6 13.3 %weight_two.1 = f32[1184,128]{1,0:T(8,128)S(1)} custom-call(s32[6]{0:T(128)S(1)} %stack.35.s_ref, f32[12,4,136,128]{3,2,1,0:T(8,128)} %get-tuple-element.120.refs_0_.refs_2_.refs_4_.refs_1_.refs_10_, f32[12,136,128]{2,1,0:T(8,128)} %copy-done.2, f32[12,136,128]{2,1,0:T(8,128)} %copy-done.3, f32[6,4,128,128]{3,2,1,0:T(8,128)} %get-tuple-element.169.refs_3_, ...), custom_call_target="tpu_custom_call" | custom-call | tf_op jit(solution)/shard_map/weight_two/pallas_call | solution.py:173
  199.9 9.6 %conv_four.2 = (f32[6,2,128,128]{3,2,1,0:T(8,128)S(1)}, f32[6,2,128,128]{3,2,1,0:T(8,128)}) custom-call(s32[6]{0:T(128)S(1)} %stack.35.s_ref, f32[6,4,136,128]{3,2,1,0:T(8,128)} %get-tuple-element.154.refs_0_.refs_5_, f32[12,4,136,128]{3,2,1,0:T(8,128)} %get-tuple-element.120.refs_0_.refs_2_.refs_4_.refs_1_.refs_10_, f32[12,136,128]{2,1,0:T(8,128)} %copy-done.2, ...), custom_call_target="tpu_custom_call" | custom-call | tf_op jit(solution)/shard_map/conv_four/pallas_call | solution.py:173
  211.9 13.9 %weight_one.1 = f32[1184,128]{1,0:T(8,128)S(1)} custom-call(s32[6]{0:T(128)S(1)} %stack.35.s_ref, f32[12,2,136,128]{3,2,1,0:T(8,128)} %copy-done, f32[12,2,136,128]{3,2,1,0:T(8,128)} %copy-done.1, f32[12,136,128]{2,1,0:T(8,128)} %copy-done.4, f32[12,136,128]{2,1,0:T(8,128)} %copy-done.5, ...), custom_call_target="tpu_custom_call" | custom-call | tf_op jit(solution)/shard_map/weight_one/pallas_call | solution.py:173
  232.3 8.7 %conv_four.3 = (f32[6,2,128,128]{3,2,1,0:T(8,128)S(1)}, f32[6,2,128,128]{3,2,1,0:T(8,128)S(1)}) custom-call(s32[6]{0:T(128)S(1)} %stack.35.s_ref, f32[6,4,136,128]{3,2,1,0:T(8,128)} %get-tuple-element.160.refs_11_.refs_0_, f32[12,4,136,128]{3,2,1,0:T(8,128)} %get-tuple-element.120.refs_0_.refs_2_.refs_4_.refs_1_.refs_10_, f32[12,136,128]{2,1,0:T(8,128)} %copy-done.2, ...), custom_call_target="tpu_custom_call" | custom-call | tf_op jit(solution)/shard_map/conv_four/pallas_call | solution.py:173
  248.1 9.0 %collective-permute-done.46 = f32[296,128]{1,0:T(8,128)S(1)} collective-permute-done((f32[296,128]{1,0:T(8,128)S(1)}, f32[296,128]{1,0:T(8,128)S(1)}, u32[]{:S(2)}, u32[]{:S(2)}) %collective-permute-start.46) | collective-permute-done | bytes 151584 | tf_op jit(solution)/shard_map/ppermute | solution.py:28
  257.8 3.0 %collective-permute-start.50 = (f32[296,128]{1,0:T(8,128)S(1)}, f32[296,128]{1,0:T(8,128)S(1)}, u32[]{:S(2)}, u32[]{:S(2)}) collective-permute-start(f32[296,128]{1,0:T(8,128)S(1)} %add.366.refs_0_), channel_id=1, source_target_pairs={{0,10},{1,11},{2,8},{3,9},{4,14},{5,15},{6,12},{7,13},{8,2},{9,3},... | collective-permute-start | bytes 454664 | tf_op jit(solution)/shard_map/ppermute | solution.py:28
  (206 shorter events, 91.0 us)
Async XLA Ops:
  7.1 24.1 %collective-permute-start.1 = (f32[12,128,128]{2,1,0:T(8,128)S(1)}, f32[12,128,128]{2,1,0:T(8,128)S(1)}, u32[]{:S(2)}, u32[]{:S(2)}) collective-permute-start(f32[12,128,128]{2,1,0:T(8,128)S(1)} %get-tuple-element.106), channel_id=1, source_target_pairs={{0,4},{1,5},{2,6},{3,7},{4,0},{5,1},{6,2},{7,3},{8,12},{9,13},{10,... | collective-permute-start | bytes 2359304 | tf_op jit(solution)/shard_map/ppermute | solution.py:28
  11.6 19.6 %collective-permute-start.3 = (f32[12,2,8,128]{3,2,1,0:T(8,128)S(1)}, f32[12,2,8,128]{3,2,1,0:T(8,128)S(1)}, u32[]{:S(2)}, u32[]{:S(2)}) collective-permute-start(f32[12,2,8,128]{3,2,1,0:T(8,128)S(1)} %get-tuple-element.108), channel_id=1, source_target_pairs={{0,6},{1,7},{2,4},{3,5},{4,2},{5,3},{6,0},{7,1},{8,14},{9,15},{10,... | collective-permute-start | bytes 294920 | tf_op jit(solution)/shard_map/ppermute | solution.py:28
  34.1 20.0 %collective-permute-start.5 = (f32[12,128,128]{2,1,0:T(8,128)S(1)}, f32[12,128,128]{2,1,0:T(8,128)S(1)}, u32[]{:S(2)}, u32[]{:S(2)}) collective-permute-start(f32[12,128,128]{2,1,0:T(8,128)S(1)} %get-tuple-element.115), channel_id=1, source_target_pairs={{0,4},{1,5},{2,6},{3,7},{4,0},{5,1},{6,2},{7,3},{8,12},{9,13},{10,... | collective-permute-start | bytes 2359304 | tf_op jit(solution)/shard_map/ppermute | solution.py:28
  35.6 25.2 %collective-permute-start.6 = (f32[12,136,128]{2,1,0:T(8,128)S(1)}, f32[12,136,128]{2,1,0:T(8,128)S(1)}, u32[]{:S(2)}, u32[]{:S(2)}) collective-permute-start(f32[12,136,128]{2,1,0:T(8,128)S(1)} %get-tuple-element.117), channel_id=1, source_target_pairs={{0,8},{1,9},{2,10},{3,11},{4,12},{5,13},{6,14},{7,15},{8,0},{9,1},... | collective-permute-start | bytes 2506760 | tf_op jit(solution)/shard_map/ppermute | solution.py:28
  37.2 23.6 %collective-permute-start.7 = (f32[12,136,128]{2,1,0:T(8,128)S(1)}, f32[12,136,128]{2,1,0:T(8,128)S(1)}, u32[]{:S(2)}, u32[]{:S(2)}) collective-permute-start(f32[12,136,128]{2,1,0:T(8,128)S(1)} %get-tuple-element.118), channel_id=1, source_target_pairs={{8,16},{9,17},{10,18},{11,19},{12,20},{13,21},{14,22},{15,23},{16,... | collective-permute-start | bytes 2506760 | tf_op jit(solution)/shard_map/ppermute | solution.py:28
  56.0 22.2 %collective-permute-start.10 = (f32[12,136,128]{2,1,0:T(8,128)}, f32[12,136,128]{2,1,0:T(8,128)S(1)}, u32[]{:S(2)}, u32[]{:S(2)}) collective-permute-start(f32[12,136,128]{2,1,0:T(8,128)} %get-tuple-element.123), channel_id=1, source_target_pairs={{0,8},{1,9},{2,10},{3,11},{4,12},{5,13},{6,14},{7,15},{8,0},{9,1},... | collective-permute-start | bytes 2506760 | tf_op jit(solution)/shard_map/ppermute | solution.py:28
  57.7 20.6 %collective-permute-start.11 = (f32[12,136,128]{2,1,0:T(8,128)}, f32[12,136,128]{2,1,0:T(8,128)}, u32[]{:S(2)}, u32[]{:S(2)}) collective-permute-start(f32[12,136,128]{2,1,0:T(8,128)} %get-tuple-element.124), channel_id=1, source_target_pairs={{8,16},{9,17},{10,18},{11,19},{12,20},{13,21},{14,22},{15,23},{16,... | collective-permute-start | bytes 2506760 | tf_op jit(solution)/shard_map/ppermute | solution.py:28
  59.3 18.9 %collective-permute-start.12 = (f32[6,2,128,128]{3,2,1,0:T(8,128)S(1)}, f32[6,2,128,128]{3,2,1,0:T(8,128)}, u32[]{:S(2)}, u32[]{:S(2)}) collective-permute-start(f32[6,2,128,128]{3,2,1,0:T(8,128)S(1)} %get-tuple-element.125), channel_id=1, source_target_pairs={{0,4},{1,5},{2,6},{3,7},{4,0},{5,1},{6,2},{7,3},{8,12},{9,13},{10,... | collective-permute-start | bytes 2359304 | tf_op jit(solution)/shard_map/ppermute | solution.py:28
  81.5 17.6 %collective-permute-start.14 = (f32[12,2,8,128]{3,2,1,0:T(8,128)S(1)}, f32[12,2,8,128]{3,2,1,0:T(8,128)S(1)}, u32[]{:S(2)}, u32[]{:S(2)}) collective-permute-start(f32[12,2,8,128]{3,2,1,0:T(8,128)S(1)} %get-tuple-element.130), channel_id=1, source_target_pairs={{0,2},{1,3},{2,0},{3,1},{4,6},{5,7},{6,4},{7,5},{8,10},{9,11},{10,... | collective-permute-start | bytes 294920 | tf_op jit(solution)/shard_map/ppermute | solution.py:28
  82.0 17.1 %collective-permute-start.15 = (f32[12,2,8,128]{3,2,1,0:T(8,128)S(1)}, f32[12,2,8,128]{3,2,1,0:T(8,128)S(1)}, u32[]{:S(2)}, u32[]{:S(2)}) collective-permute-start(f32[12,2,8,128]{3,2,1,0:T(8,128)S(1)} %get-tuple-element.131), channel_id=1, source_target_pairs={{0,6},{1,7},{2,4},{3,5},{4,2},{5,3},{6,0},{7,1},{8,14},{9,15},{10,... | collective-permute-start | bytes 294920 | tf_op jit(solution)/shard_map/ppermute | solution.py:28
  84.5 18.6 %collective-permute-start.16 = (f32[8,128]{1,0:T(8,128)S(1)}, f32[8,128]{1,0:T(8,128)S(1)}, u32[]{:S(2)}, u32[]{:S(2)}) collective-permute-start(f32[8,128]{1,0:T(8,128)S(1)} %concatenate.40), channel_id=1, source_target_pairs={{0,16},{1,17},{2,18},{3,19},{4,20},{5,21},{6,22},{7,23},{8,24},{9,... | collective-permute-start | bytes 12296 | tf_op jit(solution)/shard_map/ppermute | solution.py:28
  86.1 19.5 %collective-permute-start.8 = (f32[6,2,128,128]{3,2,1,0:T(8,128)S(1)}, f32[6,2,128,128]{3,2,1,0:T(8,128)S(1)}, u32[]{:S(2)}, u32[]{:S(2)}) collective-permute-start(f32[6,2,128,128]{3,2,1,0:T(8,128)S(1)} %get-tuple-element.121), channel_id=1, source_target_pairs={{0,4},{1,5},{2,6},{3,7},{4,0},{5,1},{6,2},{7,3},{8,12},{9,13},{10,... | collective-permute-start | bytes 2359304 | tf_op jit(solution)/shard_map/ppermute | solution.py:28
  102.3 18.3 %collective-permute-start.18 = (f32[6,136,128]{2,1,0:T(8,128)S(1)}, f32[6,136,128]{2,1,0:T(8,128)S(1)}, u32[]{:S(2)}, u32[]{:S(2)}) collective-permute-start(f32[6,136,128]{2,1,0:T(8,128)S(1)} %get-tuple-element.139), channel_id=1, source_target_pairs={{8,16},{9,17},{10,18},{11,19},{12,20},{13,21},{14,22},{15,23},{16,... | collective-permute-start | bytes 1253384 | tf_op jit(solution)/shard_map/ppermute | solution.py:28
  103.3 18.1 %collective-permute-start.17 = (f32[6,136,128]{2,1,0:T(8,128)S(1)}, f32[6,136,128]{2,1,0:T(8,128)S(1)}, u32[]{:S(2)}, u32[]{:S(2)}) collective-permute-start(f32[6,136,128]{2,1,0:T(8,128)S(1)} %get-tuple-element.138), channel_id=1, source_target_pairs={{0,8},{1,9},{2,10},{3,11},{4,12},{5,13},{6,14},{7,15},{8,0},{9,1},... | collective-permute-start | bytes 1253384 | tf_op jit(solution)/shard_map/ppermute | solution.py:28
  108.4 21.8 %collective-permute-start.20 = (f32[6,136,128]{2,1,0:T(8,128)}, f32[6,136,128]{2,1,0:T(8,128)}, u32[]{:S(2)}, u32[]{:S(2)}) collective-permute-start(f32[6,136,128]{2,1,0:T(8,128)} %get-tuple-element.147), channel_id=1, source_target_pairs={{8,16},{9,17},{10,18},{11,19},{12,20},{13,21},{14,22},{15,23},{16,... | collective-permute-start | bytes 1253384 | tf_op jit(solution)/shard_map/ppermute | solution.py:28
  109.9 20.4 %collective-permute-start.19 = (f32[6,136,128]{2,1,0:T(8,128)}, f32[6,136,128]{2,1,0:T(8,128)}, u32[]{:S(2)}, u32[]{:S(2)}) collective-permute-start(f32[6,136,128]{2,1,0:T(8,128)} %get-tuple-element.146), channel_id=1, source_target_pairs={{0,8},{1,9},{2,10},{3,11},{4,12},{5,13},{6,14},{7,15},{8,0},{9,1},... | collective-permute-start | bytes 1253384 | tf_op jit(solution)/shard_map/ppermute | solution.py:28
  142.4 17.5 %collective-permute-start.26 = (f32[6,136,128]{2,1,0:T(8,128)S(1)}, f32[6,136,128]{2,1,0:T(8,128)S(1)}, u32[]{:S(2)}, u32[]{:S(2)}) collective-permute-start(f32[6,136,128]{2,1,0:T(8,128)S(1)} %get-tuple-element.153), channel_id=1, source_target_pairs={{8,16},{9,17},{10,18},{11,19},{12,20},{13,21},{14,22},{15,23},{16,... | collective-permute-start | bytes 1253384 | tf_op jit(solution)/shard_map/ppermute | solution.py:28
  156.6 19.0 %collective-permute-start.33 = (f32[6,136,128]{2,1,0:T(8,128)S(1)}, f32[6,136,128]{2,1,0:T(8,128)S(1)}, u32[]{:S(2)}, u32[]{:S(2)}) collective-permute-start(f32[6,136,128]{2,1,0:T(8,128)S(1)} %get-tuple-element.164), channel_id=1, source_target_pairs={{0,8},{1,9},{2,10},{3,11},{4,12},{5,13},{6,14},{7,15},{8,0},{9,1},... | collective-permute-start | bytes 1253384 | tf_op jit(solution)/shard_map/ppermute | solution.py:28
  157.6 17.9 %collective-permute-start.34 = (f32[6,136,128]{2,1,0:T(8,128)S(1)}, f32[6,136,128]{2,1,0:T(8,128)S(1)}, u32[]{:S(2)}, u32[]{:S(2)}) collective-permute-start(f32[6,136,128]{2,1,0:T(8,128)S(1)} %get-tuple-element.165), channel_id=1, source_target_pairs={{8,16},{9,17},{10,18},{11,19},{12,20},{13,21},{14,22},{15,23},{16,... | collective-permute-start | bytes 1253384 | tf_op jit(solution)/shard_map/ppermute | solution.py:28
  158.3 41.6 %collective-permute-start.30 = (f32[6,2,128,128]{3,2,1,0:T(8,128)}, f32[6,2,128,128]{3,2,1,0:T(8,128)}, u32[]{:S(2)}, u32[]{:S(2)}) collective-permute-start(f32[6,2,128,128]{3,2,1,0:T(8,128)} %get-tuple-element.159), channel_id=1, source_target_pairs={{0,4},{1,5},{2,6},{3,7},{4,0},{5,1},{6,2},{7,3},{8,12},{9,13},{10,... | collective-permute-start | bytes 2359304 | tf_op jit(solution)/shard_map/ppermute | solution.py:28
  171.3 28.6 %collective-permute-start.28 = (f32[6,2,128,128]{3,2,1,0:T(8,128)}, f32[6,2,128,128]{3,2,1,0:T(8,128)S(1)}, u32[]{:S(2)}, u32[]{:S(2)}) collective-permute-start(f32[6,2,128,128]{3,2,1,0:T(8,128)} %get-tuple-element.157), channel_id=1, source_target_pairs={{0,4},{1,5},{2,6},{3,7},{4,0},{5,1},{6,2},{7,3},{8,12},{9,13},{10,... | collective-permute-start | bytes 2359304 | tf_op jit(solution)/shard_map/ppermute | solution.py:28
  183.1 16.8 %collective-permute-start.37 = (f32[6,136,128]{2,1,0:T(8,128)}, f32[6,136,128]{2,1,0:T(8,128)}, u32[]{:S(2)}, u32[]{:S(2)}) collective-permute-start(f32[6,136,128]{2,1,0:T(8,128)} %get-tuple-element.168), channel_id=1, source_target_pairs={{8,16},{9,17},{10,18},{11,19},{12,20},{13,21},{14,22},{15,23},{16,... | collective-permute-start | bytes 1253384 | tf_op jit(solution)/shard_map/ppermute | solution.py:28
  245.3 19.5 %collective-permute-start.40 = (f32[2,6,2,64,128]{4,3,2,1,0:T(8,128)S(1)}, f32[2,6,2,64,128]{4,3,2,1,0:T(8,128)S(1)}, u32[]{:S(2)}, u32[]{:S(2)}) collective-permute-start(f32[2,6,2,64,128]{4,3,2,1,0:T(8,128)S(1)} %grad_halves.2), channel_id=1, source_target_pairs={{0,1},{1,0},{2,3},{3,2},{4,5},{5,4},{6,7},{7,6},{8,9},{9,8},{10,11... | collective-permute-start | bytes 2359304 | tf_op jit(solution)/shard_map/ppermute | solution.py:28
  246.3 20.9 %collective-permute-start.47 = (f32[6,2,128,128]{3,2,1,0:T(8,128)S(1)}, f32[6,2,128,128]{3,2,1,0:T(8,128)S(1)}, u32[]{:S(2)}, u32[]{:S(2)}) collective-permute-start(f32[6,2,128,128]{3,2,1,0:T(8,128)S(1)} %get-tuple-element.186), channel_id=1, source_target_pairs={{0,4},{1,5},{2,6},{3,7},{4,0},{5,1},{6,2},{7,3},{8,12},{9,13},{10,... | collective-permute-start | bytes 2359304 | tf_op jit(solution)/shard_map/ppermute | solution.py:28
  (56 other events, 572.9 us)

commit v5 on v4

--- a/solution.py
+++ b/solution.py
@@ -734,9 +734,9 @@
         at = slice(two * 6 * chans, (two * 6 + 12) * chans)
         slope = jnp.concatenate([s.reshape(-1, chans) for s in slopes[2 * two : 2 * two + 2]], axis=1)
         slope_high, slope_low = split(slope)
-        part = product(high[:, at], slope_high)
+        both = product(high[:, at], jnp.concatenate([slope_high, slope_low], axis=1))
+        part = both[:, : 2 * chans] + both[:, 2 * chans :]
         part += product(low[:, at], slope_high)
-        part += product(high[:, at], slope_low)
         sums = part if sums is None else sums + part
     total[...] += sums
 

time: 274 us -> 274 us (level)
  no operation moved by 1% of the time
where the time goes in v5:
time: 274 us; the launch traced here: 273 us
  Pallas kernels  138 us (50%)
  starting transfers between devices  67 us (24%)
  waiting for transfers between devices  60.2 us (22%)
  local copies, waits for them, and re-layouts  3.55 us (1%)
    pallas_call x22, Pallas kernels, call(): pl.pallas_call(kernel, in_specs=[SMEM] + [HBM if isinstance(a, Stream) el...  122 us
    ppermute x53, starting transfers between devices, permute(): return lax.ppermute(value, AXES, pairs)  67 us
    ppermute x53, waiting for transfers between devices, permute(): return lax.ppermute(value, AXES, pairs)  60.2 us
    pallas_call x4, Pallas kernels, place(): pl.pallas_call(functools.partial(place_kernel, chunk), in_specs=[SMEM] +...  8.06 us
    pallas_call x4, Pallas kernels, pack(): pl.pallas_call(functools.partial(pack_kernel, other_core), in_specs=[SMEM...  7.87 us
  transfers between devices with their start and end apart: 53, of which 14 were waited for; matrix products, arithmetic and copies ran while one was open for 1% of the time, Pallas kernels for 44%

profile of v5, /device:TPU:0, one launch (start us, length us, event | category | flops | bytes accessed | tf_op | source)
XLA Modules:
  0.0 272.8 jit_solution(13439352398845462756)
XLA Ops:
  7.1 2.9 %collective-permute-start.1 = (f32[12,128,128]{2,1,0:T(8,128)S(1)}, f32[12,128,128]{2,1,0:T(8,128)S(1)}, u32[]{:S(2)}, u32[]{:S(2)}) collective-permute-start(f32[12,128,128]{2,1,0:T(8,128)S(1)} %get-tuple-element.106), channel_id=1, source_target_pairs={{0,4},{1,5},{2,6},{3,7},{4,0},{5,1},{6,2},{7,3},{8,12},{9,13},{10,... | collective-permute-start | bytes 2359304 | tf_op jit(solution)/shard_map/ppermute | solution.py:28
  11.6 3.1 %collective-permute-done.2.refs_2_ = f32[12,2,8,128]{3,2,1,0:T(8,128)S(1)} collective-permute-done((f32[12,2,8,128]{3,2,1,0:T(8,128)S(1)}, f32[12,2,8,128]{3,2,1,0:T(8,128)S(1)}, u32[]{:S(2)}, u32[]{:S(2)}) %collective-permute-start.2) | collective-permute-done | bytes 98336 | tf_op jit(solution)/shard_map/ppermute | solution.py:28
  14.7 16.5 %collective-permute-done.3.refs_3_ = f32[12,2,8,128]{3,2,1,0:T(8,128)S(1)} collective-permute-done((f32[12,2,8,128]{3,2,1,0:T(8,128)S(1)}, f32[12,2,8,128]{3,2,1,0:T(8,128)S(1)}, u32[]{:S(2)}, u32[]{:S(2)}) %collective-permute-start.3) | collective-permute-done | bytes 98336 | tf_op jit(solution)/shard_map/ppermute | solution.py:28
  41.9 12.2 %collective-permute-done.5.refs_1_ = f32[12,128,128]{2,1,0:T(8,128)S(1)} collective-permute-done((f32[12,128,128]{2,1,0:T(8,128)S(1)}, f32[12,128,128]{2,1,0:T(8,128)S(1)}, u32[]{:S(2)}, u32[]{:S(2)}) %collective-permute-start.5) | collective-permute-done | bytes 786464 | tf_op jit(solution)/shard_map/ppermute | solution.py:28
  60.8 11.8 %conv_one.1 = (f32[12,4,136,128]{3,2,1,0:T(8,128)}, f32[8,128]{1,0:T(8,128)S(1)}) custom-call(s32[6]{0:T(128)S(1)} %stack.35.s_ref, f32[12,2,136,128]{3,2,1,0:T(8,128)S(1)} %get-tuple-element.127.refs_0_.refs_3_.refs_6_, f32[12,2,136,128]{3,2,1,0:T(8,128)S(1)} %get-tuple-element.116.refs_1_.refs_4_.refs_7_, ...), custom_call_target="tpu_custom_call" | custom-call | tf_op jit(solution)/shard_map/conv_one/pallas_call | solution.py:173
  73.2 3.1 %collective-permute-done.9 = f32[8,128]{1,0:T(8,128)S(1)} collective-permute-done((f32[8,128]{1,0:T(8,128)S(1)}, f32[8,128]{1,0:T(8,128)S(1)}, u32[]{:S(2)}, u32[]{:S(2)}) %collective-permute-start.9) | collective-permute-done | bytes 4128 | tf_op jit(solution)/shard_map/ppermute | solution.py:28
  78.2 3.3 %collective-permute-start.13 = (f32[8,128]{1,0:T(8,128)S(1)}, f32[8,128]{1,0:T(8,128)S(1)}, u32[]{:S(2)}, u32[]{:S(2)}) collective-permute-start(f32[8,128]{1,0:T(8,128)S(1)} %concatenate.39), channel_id=1, source_target_pairs={{0,8},{1,9},{2,10},{3,11},{4,12},{5,13},{6,14},{7,15},{8,0},{9,1},... | collective-permute-start | bytes 12296 | tf_op jit(solution)/shard_map/ppermute | solution.py:28
  88.7 10.4 %conv_one_halo.1 = (f32[12,136,128]{2,1,0:T(8,128)S(1)}, f32[12,136,128]{2,1,0:T(8,128)S(1)}) custom-call(s32[6]{0:T(128)S(1)} %stack.35.s_ref, f32[12,2,136,128]{3,2,1,0:T(8,128)} %copy-done, f32[12,136,128]{2,1,0:T(8,128)} %copy-done.4, f32[12,136,128]{2,1,0:T(8,128)} %copy-done.5, f32[12,136,128]{2,1,0:T(8,128)} %copy-done.16, ...), custom_call_target="tpu_custom_call" | custom-call | tf_op jit(solution)/shard_map/conv_one_halo/pallas_call | solution.py:173
  99.2 3.1 %g_cell.3 = (f32[6,4,136,128]{3,2,1,0:T(8,128)}, f32[6,136,128]{2,1,0:T(8,128)S(1)}, f32[6,136,128]{2,1,0:T(8,128)S(1)}) custom-call(s32[6]{0:T(128)S(1)} %stack.35.s_ref, f32[12,2,128,128]{3,2,1,0:T(8,128)S(1)} %copy-done.11, f32[6,2,128,128]{3,2,1,0:T(8,128)} %collective-permute-done.12.refs_1_, f32[12,2,8,128]{3,2,1,0:T(8,128)S(1)} %collective-permute-done.14.refs_2_, ...), custom_call_target="tpu_custom_call" | custom-call | tf_op jit(solution)/shard_map/g_cell/pallas_call | solution.py:173
  111.8 8.7 %conv_two.2 = (f32[6,4,136,128]{3,2,1,0:T(8,128)}, f32[6,136,128]{2,1,0:T(8,128)S(1)}, f32[6,136,128]{2,1,0:T(8,128)S(1)}, f32[8,128]{1,0:T(8,128)S(1)}) custom-call(s32[6]{0:T(128)S(1)} %stack.35.s_ref, f32[12,4,136,128]{3,2,1,0:T(8,128)} %get-tuple-element.120.refs_0_.refs_2_.refs_4_.refs_1_.refs_10_, ...), custom_call_target="tpu_custom_call" | custom-call | tf_op jit(solution)/shard_map/conv_two/pallas_call | solution.py:173
  121.4 8.7 %conv_two.3 = (f32[6,4,136,128]{3,2,1,0:T(8,128)}, f32[6,136,128]{2,1,0:T(8,128)S(1)}, f32[6,136,128]{2,1,0:T(8,128)S(1)}, f32[8,128]{1,0:T(8,128)S(1)}) custom-call(s32[6]{0:T(128)S(1)} %stack.35.s_ref, f32[12,4,136,128]{3,2,1,0:T(8,128)} %get-tuple-element.120.refs_0_.refs_2_.refs_4_.refs_1_.refs_10_, ...), custom_call_target="tpu_custom_call" | custom-call | tf_op jit(solution)/shard_map/conv_two/pallas_call | solution.py:173
  130.8 3.1 %collective-permute-done.21 = f32[8,128]{1,0:T(8,128)S(1)} collective-permute-done((f32[8,128]{1,0:T(8,128)S(1)}, f32[8,128]{1,0:T(8,128)S(1)}, u32[]{:S(2)}, u32[]{:S(2)}) %collective-permute-start.21) | collective-permute-done | bytes 4128 | tf_op jit(solution)/shard_map/ppermute | solution.py:28
  134.0 3.9 %collective-permute-start.24 = (f32[8,128]{1,0:T(8,128)S(1)}, f32[8,128]{1,0:T(8,128)S(1)}, u32[]{:S(2)}, u32[]{:S(2)}) collective-permute-start(f32[8,128]{1,0:T(8,128)S(1)} %concatenate.44), channel_id=1, source_target_pairs={{0,8},{1,9},{2,10},{3,11},{4,12},{5,13},{6,14},{7,15},{8,0},{9,1},... | collective-permute-start | bytes 12296 | tf_op jit(solution)/shard_map/ppermute | solution.py:28
  139.5 2.9 %collective-permute-start.27 = (f32[8,128]{1,0:T(8,128)S(1)}, f32[8,128]{1,0:T(8,128)S(1)}, u32[]{:S(2)}, u32[]{:S(2)}) collective-permute-start(f32[8,128]{1,0:T(8,128)S(1)} %concatenate.45), channel_id=1, source_target_pairs={{0,16},{1,17},{2,18},{3,19},{4,20},{5,21},{6,22},{7,23},{8,24},{9,... | collective-permute-start | bytes 12296 | tf_op jit(solution)/shard_map/ppermute | solution.py:28
  145.3 11.2 %conv_three.2 = (f32[6,4,136,128]{3,2,1,0:T(8,128)}, f32[6,4,128,128]{3,2,1,0:T(8,128)}, f32[6,136,128]{2,1,0:T(8,128)S(1)}, f32[6,136,128]{2,1,0:T(8,128)S(1)},...) custom-call(s32[6]{0:T(128)S(1)} %stack.35.s_ref, ...), custom_call_target="tpu_custom_call" | custom-call | tf_op jit(solution)/shard_map/conv_three/pallas_call | solution.py:173
  159.9 11.4 %conv_three.3 = (f32[6,4,136,128]{3,2,1,0:T(8,128)}, f32[6,4,128,128]{3,2,1,0:T(8,128)}, f32[6,136,128]{2,1,0:T(8,128)S(1)}, f32[6,136,128]{2,1,0:T(8,128)}, f32...) custom-call(s32[6]{0:T(128)S(1)} %stack.35.s_ref, ...), custom_call_target="tpu_custom_call" | custom-call | tf_op jit(solution)/shard_map/conv_three/pallas_call | solution.py:173
  172.4 3.1 %collective-permute-done.32 = f32[8,128]{1,0:T(8,128)S(1)} collective-permute-done((f32[8,128]{1,0:T(8,128)S(1)}, f32[8,128]{1,0:T(8,128)S(1)}, u32[]{:S(2)}, u32[]{:S(2)}) %collective-permute-start.32) | collective-permute-done | bytes 4128 | tf_op jit(solution)/shard_map/ppermute | solution.py:28
  175.6 3.7 %collective-permute-start.35 = (f32[8,128]{1,0:T(8,128)S(1)}, f32[8,128]{1,0:T(8,128)S(1)}, u32[]{:S(2)}, u32[]{:S(2)}) collective-permute-start(f32[8,128]{1,0:T(8,128)S(1)} %add.358), channel_id=1, source_target_pairs={{0,8},{1,9},{2,10},{3,11},{4,12},{5,13},{6,14},{7,15},{8,0},{9,1},... | collective-permute-start | bytes 12296 | tf_op jit(solution)/shard_map/ppermute | solution.py:28
  186.6 12.9 %weight_two.1 = f32[1184,128]{1,0:T(8,128)S(1)} custom-call(s32[6]{0:T(128)S(1)} %stack.35.s_ref, f32[12,4,136,128]{3,2,1,0:T(8,128)} %get-tuple-element.120.refs_0_.refs_2_.refs_4_.refs_1_.refs_10_, f32[12,136,128]{2,1,0:T(8,128)} %copy-done.2, f32[12,136,128]{2,1,0:T(8,128)} %copy-done.3, f32[6,4,128,128]{3,2,1,0:T(8,128)} %get-tuple-element.169.refs_3_, ...), custom_call_target="tpu_custom_call" | custom-call | tf_op jit(solution)/shard_map/weight_two/pallas_call | solution.py:173
  199.5 9.6 %conv_four.2 = (f32[6,2,128,128]{3,2,1,0:T(8,128)S(1)}, f32[6,2,128,128]{3,2,1,0:T(8,128)}) custom-call(s32[6]{0:T(128)S(1)} %stack.35.s_ref, f32[6,4,136,128]{3,2,1,0:T(8,128)} %get-tuple-element.154.refs_0_.refs_5_, f32[12,4,136,128]{3,2,1,0:T(8,128)} %get-tuple-element.120.refs_0_.refs_2_.refs_4_.refs_1_.refs_10_, f32[12,136,128]{2,1,0:T(8,128)} %copy-done.2, ...), custom_call_target="tpu_custom_call" | custom-call | tf_op jit(solution)/shard_map/conv_four/pallas_call | solution.py:173
  211.5 13.8 %weight_one.1 = f32[1184,128]{1,0:T(8,128)S(1)} custom-call(s32[6]{0:T(128)S(1)} %stack.35.s_ref, f32[12,2,136,128]{3,2,1,0:T(8,128)} %copy-done, f32[12,2,136,128]{3,2,1,0:T(8,128)} %copy-done.1, f32[12,136,128]{2,1,0:T(8,128)} %copy-done.4, f32[12,136,128]{2,1,0:T(8,128)} %copy-done.5, ...), custom_call_target="tpu_custom_call" | custom-call | tf_op jit(solution)/shard_map/weight_one/pallas_call | solution.py:173
  231.7 8.7 %conv_four.3 = (f32[6,2,128,128]{3,2,1,0:T(8,128)S(1)}, f32[6,2,128,128]{3,2,1,0:T(8,128)S(1)}) custom-call(s32[6]{0:T(128)S(1)} %stack.35.s_ref, f32[6,4,136,128]{3,2,1,0:T(8,128)} %get-tuple-element.160.refs_11_.refs_0_, f32[12,4,136,128]{3,2,1,0:T(8,128)} %get-tuple-element.120.refs_0_.refs_2_.refs_4_.refs_1_.refs_10_, f32[12,136,128]{2,1,0:T(8,128)} %copy-done.2, ...), custom_call_target="tpu_custom_call" | custom-call | tf_op jit(solution)/shard_map/conv_four/pallas_call | solution.py:173
  247.6 9.0 %collective-permute-done.46 = f32[296,128]{1,0:T(8,128)S(1)} collective-permute-done((f32[296,128]{1,0:T(8,128)S(1)}, f32[296,128]{1,0:T(8,128)S(1)}, u32[]{:S(2)}, u32[]{:S(2)}) %collective-permute-start.46) | collective-permute-done | bytes 151584 | tf_op jit(solution)/shard_map/ppermute | solution.py:28
  257.2 3.0 %collective-permute-start.50 = (f32[296,128]{1,0:T(8,128)S(1)}, f32[296,128]{1,0:T(8,128)S(1)}, u32[]{:S(2)}, u32[]{:S(2)}) collective-permute-start(f32[296,128]{1,0:T(8,128)S(1)} %add.366.refs_0_), channel_id=1, source_target_pairs={{0,10},{1,11},{2,8},{3,9},{4,14},{5,15},{6,12},{7,13},{8,2},{9,3},... | collective-permute-start | bytes 454664 | tf_op jit(solution)/shard_map/ppermute | solution.py:28
  (206 shorter events, 91.0 us)
Async XLA Ops:
  7.1 24.1 %collective-permute-start.1 = (f32[12,128,128]{2,1,0:T(8,128)S(1)}, f32[12,128,128]{2,1,0:T(8,128)S(1)}, u32[]{:S(2)}, u32[]{:S(2)}) collective-permute-start(f32[12,128,128]{2,1,0:T(8,128)S(1)} %get-tuple-element.106), channel_id=1, source_target_pairs={{0,4},{1,5},{2,6},{3,7},{4,0},{5,1},{6,2},{7,3},{8,12},{9,13},{10,... | collective-permute-start | bytes 2359304 | tf_op jit(solution)/shard_map/ppermute | solution.py:28
  11.6 19.6 %collective-permute-start.3 = (f32[12,2,8,128]{3,2,1,0:T(8,128)S(1)}, f32[12,2,8,128]{3,2,1,0:T(8,128)S(1)}, u32[]{:S(2)}, u32[]{:S(2)}) collective-permute-start(f32[12,2,8,128]{3,2,1,0:T(8,128)S(1)} %get-tuple-element.108), channel_id=1, source_target_pairs={{0,6},{1,7},{2,4},{3,5},{4,2},{5,3},{6,0},{7,1},{8,14},{9,15},{10,... | collective-permute-start | bytes 294920 | tf_op jit(solution)/shard_map/ppermute | solution.py:28
  34.1 20.0 %collective-permute-start.5 = (f32[12,128,128]{2,1,0:T(8,128)S(1)}, f32[12,128,128]{2,1,0:T(8,128)S(1)}, u32[]{:S(2)}, u32[]{:S(2)}) collective-permute-start(f32[12,128,128]{2,1,0:T(8,128)S(1)} %get-tuple-element.115), channel_id=1, source_target_pairs={{0,4},{1,5},{2,6},{3,7},{4,0},{5,1},{6,2},{7,3},{8,12},{9,13},{10,... | collective-permute-start | bytes 2359304 | tf_op jit(solution)/shard_map/ppermute | solution.py:28
  35.6 25.2 %collective-permute-start.6 = (f32[12,136,128]{2,1,0:T(8,128)S(1)}, f32[12,136,128]{2,1,0:T(8,128)S(1)}, u32[]{:S(2)}, u32[]{:S(2)}) collective-permute-start(f32[12,136,128]{2,1,0:T(8,128)S(1)} %get-tuple-element.117), channel_id=1, source_target_pairs={{0,8},{1,9},{2,10},{3,11},{4,12},{5,13},{6,14},{7,15},{8,0},{9,1},... | collective-permute-start | bytes 2506760 | tf_op jit(solution)/shard_map/ppermute | solution.py:28
  37.2 23.6 %collective-permute-start.7 = (f32[12,136,128]{2,1,0:T(8,128)S(1)}, f32[12,136,128]{2,1,0:T(8,128)S(1)}, u32[]{:S(2)}, u32[]{:S(2)}) collective-permute-start(f32[12,136,128]{2,1,0:T(8,128)S(1)} %get-tuple-element.118), channel_id=1, source_target_pairs={{8,16},{9,17},{10,18},{11,19},{12,20},{13,21},{14,22},{15,23},{16,... | collective-permute-start | bytes 2506760 | tf_op jit(solution)/shard_map/ppermute | solution.py:28
  56.0 22.2 %collective-permute-start.10 = (f32[12,136,128]{2,1,0:T(8,128)}, f32[12,136,128]{2,1,0:T(8,128)S(1)}, u32[]{:S(2)}, u32[]{:S(2)}) collective-permute-start(f32[12,136,128]{2,1,0:T(8,128)} %get-tuple-element.123), channel_id=1, source_target_pairs={{0,8},{1,9},{2,10},{3,11},{4,12},{5,13},{6,14},{7,15},{8,0},{9,1},... | collective-permute-start | bytes 2506760 | tf_op jit(solution)/shard_map/ppermute | solution.py:28
  57.7 20.6 %collective-permute-start.11 = (f32[12,136,128]{2,1,0:T(8,128)}, f32[12,136,128]{2,1,0:T(8,128)}, u32[]{:S(2)}, u32[]{:S(2)}) collective-permute-start(f32[12,136,128]{2,1,0:T(8,128)} %get-tuple-element.124), channel_id=1, source_target_pairs={{8,16},{9,17},{10,18},{11,19},{12,20},{13,21},{14,22},{15,23},{16,... | collective-permute-start | bytes 2506760 | tf_op jit(solution)/shard_map/ppermute | solution.py:28
  59.3 18.9 %collective-permute-start.12 = (f32[6,2,128,128]{3,2,1,0:T(8,128)S(1)}, f32[6,2,128,128]{3,2,1,0:T(8,128)}, u32[]{:S(2)}, u32[]{:S(2)}) collective-permute-start(f32[6,2,128,128]{3,2,1,0:T(8,128)S(1)} %get-tuple-element.125), channel_id=1, source_target_pairs={{0,4},{1,5},{2,6},{3,7},{4,0},{5,1},{6,2},{7,3},{8,12},{9,13},{10,... | collective-permute-start | bytes 2359304 | tf_op jit(solution)/shard_map/ppermute | solution.py:28
  81.5 17.6 %collective-permute-start.14 = (f32[12,2,8,128]{3,2,1,0:T(8,128)S(1)}, f32[12,2,8,128]{3,2,1,0:T(8,128)S(1)}, u32[]{:S(2)}, u32[]{:S(2)}) collective-permute-start(f32[12,2,8,128]{3,2,1,0:T(8,128)S(1)} %get-tuple-element.130), channel_id=1, source_target_pairs={{0,2},{1,3},{2,0},{3,1},{4,6},{5,7},{6,4},{7,5},{8,10},{9,11},{10,... | collective-permute-start | bytes 294920 | tf_op jit(solution)/shard_map/ppermute | solution.py:28
  82.0 17.1 %collective-permute-start.15 = (f32[12,2,8,128]{3,2,1,0:T(8,128)S(1)}, f32[12,2,8,128]{3,2,1,0:T(8,128)S(1)}, u32[]{:S(2)}, u32[]{:S(2)}) collective-permute-start(f32[12,2,8,128]{3,2,1,0:T(8,128)S(1)} %get-tuple-element.131), channel_id=1, source_target_pairs={{0,6},{1,7},{2,4},{3,5},{4,2},{5,3},{6,0},{7,1},{8,14},{9,15},{10,... | collective-permute-start | bytes 294920 | tf_op jit(solution)/shard_map/ppermute | solution.py:28
  84.5 18.6 %collective-permute-start.16 = (f32[8,128]{1,0:T(8,128)S(1)}, f32[8,128]{1,0:T(8,128)S(1)}, u32[]{:S(2)}, u32[]{:S(2)}) collective-permute-start(f32[8,128]{1,0:T(8,128)S(1)} %concatenate.40), channel_id=1, source_target_pairs={{0,16},{1,17},{2,18},{3,19},{4,20},{5,21},{6,22},{7,23},{8,24},{9,... | collective-permute-start | bytes 12296 | tf_op jit(solution)/shard_map/ppermute | solution.py:28
  86.1 19.5 %collective-permute-start.8 = (f32[6,2,128,128]{3,2,1,0:T(8,128)S(1)}, f32[6,2,128,128]{3,2,1,0:T(8,128)S(1)}, u32[]{:S(2)}, u32[]{:S(2)}) collective-permute-start(f32[6,2,128,128]{3,2,1,0:T(8,128)S(1)} %get-tuple-element.121), channel_id=1, source_target_pairs={{0,4},{1,5},{2,6},{3,7},{4,0},{5,1},{6,2},{7,3},{8,12},{9,13},{10,... | collective-permute-start | bytes 2359304 | tf_op jit(solution)/shard_map/ppermute | solution.py:28
  102.3 18.3 %collective-permute-start.18 = (f32[6,136,128]{2,1,0:T(8,128)S(1)}, f32[6,136,128]{2,1,0:T(8,128)S(1)}, u32[]{:S(2)}, u32[]{:S(2)}) collective-permute-start(f32[6,136,128]{2,1,0:T(8,128)S(1)} %get-tuple-element.139), channel_id=1, source_target_pairs={{8,16},{9,17},{10,18},{11,19},{12,20},{13,21},{14,22},{15,23},{16,... | collective-permute-start | bytes 1253384 | tf_op jit(solution)/shard_map/ppermute | solution.py:28
  103.3 18.1 %collective-permute-start.17 = (f32[6,136,128]{2,1,0:T(8,128)S(1)}, f32[6,136,128]{2,1,0:T(8,128)S(1)}, u32[]{:S(2)}, u32[]{:S(2)}) collective-permute-start(f32[6,136,128]{2,1,0:T(8,128)S(1)} %get-tuple-element.138), channel_id=1, source_target_pairs={{0,8},{1,9},{2,10},{3,11},{4,12},{5,13},{6,14},{7,15},{8,0},{9,1},... | collective-permute-start | bytes 1253384 | tf_op jit(solution)/shard_map/ppermute | solution.py:28
  108.4 21.8 %collective-permute-start.20 = (f32[6,136,128]{2,1,0:T(8,128)}, f32[6,136,128]{2,1,0:T(8,128)}, u32[]{:S(2)}, u32[]{:S(2)}) collective-permute-start(f32[6,136,128]{2,1,0:T(8,128)} %get-tuple-element.147), channel_id=1, source_target_pairs={{8,16},{9,17},{10,18},{11,19},{12,20},{13,21},{14,22},{15,23},{16,... | collective-permute-start | bytes 1253384 | tf_op jit(solution)/shard_map/ppermute | solution.py:28
  109.9 20.4 %collective-permute-start.19 = (f32[6,136,128]{2,1,0:T(8,128)}, f32[6,136,128]{2,1,0:T(8,128)}, u32[]{:S(2)}, u32[]{:S(2)}) collective-permute-start(f32[6,136,128]{2,1,0:T(8,128)} %get-tuple-element.146), channel_id=1, source_target_pairs={{0,8},{1,9},{2,10},{3,11},{4,12},{5,13},{6,14},{7,15},{8,0},{9,1},... | collective-permute-start | bytes 1253384 | tf_op jit(solution)/shard_map/ppermute | solution.py:28
  142.4 17.5 %collective-permute-start.26 = (f32[6,136,128]{2,1,0:T(8,128)S(1)}, f32[6,136,128]{2,1,0:T(8,128)S(1)}, u32[]{:S(2)}, u32[]{:S(2)}) collective-permute-start(f32[6,136,128]{2,1,0:T(8,128)S(1)} %get-tuple-element.153), channel_id=1, source_target_pairs={{8,16},{9,17},{10,18},{11,19},{12,20},{13,21},{14,22},{15,23},{16,... | collective-permute-start | bytes 1253384 | tf_op jit(solution)/shard_map/ppermute | solution.py:28
  143.3 16.6 %collective-permute-start.25 = (f32[6,136,128]{2,1,0:T(8,128)S(1)}, f32[6,136,128]{2,1,0:T(8,128)S(1)}, u32[]{:S(2)}, u32[]{:S(2)}) collective-permute-start(f32[6,136,128]{2,1,0:T(8,128)S(1)} %get-tuple-element.152), channel_id=1, source_target_pairs={{0,8},{1,9},{2,10},{3,11},{4,12},{5,13},{6,14},{7,15},{8,0},{9,1},... | collective-permute-start | bytes 1253384 | tf_op jit(solution)/shard_map/ppermute | solution.py:28
  156.6 19.0 %collective-permute-start.33 = (f32[6,136,128]{2,1,0:T(8,128)S(1)}, f32[6,136,128]{2,1,0:T(8,128)S(1)}, u32[]{:S(2)}, u32[]{:S(2)}) collective-permute-start(f32[6,136,128]{2,1,0:T(8,128)S(1)} %get-tuple-element.164), channel_id=1, source_target_pairs={{0,8},{1,9},{2,10},{3,11},{4,12},{5,13},{6,14},{7,15},{8,0},{9,1},... | collective-permute-start | bytes 1253384 | tf_op jit(solution)/shard_map/ppermute | solution.py:28
  157.6 17.9 %collective-permute-start.34 = (f32[6,136,128]{2,1,0:T(8,128)S(1)}, f32[6,136,128]{2,1,0:T(8,128)S(1)}, u32[]{:S(2)}, u32[]{:S(2)}) collective-permute-start(f32[6,136,128]{2,1,0:T(8,128)S(1)} %get-tuple-element.165), channel_id=1, source_target_pairs={{8,16},{9,17},{10,18},{11,19},{12,20},{13,21},{14,22},{15,23},{16,... | collective-permute-start | bytes 1253384 | tf_op jit(solution)/shard_map/ppermute | solution.py:28
  158.3 41.2 %collective-permute-start.30 = (f32[6,2,128,128]{3,2,1,0:T(8,128)}, f32[6,2,128,128]{3,2,1,0:T(8,128)}, u32[]{:S(2)}, u32[]{:S(2)}) collective-permute-start(f32[6,2,128,128]{3,2,1,0:T(8,128)} %get-tuple-element.159), channel_id=1, source_target_pairs={{0,4},{1,5},{2,6},{3,7},{4,0},{5,1},{6,2},{7,3},{8,12},{9,13},{10,... | collective-permute-start | bytes 2359304 | tf_op jit(solution)/shard_map/ppermute | solution.py:28
  171.3 28.2 %collective-permute-start.28 = (f32[6,2,128,128]{3,2,1,0:T(8,128)}, f32[6,2,128,128]{3,2,1,0:T(8,128)S(1)}, u32[]{:S(2)}, u32[]{:S(2)}) collective-permute-start(f32[6,2,128,128]{3,2,1,0:T(8,128)} %get-tuple-element.157), channel_id=1, source_target_pairs={{0,4},{1,5},{2,6},{3,7},{4,0},{5,1},{6,2},{7,3},{8,12},{9,13},{10,... | collective-permute-start | bytes 2359304 | tf_op jit(solution)/shard_map/ppermute | solution.py:28
  244.7 19.5 %collective-permute-start.40 = (f32[2,6,2,64,128]{4,3,2,1,0:T(8,128)S(1)}, f32[2,6,2,64,128]{4,3,2,1,0:T(8,128)S(1)}, u32[]{:S(2)}, u32[]{:S(2)}) collective-permute-start(f32[2,6,2,64,128]{4,3,2,1,0:T(8,128)S(1)} %grad_halves.2), channel_id=1, source_target_pairs={{0,1},{1,0},{2,3},{3,2},{4,5},{5,4},{6,7},{7,6},{8,9},{9,8},{10,11... | collective-permute-start | bytes 2359304 | tf_op jit(solution)/shard_map/ppermute | solution.py:28
  245.7 20.9 %collective-permute-start.47 = (f32[6,2,128,128]{3,2,1,0:T(8,128)S(1)}, f32[6,2,128,128]{3,2,1,0:T(8,128)S(1)}, u32[]{:S(2)}, u32[]{:S(2)}) collective-permute-start(f32[6,2,128,128]{3,2,1,0:T(8,128)S(1)} %get-tuple-element.186), channel_id=1, source_target_pairs={{0,4},{1,5},{2,6},{3,7},{4,0},{5,1},{6,2},{7,3},{8,12},{9,13},{10,... | collective-permute-start | bytes 2359304 | tf_op jit(solution)/shard_map/ppermute | solution.py:28
  (56 other events, 571.8 us)
